TPU v7x, 32 devices: a whole 2x2x4 slice. The times are simulated.
32 devices in a mesh: groups: 1, chan: 16 (over z, y, x), grow: 2 (over core).
Axes of the slice: x: 2, y: 2, z: 4, core: 2. Of those that a mesh axis runs over, the one named last changes fastest.
Arguments:
- pair_input: bfloat16 [768, 768, 128], P(('groups', 'chan'), 'grow'), may hold values from -6 to 6
- token_mask: int32 [768], P('groups'), may hold values 0 or 1
- norm_gain: float32 [128], replicated, may hold values from 0.1 to 1.9
- left_gate: bfloat16 [128, 128], replicated, may hold values from -0.5 to 0.5
- left_value: bfloat16 [128, 128], replicated, may hold values from -0.5 to 0.5
- right_gate: bfloat16 [128, 128], replicated, may hold values from -0.5 to 0.5
- right_value: bfloat16 [128, 128], replicated, may hold values from -0.5 to 0.5
- sum_gain: float32 [128], replicated, may hold values from 0.1 to 1.9
- out_gate: bfloat16 [128, 128], replicated, may hold values from -0.5 to 0.5
- out_proj: bfloat16 [128, 128], replicated, may hold values from -0.5 to 0.5
Outputs:
- update: bfloat16 [768, 768, 128], P(('groups', 'chan'), 'grow')
All inputs are finite; a program needn't handle non-finite values.
Results may differ from a plain program's by a relative error of at most 0.0083.
Values may be sent and summed in bfloat16 or wider, within the bound.
No kernel may reach another device: no remote copies, remote signals or barrier semaphores. Data moves between devices by JAX's collectives and lax.ppermute only.
A program may use at most 128 MiB of HBM per device.

v0:
```python
import jax
import jax.numpy as jnp
from jax import lax
from jax.sharding import PartitionSpec as P

norm_eps = 1e-05


def layer_norm(values, gain_vec, along_axis):
    average = jnp.mean(values, axis=along_axis, keepdims=True)
    centred = values - average
    spread = jnp.mean(centred * centred, axis=along_axis, keepdims=True)
    return centred * lax.rsqrt(spread + norm_eps) * gain_vec


def per_device(
    pair_input,
    token_mask,
    norm_gain,
    left_gate,
    left_value,
    right_gate,
    right_value,
    sum_gain,
    out_gate,
    out_proj,
):
    row_count, col_count, pair_width = pair_input.shape
    row_start = lax.axis_index("chan") * row_count
    grow_index = lax.axis_index("grow")
    col_start = grow_index * col_count
    row_valid = lax.dynamic_slice_in_dim(token_mask, row_start, row_count, 0).astype(jnp.float32)
    col_valid = lax.dynamic_slice_in_dim(token_mask, col_start, col_count, 0).astype(jnp.float32)
    pair_mask = row_valid[None, :, None] * col_valid[None, None, :]
    normed = layer_norm(pair_input.astype(jnp.float32), norm_gain, -1).astype(jnp.bfloat16)

    def project(weight):
        return jnp.einsum("ikd,dh->hik", normed, weight, preferred_element_type=jnp.float32)

    left_op = (jax.nn.sigmoid(project(left_gate)) * project(left_value) * pair_mask).astype(
        jnp.bfloat16
    )
    right_op = (jax.nn.sigmoid(project(right_gate)) * project(right_value) * pair_mask).astype(
        jnp.bfloat16
    )
    left_ex, right_ex = (
        lax.all_to_all(left_op, "chan", split_axis=0, concat_axis=1, tiled=True),
        lax.all_to_all(right_op, "chan", split_axis=0, concat_axis=1, tiled=True),
    )
    partial_value = jnp.einsum(
        "cik,cjk->cij", left_ex, right_ex, preferred_element_type=jnp.float32
    )
    summed = lax.psum_scatter(partial_value, "grow", scatter_dimension=2, tiled=True)
    returned = lax.all_to_all(
        summed.astype(jnp.bfloat16), "chan", split_axis=1, concat_axis=0, tiled=True
    )
    mixed_out = layer_norm(returned.astype(jnp.float32), sum_gain[:, None, None], 0).astype(
        jnp.bfloat16
    )
    linear = jnp.einsum("cij,cd->ijd", mixed_out, out_proj, preferred_element_type=jnp.float32)
    gate_act = jax.nn.sigmoid(
        jnp.einsum("ijd,de->ije", normed, out_gate, preferred_element_type=jnp.float32)
    )
    return (gate_act * linear).astype(jnp.bfloat16)


def solution(mesh):
    in_specs = (
        P(("groups", "chan"), "grow", None),
        P("groups"),
        P(),
        P(),
        P(),
        P(),
        P(),
        P(),
        P(),
        P(),
    )
    out_specs = P(("groups", "chan"), "grow", None)
    return jax.shard_map(
        per_device, mesh=mesh, in_specs=in_specs, out_specs=out_specs, check_vma=False
    )
```

profile of v0, /device:TPU:0, one launch (start us, length us, event | category | flops | bytes accessed | tf_op | source)
XLA Modules:
  0.0 457.8 jit_solution(6538775323894096816)
XLA Ops:
  6.5 0.0 copy-start
  6.5 0.9 dynamic-slice_convert_fusion.1
  7.5 1.2 dynamic-slice_convert_fusion
  8.7 3.6 convert_reduce_fusion
  12.4 7.1 %fusion.2 = f32[48,384]{1,0:T(8,128)S(1)} fusion(bf16[48,384,128]{2,1,0:T(8,128)(2,1)} %param.10, f32[48,384]{1,0:T(8,128)S(1)} %broadcast_multiply_fusion.2), kind=kLoop, calls=%fused_computation.4 | loop fusion | flops 9418752 | bytes 4866048 | tf_op jit(solution)/shard_map/reduce_sum | solution.py:12
  19.5 0.1 add_rsqrt_fusion.1
  19.6 0.0 copy-done
  19.6 0.0 copy-done.5
  19.6 0.0 copy-done.2
  19.6 0.0 copy-start.7
  19.6 5.1 %fusion.18 = f32[48,384,128]{2,1,0:T(8,128)S(1)} fusion(bf16[128,128]{1,0:T(8,128)(2,1)S(1)} %copy-done, bf16[48,384,128]{2,1,0:T(8,128)(2,1)S(1)} %copy-done.2, f32[128]{0:T(128)S(1)} %copy-done.5, f32[48,384]{1,0:T(8,128)S(1)} %get-tuple-element.5, f32[48,384]{1,0:T(8,128)S(1)} %broadcast_multiply_fusion.2), kind=kOutput, calls=%fused_computation.31 | convolution fusion | flops 615776256 | bytes 14336512 | tf_op jit(solution)/shard_map/ikd,dh->hik/dot_general | solution.py:38
  24.7 0.0 copy-done.7
  24.7 10.6 %fusion.11 = bf16[128,48,384]{0,2,1:T(8,128)(2,1)} fusion(f32[48,384]{1,0:T(8,128)S(1)} %get-tuple-element.6, f32[48,384,128]{2,1,0:T(8,128)S(1)} %fusion.18, bf16[128,128]{1,0:T(8,128)(2,1)S(1)} %copy-done.7, bf16[48,384,128]{2,1,0:T(8,128)(2,1)S(1)} %copy-done.2, f32[128]{0:T(128)S(1)} %copy-done.5, f32[48,384]{1,0:T(8,128)S(1)} %get-tuple-element.5, ...), kind=kOutput, calls=%fused_computation.19 | convolution fusion | flops 629932032 | bytes 19128832 | tf_op jit(solution)/shard_map/ikd,dh->hik/dot_general | solution.py:38
  35.3 7.1 %copy.26 = bf16[128,48,384]{2,1,0:T(8,128)(2,1)} copy(bf16[128,48,384]{0,2,1:T(8,128)(2,1)} %fusion.11) | data formatting | bytes 9437184 | tf_op jit(solution)/shard_map/convert_element_type | solution.py:40
  42.4 8.5 %all-to-all-start = ((bf16[128,48,384]{2,1,0:T(8,128)(2,1)}), bf16[128,48,384]{2,1,0:T(8,128)(2,1)}, u32[]{:S(2)}, u32[]{:S(2)}) async-start(bf16[128,48,384]{2,1,0:T(8,128)(2,1)} %copy.26), calls=%async_computation | async-start | bytes 9437184 | tf_op jit(solution)/shard_map/all_to_all | solution.py:47
  50.9 0.0 copy-done.3
  50.9 0.0 slice-start.1
  50.9 0.0 copy-start.8
  50.9 9.5 %fusion.15 = f32[48,384,128]{2,1,0:T(8,128)S(1)} fusion(bf16[128,128]{1,0:T(8,128)(2,1)S(1)} %copy-done.3, bf16[48,384,128]{2,1,0:T(8,128)(2,1)} %param.10, f32[128]{0:T(128)S(1)} %copy-done.5, f32[48,384]{1,0:T(8,128)S(1)} %get-tuple-element.5, f32[48,384]{1,0:T(8,128)S(1)} %broadcast_multiply_fusion.2), kind=kOutput, calls=%fused_computation.28 | convolution fusion | flops 615776256 | bytes 14336512 | tf_op jit(solution)/shard_map/ikd,dh->hik/dot_general | solution.py:38
  60.4 0.0 slice-done
  60.4 0.0 slice-done.1
  60.4 10.6 %fusion.12 = bf16[128,48,384]{0,2,1:T(8,128)(2,1)} fusion(f32[48,384]{1,0:T(8,128)S(1)} %get-tuple-element.6, f32[48,384,128]{2,1,0:T(8,128)S(1)} %fusion.15, bf16[128,128]{1,0:T(8,128)(2,1)S(1)} %copy-done.8, bf16[48,384,128]{2,1,0:T(8,128)(2,1)S(1)} %bitcast.49, f32[128]{0:T(128)S(1)} %copy-done.5, f32[48,384]{1,0:T(8,128)S(1)} %get-tuple-element.5, ...), kind=kOutput, calls=%fused_computation.20 | convolution fusion | flops 629932032 | bytes 19128832 | tf_op jit(solution)/shard_map/ikd,dh->hik/dot_general | solution.py:38
  71.0 7.1 %copy.28 = bf16[128,48,384]{2,1,0:T(8,128)(2,1)} copy(bf16[128,48,384]{0,2,1:T(8,128)(2,1)} %fusion.12) | data formatting | bytes 9437184 | tf_op jit(solution)/shard_map/convert_element_type | solution.py:43
  78.1 62.1 %all-to-all-done = bf16[128,48,384]{2,1,0:T(8,128)(2,1)} async-done(((bf16[128,48,384]{2,1,0:T(8,128)(2,1)}), bf16[128,48,384]{2,1,0:T(8,128)(2,1)}, u32[]{:S(2)}, u32[]{:S(2)}) %all-to-all-start) | async-done | bytes 4718624 | tf_op jit(solution)/shard_map/all_to_all | solution.py:47
  140.2 22.4 %all-to-all-start.1 = ((bf16[128,48,384]{2,1,0:T(8,128)(2,1)}), bf16[128,48,384]{2,1,0:T(8,128)(2,1)}, u32[]{:S(2)}, u32[]{:S(2)}) async-start(bf16[128,48,384]{2,1,0:T(8,128)(2,1)} %copy.28), calls=%async_computation.1 | async-start | bytes 9437184 | tf_op jit(solution)/shard_map/all_to_all | solution.py:48
  162.5 0.2 reduce-scatter.2.cloned.1.call-start
  162.8 5.0 %copy.27 = bf16[8,16,48,384]{3,2,1,0:T(8,128)(2,1)} copy(bf16[8,16,48,384]{3,2,0,1:T(8,128)(2,1)} %bitcast.5) | data formatting | bytes 9437184 | tf_op jit(solution)/shard_map/all_to_all | solution.py:47
  167.8 82.3 %all-to-all-done.1 = bf16[128,48,384]{2,1,0:T(8,128)(2,1)} async-done(((bf16[128,48,384]{2,1,0:T(8,128)(2,1)}), bf16[128,48,384]{2,1,0:T(8,128)(2,1)}, u32[]{:S(2)}, u32[]{:S(2)}) %all-to-all-start.1) | async-done | bytes 4718624 | tf_op jit(solution)/shard_map/all_to_all | solution.py:48
  250.1 3.0 copy.29
  253.1 0.6 slice-done.5
  253.8 9.1 %fusion.26 = f32[8,768,768]{2,1,0:T(8,128)} fusion(bf16[8,768,384]{2,1,0:T(8,128)(2,1)S(1)} %bitcast.57, bf16[8,768,384]{2,1,0:T(8,128)(2,1)S(1)} %bitcast.58), kind=kOutput, calls=%fused_computation.36 | convolution fusion | flops 3623878656 | bytes 28311552 | tf_op jit(solution)/shard_map/cik,cjk->cij/dot_general | solution.py:50
  262.9 0.0 reduce-scatter.2.cloned.1.call-update
  262.9 44.5 %reduce-scatter.2.cloned.1.call-done = f32[8,768,384]{2,1,0:T(8,128)} async-done(((f32[8,768,768]{2,1,0:T(8,128)}), f32[8,768,384]{2,1,0:T(8,128)}) %reduce-scatter.2.cloned.1.call-update) | async-done | bytes 9437200 | tf_op jit(solution)/shard_map/reduce_scatter | solution.py:53
  307.4 4.3 convert_element_type.51
  311.7 2.8 copy.30
  314.5 112.0 %all_to_all.45 = bf16[8,768,384]{2,0,1:T(8,128)(2,1)S(1)} all-to-all(bf16[8,768,384]{2,0,1:T(8,128)(2,1)S(1)} %copy.30), channel_id=1, replica_groups=mesh['groups'=1,'chan'=16,'grow'=2] {'chan'}, dimensions={1} | all-to-all | bytes 9437184 | tf_op jit(solution)/shard_map/all_to_all | solution.py:54
  426.6 0.6 copy.31
  427.2 0.7 fusion.8
  427.9 0.8 convert_bitcast_fusion
  428.8 1.3 multiply_reduce_fusion
  430.1 0.0 copy-start.6
  430.1 0.0 slice-start.2
  430.1 4.7 %copy.32 = f32[16,8,48,384]{3,2,1,0:T(8,128)} copy(f32[16,8,48,384]{3,2,0,1:T(8,128)S(1)} %convert_bitcast_fusion) | data formatting | bytes 18874368 | tf_op jit(solution)/shard_map/convert_element_type | solution.py:57
  434.8 5.0 %fusion.7 = bf16[128,48,384]{2,1,0:T(8,128)(2,1)S(1)} fusion(f32[16,8,48,384]{3,2,1,0:T(8,128)} %copy.32, f32[128]{0:T(128)S(1)} %copy-done.6, f32[48,384]{1,0:T(8,128)S(1)} %add_rsqrt_fusion, f32[48,384]{1,0:T(8,128)S(1)} %broadcast_multiply_fusion.1), kind=kLoop, calls=%fused_computation.11 | loop fusion | flops 9437184 | bytes 14303744 | tf_op jit(solution)/shard_map/convert_element_type | solution.py:57
  439.8 0.0 copy-start.9
  439.8 1.5 fusion.9
  441.3 0.0 copy-start.1
  441.4 9.6 %multiply_convert_fusion.2 = bf16[48,384,128]{2,1,0:T(8,128)(2,1)} fusion(f32[48,384,128]{2,1,0:T(8,128)S(1)} %fusion.9, bf16[128,128]{1,0:T(8,128)(2,1)S(1)} %copy-done.9, bf16[48,384,128]{2,1,0:T(8,128)(2,1)S(1)} %bitcast.51, f32[128]{0:T(128)S(1)} %copy-done.5, f32[48,384]{1,0:T(8,128)S(1)} %get-tuple-element.5, f32[48,384]{1,0:T(8,128)S(1)} %broadcast_multiply_fusion.2), kind=kOutput, calls=%fused_computation.14 | convolution fusion | flops 627572736 | bytes 19055104 | tf_op jit(solution)/shard_map/ijd,de->ije/dot_general | solution.py:62
  (22 shorter events, 0.1 us)
Async XLA Ops:
  6.5 13.0 %copy-start = (bf16[128,128]{1,0:T(8,128)(2,1)S(1)}, bf16[128,128]{1,0:T(8,128)(2,1)}, u32[]{:S(2)}) copy-start(bf16[128,128]{1,0:T(8,128)(2,1)} %param.13) | copy-start | bytes 98308
  6.5 13.0 %copy-start.5 = (f32[128]{0:T(128)S(1)}, f32[128]{0:T(128)}, u32[]{:S(2)}) copy-start(f32[128]{0:T(128)} %param.12) | copy-start | bytes 1540
  6.5 13.1 %copy-start.2 = (bf16[48,384,128]{2,1,0:T(8,128)(2,1)S(1)}, bf16[48,384,128]{2,1,0:T(8,128)(2,1)}, u32[]{:S(2)}) copy-start(bf16[48,384,128]{2,1,0:T(8,128)(2,1)} %param.10) | copy-start | bytes 14155780
  19.6 5.1 %copy-start.7 = (bf16[128,128]{1,0:T(8,128)(2,1)S(1)}, bf16[128,128]{1,0:T(8,128)(2,1)}, u32[]{:S(2)}) copy-start(bf16[128,128]{1,0:T(8,128)(2,1)} %param.14) | copy-start | bytes 98308
  35.3 15.6 %copy-start.3 = (bf16[128,128]{1,0:T(8,128)(2,1)S(1)}, bf16[128,128]{1,0:T(8,128)(2,1)}, u32[]{:S(2)}) copy-start(bf16[128,128]{1,0:T(8,128)(2,1)} %param.15) | copy-start | bytes 98308
  42.4 18.0 %slice-start = ((s8[4718592]{0:T(1024)(128)(4,1)}), s8[524288]{0:T(1024)(128)(4,1)S(1)}, s32[]{:S(2)}) async-start(s8[4718592]{0:T(1024)(128)(4,1)} %bitcast.48), calls=%async_computation.5 | async-start | bytes 1048576
  42.4 97.8 %all-to-all-start = ((bf16[128,48,384]{2,1,0:T(8,128)(2,1)}), bf16[128,48,384]{2,1,0:T(8,128)(2,1)}, u32[]{:S(2)}, u32[]{:S(2)}) async-start(bf16[128,48,384]{2,1,0:T(8,128)(2,1)} %copy.26), calls=%async_computation | async-start | bytes 9437184 | tf_op jit(solution)/shard_map/all_to_all | solution.py:47
  50.9 9.5 %slice-start.1 = ((s8[4718592]{0:T(1024)(128)(4,1)}), s8[4194304]{0:T(1024)(128)(4,1)S(1)}, s32[]{:S(2)}) async-start(s8[4718592]{0:T(1024)(128)(4,1)} %bitcast.48), calls=%async_computation.6 | async-start | bytes 8388608
  50.9 9.5 %copy-start.8 = (bf16[128,128]{1,0:T(8,128)(2,1)S(1)}, bf16[128,128]{1,0:T(8,128)(2,1)}, u32[]{:S(2)}) copy-start(bf16[128,128]{1,0:T(8,128)(2,1)} %param.16) | copy-start | bytes 98308
  140.2 110.0 %all-to-all-start.1 = ((bf16[128,48,384]{2,1,0:T(8,128)(2,1)}), bf16[128,48,384]{2,1,0:T(8,128)(2,1)}, u32[]{:S(2)}, u32[]{:S(2)}) async-start(bf16[128,48,384]{2,1,0:T(8,128)(2,1)} %copy.28), calls=%async_computation.1 | async-start | bytes 9437184 | tf_op jit(solution)/shard_map/all_to_all | solution.py:48
  162.5 144.9 %reduce-scatter.2.cloned.1.call-start = ((), (), s32[]{:S(2)}) async-start(), calls=%async_computation.4 | async-start | bytes 28311552 | tf_op jit(solution)/shard_map/reduce_scatter | solution.py:53
  167.8 85.3 %slice-start.4 = ((s8[4718592]{0:T(1024)(128)(4,1)}), s8[524288]{0:T(1024)(128)(4,1)S(1)}, s32[]{:S(2)}) async-start(s8[4718592]{0:T(1024)(128)(4,1)} %bitcast.55), calls=%async_computation.9 | async-start | bytes 1048576
  250.1 3.6 slice-start.5
  430.1 4.7 %copy-start.6 = (f32[128]{0:T(128)S(1)}, f32[128]{0:T(128)}, u32[]{:S(2)}) copy-start(f32[128]{0:T(128)} %param.17) | copy-start | bytes 1540
  430.1 11.2 %slice-start.2 = ((s8[4718592]{0:T(1024)(128)(4,1)}), s8[4194304]{0:T(1024)(128)(4,1)S(1)}, s32[]{:S(2)}) async-start(s8[4718592]{0:T(1024)(128)(4,1)} %bitcast.50), calls=%async_computation.7 | async-start | bytes 8388608
  434.8 5.0 %copy-start.4 = (bf16[128,128]{1,0:T(8,128)(2,1)S(1)}, bf16[128,128]{1,0:T(8,128)(2,1)}, u32[]{:S(2)}) copy-start(bf16[128,128]{1,0:T(8,128)(2,1)} %param.19) | copy-start | bytes 98308
  434.8 6.5 %slice-start.3 = ((s8[4718592]{0:T(1024)(128)(4,1)}), s8[524288]{0:T(1024)(128)(4,1)S(1)}, s32[]{:S(2)}) async-start(s8[4718592]{0:T(1024)(128)(4,1)} %bitcast.50), calls=%async_computation.8 | async-start | bytes 1048576
  439.8 1.5 copy-start.9
  441.3 9.6 %copy-start.1 = (bf16[128,128]{1,0:T(8,128)(2,1)S(1)}, bf16[128,128]{1,0:T(8,128)(2,1)}, u32[]{:S(2)}) copy-start(bf16[128,128]{1,0:T(8,128)(2,1)} %param.13) | copy-start | bytes 98308
Sparse Core Ops, SparseCore 0:
  263.0 44.3 reduce-scatter.1
where the time goes:
time: 459 us; the launch traced here: 458 us
  waiting for transfers between devices  189 us (41%)
  blocking collectives  112 us (24%)
  matrix products  55.8 us (12%)
  starting transfers between devices  31.1 us (7%)
  local copies, waits for them, and re-layouts  31 us (7%)
  other arithmetic  25.2 us (5%)
  between operations  13.7 us (3%)
    all_to_all x1, blocking collectives, per_device(): lax.all_to_all(summed.astype(jnp.bfloat16), 'chan', split_axis=1, concat_...  112 us
    all_to_all x1, waiting for transfers between devices, per_device(): lax.all_to_all(right_op, 'chan', split_axis=0, concat_axis=1, tiled=True)  82.3 us
    all_to_all x1, waiting for transfers between devices, per_device(): lax.all_to_all(left_op, 'chan', split_axis=0, concat_axis=1, tiled=True)  62.1 us
    reduce_scatter x1, waiting for transfers between devices, per_device(): lax.psum_scatter(partial_value, 'grow', scatter_dimension=2, tiled=True)  44.5 us
    dot_general x4, matrix products, project(): jnp.einsum('ikd,dh->hik', normed, weight, preferred_element_type=jnp.floa...  35.7 us
    all_to_all x1, starting transfers between devices, per_device(): lax.all_to_all(right_op, 'chan', split_axis=0, concat_axis=1, tiled=True)  22.4 us
    dot_general x1, matrix products, per_device(): jnp.einsum('ijd,de->ije', normed, out_gate, preferred_element_type=jnp.fl...  9.55 us
  transfers between devices with their start and end apart: 3, of which 3 were waited for; matrix products, arithmetic and copies ran while one was open for 7% of the time, Pallas kernels for 0%

commit v1 on v0

v1 whole, which is shorter than its diff:
```python
import functools
import jax
import jax.numpy as jnp
from jax import lax
from jax.experimental import pallas as pl
from jax.experimental.pallas import tpu as pltpu
from jax.sharding import Mesh
from jax.sharding import PartitionSpec as P

norm_eps = 1e-05
ROWS = 16
LANES = 128
VMEM_BYTES = 56 * 1024 * 1024


def params(**kw):
    return pltpu.CompilerParams(vmem_limit_bytes=VMEM_BYTES, **kw)


def sigmoid(x):
    return 1.0 / (1.0 + jnp.exp(-x))


def project_kernel(sizes, owners, hidden, norm_first, row_ref, col_ref, x_ref, w_ref, gain_ref, *refs):
    if norm_first:
        normed_ref, *outs, held = refs
    else:
        *outs, held = refs
    at = pl.program_id(0) * ROWS

    def one_row(i, _):
        if norm_first:
            x = x_ref[i].astype(jnp.float32)
            centred = x - jnp.mean(x, axis=-1, keepdims=True)
            spread = jnp.mean(centred * centred, axis=-1, keepdims=True)
            normed = (centred * lax.rsqrt(spread + norm_eps) * gain_ref[...]).astype(jnp.bfloat16)
            normed_ref[i] = normed
        else:
            normed = x_ref[i]
        both = lax.dot_general(
            w_ref[...], normed, (((1,), (1,)), ((), ())), preferred_element_type=jnp.float32
        )
        valid = col_ref[...] * row_ref[at + i]
        gated = sigmoid(both[:hidden]) * both[hidden:] * valid
        for j in range(held.shape[0]):
            held[j, pl.ds(pl.multiple_of(i * hidden, hidden), hidden), :] = gated[:, j * LANES:(j + 1) * LANES]
        return 0

    lax.fori_loop(0, ROWS, one_row, 0, unroll=2)
    offset = 0
    for out, size in zip(outs, sizes):
        def one_owner(d, _, out=out, size=size, offset=offset):
            for e in range(size):
                channel = offset * owners + d * size + e
                for j in range(held.shape[0]):
                    out[d, e, :, j * LANES:(j + 1) * LANES] = held[j, pl.ds(channel, ROWS, stride=hidden), :].astype(jnp.bfloat16)
            return 0
        lax.fori_loop(0, owners, one_owner, 0, unroll=2)
        offset += size


def project(x, gate, value, gain, row_valid, col_valid, sizes, owners, norm_first):
    rows, cols, width = x.shape
    hidden = gate.shape[1]
    w = jnp.concatenate([gate, value], axis=1).T
    out_shape = [jax.ShapeDtypeStruct((owners, s, rows, cols), jnp.bfloat16) for s in sizes]
    out_specs = [pl.BlockSpec((owners, s, ROWS, cols), lambda r: (0, 0, r, 0)) for s in sizes]
    x_spec = pl.BlockSpec((ROWS, cols, width), lambda r: (r, 0, 0))
    if norm_first:
        out_shape = [jax.ShapeDtypeStruct(x.shape, jnp.bfloat16)] + out_shape
        out_specs = [x_spec] + out_specs
    whole = lambda shape: pl.BlockSpec(shape, lambda r: (0,) * len(shape))
    return pl.pallas_call(
        functools.partial(project_kernel, sizes, owners, hidden, norm_first),
        grid=(rows // ROWS,),
        in_specs=[
            pl.BlockSpec(memory_space=pltpu.SMEM),
            whole((1, cols)),
            x_spec,
            whole(w.shape),
            whole((1, width)),
        ],
        out_specs=out_specs,
        out_shape=out_shape,
        scratch_shapes=[pltpu.VMEM((cols // LANES, ROWS * hidden, LANES), jnp.float32)],
        compiler_params=params(),
        name="project",
    )(row_valid, col_valid[None], x, w, gain[None])


def contract_kernel(n_left, n_right, rows, cols, place_ref, *refs):
    lefts, rights = refs[:n_left], refs[n_left:n_left + n_right]
    outs = refs[n_left + n_right:2 * n_left + n_right]
    left_all, right_all = refs[2 * n_left + n_right:]
    for s, right in enumerate(rights):
        base = place_ref[s] * (4 * rows)
        for b in range(4):
            for k in range(2):
                right_all[pl.ds(pl.multiple_of(base + b * rows, rows), rows), k * cols:(k + 1) * cols] = right[2 * b + k, 0]
    for s, left in enumerate(lefts):
        for b in range(4):
            for k in range(2):
                left_all[(s * 4 + b) * rows:(s * 4 + b + 1) * rows, k * cols:(k + 1) * cols] = left[2 * b + k, 0]
    for k in range(2):
        total = lax.dot_general(
            left_all[...], right_all[k * cols:(k + 1) * cols, :], (((1,), (1,)), ((), ())),
            preferred_element_type=jnp.float32,
        ).astype(jnp.bfloat16)
        for s, out in enumerate(outs):
            for b in range(4):
                out[2 * b + k, 0] = total[(s * 4 + b) * rows:(s * 4 + b + 1) * rows]


def contract(lefts, rights, place):
    size, rows, cols = lefts[0][0].shape[1:]
    spec = lambda at: pl.BlockSpec((8, 1, rows, cols), lambda q, at=at: (at, q, 0, 0))
    blocks = [*lefts, *rights]
    return pl.pallas_call(
        functools.partial(contract_kernel, len(lefts), len(rights), rows, cols),
        grid=(size,),
        in_specs=[pl.BlockSpec(memory_space=pltpu.SMEM)] + [spec(at) for _, at in blocks],
        out_specs=[spec(0) for _ in lefts],
        out_shape=[jax.ShapeDtypeStruct((8, size, rows, cols), jnp.bfloat16) for _ in lefts],
        scratch_shapes=[
            pltpu.VMEM((len(lefts) * 4 * rows, 2 * cols), jnp.bfloat16),
            pltpu.VMEM((len(rights) * 4 * rows, 2 * cols), jnp.bfloat16),
        ],
        compiler_params=params(),
        name="contract",
    )(place, *[a for a, _ in blocks])


def finish_kernel(n, gain_ref, normed_ref, proj_ref, gate_ref, *refs):
    chunks, out_ref, held = refs[:n], refs[n], refs[n + 1]
    channels = sum(c.shape[0] for c in chunks)
    rows, cols = chunks[0].shape[1:]
    total = jnp.zeros((rows, cols), jnp.float32)
    for c in chunks:
        total = total + jnp.sum(c[...].astype(jnp.float32), axis=0)
    average = total * (1.0 / channels)
    spread = jnp.zeros((rows, cols), jnp.float32)
    for c in chunks:
        centred = c[...].astype(jnp.float32) - average
        spread = spread + jnp.sum(centred * centred, axis=0)
    scale = lax.rsqrt(spread * (1.0 / channels) + norm_eps)
    at = 0
    for c in chunks:
        for h in range(c.shape[0]):
            mixed = (c[h].astype(jnp.float32) - average) * scale * gain_ref[at + h]
            for j in range(held.shape[0]):
                held[j, (at + h) * rows:(at + h + 1) * rows, :] = mixed[:, j * LANES:(j + 1) * LANES]
        at += c.shape[0]

    def one_row(i, _):
        mixed = jnp.concatenate([held[j, pl.ds(i, channels, stride=rows), :] for j in range(held.shape[0])], axis=1).astype(jnp.bfloat16)
        linear = lax.dot_general(mixed, proj_ref[...], (((0,), (0,)), ((), ())), preferred_element_type=jnp.float32)
        gate = jnp.dot(normed_ref[i], gate_ref[...], preferred_element_type=jnp.float32)
        out_ref[i] = (sigmoid(gate) * linear).astype(jnp.bfloat16)
        return 0

    lax.fori_loop(0, rows, one_row, 0, unroll=2)


def finish(chunks, normed, gain, proj, out_gate):
    rows, cols, width = normed.shape
    channels = sum(c.shape[0] for c in chunks)
    block = pl.BlockSpec((ROWS, cols, width), lambda r: (r, 0, 0))
    whole = lambda shape: pl.BlockSpec(shape, lambda r: (0,) * len(shape))
    return pl.pallas_call(
        functools.partial(finish_kernel, len(chunks)),
        grid=(rows // ROWS,),
        in_specs=[pl.BlockSpec(memory_space=pltpu.SMEM), block, whole(proj.shape), whole(out_gate.shape)]
        + [pl.BlockSpec((c.shape[0], ROWS, cols), lambda r: (0, r, 0)) for c in chunks],
        out_specs=block,
        out_shape=jax.ShapeDtypeStruct(normed.shape, jnp.bfloat16),
        scratch_shapes=[pltpu.VMEM((cols // LANES, channels * ROWS, LANES), jnp.float32)],
        compiler_params=params(),
        name="finish",
    )(gain, normed, proj, out_gate, *chunks)

ALL = ("z", "y", "x", "core")


def exchange(x, axes):
    return lax.all_to_all(x, axes, split_axis=0, concat_axis=0, tiled=True)


def per_device(
    pair_input, token_mask, norm_gain, left_gate, left_value, right_gate, right_value, sum_gain, out_gate, out_proj
):
    rows, cols, _ = pair_input.shape
    hidden = left_gate.shape[1]
    chip = lax.axis_index(("z", "y", "x"))
    valid = token_mask.astype(jnp.float32)
    row_valid = lax.dynamic_slice_in_dim(valid, chip * rows, rows, 0)
    col_valid = lax.dynamic_slice_in_dim(valid, lax.axis_index("core") * cols, cols, 0)
    owners = lax.axis_size(ALL)
    sizes = (hidden // owners,)
    planes = lax.axis_size("z")
    place = jnp.arange(planes, dtype=jnp.int32)
    normed, right = project(
        pair_input, right_gate, right_value, norm_gain, row_valid, col_valid, sizes, owners, True
    )
    right = exchange(right, ALL)
    (left,) = project(normed, left_gate, left_value, norm_gain, row_valid, col_valid, sizes, owners, False)
    left = exchange(left, ALL)
    outs = contract([(left, p) for p in range(planes)], [(right, p) for p in range(planes)], place)
    returned = exchange(jnp.concatenate(outs), ALL)
    returned = returned.reshape(hidden, rows, cols)
    return finish([returned], normed, sum_gain, out_proj, out_gate)


def solution(mesh):
    grid = mesh.devices
    fine = Mesh(
        grid.reshape(grid.shape[0], grid.shape[1] // 4, 2, 2, grid.shape[2]), ("groups", "z", "y", "x", "core")
    )
    pair = P(("groups", "z", "y", "x"), "core", None)
    return jax.shard_map(
        per_device, mesh=fine, in_specs=(pair, P("groups")) + (P(),) * 8, out_specs=pair, check_vma=False
    )
```

time: 459 us -> 405 us (0.88)
  blocking collectives: 112 us -> 330 us
  waiting for transfers between devices: 189 us -> 0 us
  Pallas kernels: 0 us -> 63.6 us
  matrix products: 55.8 us -> 0 us
  starting transfers between devices: 31.1 us -> 0 us
  local copies, waits for them, and re-layouts: 31 us -> 5.26 us
  other arithmetic: 25.2 us -> 5.27 us
  between operations: 13.7 us -> 0.04 us
    all_to_all x1 -> x3, blocking collectives: 112 us -> 330 us  [exchange(): return lax.all_to_all(x, axes, split_axis=0, concat_axis=0, tiled=True)]
    all_to_all x2 -> x0, waiting for transfers between devices: 144 us -> none  [the longest x1 82.3 us: per_device(): lax.all_to_all(right_op, 'chan', split_axis=0, concat_axis=1, tiled=True)]
    pallas_call x0 -> x4, Pallas kernels: none -> 63.6 us  [the longest x2 37.7 us: project(): pl.pallas_call(functools.partial(project_kernel, sizes, owners, hidden, n...]
    dot_general x7 -> x0, matrix products: 55.8 us -> none  [the longest x4 35.7 us: project(): jnp.einsum('ikd,dh->hik', normed, weight, preferred_element_type=jnp.floa...]
    reduce_scatter x1 -> x0, waiting for transfers between devices: 44.5 us -> none  [per_device(): lax.psum_scatter(partial_value, 'grow', scatter_dimension=2, tiled=True)]
    all_to_all x2 -> x0, starting transfers between devices: 30.9 us -> none  [the longest x1 22.4 us: per_device(): lax.all_to_all(right_op, 'chan', split_axis=0, concat_axis=1, tiled=True)]
    convert_element_type x4 -> x0, local copies, waits for them, and re-layouts: 21.7 us -> none  [the longest x1 7.1 us: per_device(): (jax.nn.sigmoid(project(left_gate)) * project(left_value) * pair_mask).as...]
    reduce_sum x4 -> x0, other arithmetic: 12.8 us -> none  [the longest x2 8.41 us: layer_norm(): spread = jnp.mean(centred * centred, axis=along_axis, keepdims=True)]
  transfers between devices with their start and end apart: 3 -> 0, of which waited for: 3 -> 0; matrix products, arithmetic and copies ran while one was open for 7% -> 0% of each run, Pallas kernels for 0% -> 0%
where the time goes in v1:
time: 405 us; the launch traced here: 404 us
  blocking collectives  330 us (81%)
  Pallas kernels  63.6 us (16%)
  other arithmetic  5.27 us (1%)
  local copies, waits for them, and re-layouts  5.26 us (1%)
    all_to_all x3, blocking collectives, exchange(): return lax.all_to_all(x, axes, split_axis=0, concat_axis=0, tiled=True)  330 us
    pallas_call x2, Pallas kernels, project(): pl.pallas_call(functools.partial(project_kernel, sizes, owners, hidden, n...  37.7 us
    pallas_call x1, Pallas kernels, finish(): pl.pallas_call(functools.partial(finish_kernel, len(chunks)), grid=(rows...  16.5 us
    pallas_call x1, Pallas kernels, contract(): pl.pallas_call(functools.partial(contract_kernel, len(lefts), len(rights)...  9.45 us

profile of v1, /device:TPU:0, one launch (start us, length us, event | category | flops | bytes accessed | tf_op | source)
XLA Modules:
  0.0 404.0 jit_solution(7230913622806051552)
XLA Ops:
  0.0 0.7 convert_element_type.3
  0.7 0.6 dynamic_slice.6.row_ref
  1.2 0.1 dynamic_slice.7
  1.3 0.6 broadcast_in_dim.8.col_ref
  1.9 0.9 copy.11
  2.8 0.9 copy.12
  3.6 0.9 copy.13
  4.5 0.9 copy.14
  5.4 0.6 maximum_bitcast_fusion.w_ref
  6.0 0.6 maximum_bitcast_fusion.1.w_ref
  6.7 22.0 %project.2 = (bf16[48,384,128]{2,1,0:T(8,128)(2,1)}, bf16[32,4,48,384]{3,2,1,0:T(8,128)(2,1)}) custom-call(f32[48]{0:T(128)} %dynamic_slice.6.row_ref, f32[1,384]{1,0:T(1,128)} %broadcast_in_dim.8.col_ref, bf16[48,384,128]{2,1,0:T(8,128)(2,1)} %x_ref.1, bf16[256,128]{1,0:T(8,128)(2,1)} %maximum_bitcast_fusion.w_ref, f32[1,128]{1,0:T(1,128)} %bitcast.7), custom_call_target="tpu_custom_call" | custom-call | tf_op jit(solution)/shard_map/project/pallas_call | solution.py:73
  28.7 15.7 %project.3 = bf16[32,4,48,384]{3,2,1,0:T(8,128)(2,1)} custom-call(f32[48]{0:T(128)} %dynamic_slice.6.row_ref, f32[1,384]{1,0:T(1,128)} %broadcast_in_dim.8.col_ref, bf16[48,384,128]{2,1,0:T(8,128)(2,1)} %get-tuple-element.11.x_ref.normed_ref, bf16[256,128]{1,0:T(8,128)(2,1)} %maximum_bitcast_fusion.1.w_ref, f32[1,128]{1,0:T(1,128)} %bitcast.8), custom_call_target="tpu_custom_call" | custom-call | tf_op jit(solution)/shard_map/project/pallas_call | solution.py:73
  44.4 0.0 copy-start
  44.4 112.8 %all_to_all.15.refs_0_.refs_1_.refs_2_.refs_3_ = bf16[32,4,48,384]{3,2,1,0:T(8,128)(2,1)} all-to-all(bf16[32,4,48,384]{3,2,1,0:T(8,128)(2,1)} %project.3), channel_id=1, replica_groups=mesh['groups'=1,'z'=4,'y'=2,'x'=2,'core'=2] {'z','y','x','core'}, dimensions={0} | all-to-all | bytes 9437184 | tf_op jit(solution)/shard_map/all_to_all | solution.py:185
  157.2 0.0 copy-done
  157.2 108.5 %all_to_all.16.refs_4_.refs_5_.refs_6_.refs_7_ = bf16[32,4,48,384]{3,2,1,0:T(8,128)(2,1)} all-to-all(bf16[32,4,48,384]{3,2,1,0:T(8,128)(2,1)S(1)} %copy-done), channel_id=1, replica_groups=mesh['groups'=1,'z'=4,'y'=2,'x'=2,'core'=2] {'z','y','x','core'}, dimensions={0} | all-to-all | bytes 9437184 | tf_op jit(solution)/shard_map/all_to_all | solution.py:185
  265.7 0.6 iota.3.place_ref
  266.3 9.4 %contract.1 = (bf16[8,4,48,384]{3,2,1,0:T(8,128)(2,1)}, bf16[8,4,48,384]{3,2,1,0:T(8,128)(2,1)}, bf16[8,4,48,384]{3,2,1,0:T(8,128)(2,1)}, bf16[8,4,48,384]{3,2,1,0:T(8,128)(2,1)}) custom-call(s32[4]{0:T(128)} %iota.3.place_ref, bf16[32,4,48,384]{3,2,1,0:T(8,128)(2,1)} %all_to_all.15.refs_0_.refs_1_.refs_2_.refs_3_, ...), custom_call_target="tpu_custom_call" | custom-call | tf_op jit(solution)/shard_map/contract/pallas_call | solution.py:118
  275.7 3.3 pad_maximum_fusion
  279.1 108.5 %all_to_all.17 = bf16[32,4,48,384]{3,2,1,0:T(8,128)(2,1)} all-to-all(bf16[32,4,48,384]{3,2,1,0:T(8,128)(2,1)S(1)} %pad_maximum_fusion), channel_id=1, replica_groups=mesh['groups'=1,'z'=4,'y'=2,'x'=2,'core'=2] {'z','y','x','core'}, dimensions={0} | all-to-all | bytes 9437184 | tf_op jit(solution)/shard_map/all_to_all | solution.py:185
  387.6 16.5 %finish.1 = bf16[48,384,128]{2,1,0:T(8,128)(2,1)} custom-call(f32[128]{0:T(128)} %gain_ref.1, bf16[48,384,128]{2,1,0:T(8,128)(2,1)} %get-tuple-element.11.x_ref.normed_ref, bf16[128,128]{1,0:T(8,128)(2,1)} %proj_ref.1, bf16[128,128]{1,0:T(8,128)(2,1)} %gate_ref.1, bf16[128,48,384]{2,1,0:T(8,128)(2,1)} %bitcast.6), custom_call_target="tpu_custom_call" | custom-call | tf_op jit(solution)/shard_map/finish/pallas_call | solution.py:169
Async XLA Ops:
  44.4 112.8 %copy-start = (bf16[32,4,48,384]{3,2,1,0:T(8,128)(2,1)S(1)}, bf16[32,4,48,384]{3,2,1,0:T(8,128)(2,1)}, u32[]{:S(2)}) copy-start(bf16[32,4,48,384]{3,2,1,0:T(8,128)(2,1)} %get-tuple-element.12) | copy-start | bytes 14155780

commit v2 on v1

v2 whole, which is shorter than its diff:
```python
import functools

import jax
import jax.numpy as jnp
from jax import lax
from jax.experimental import pallas as pl
from jax.experimental.pallas import tpu as pltpu
from jax.sharding import Mesh
from jax.sharding import PartitionSpec as P

norm_eps = 1e-05
ROWS = 16
LANES = 128
VMEM_BYTES = 56 * 1024 * 1024
HALF = ("near", "y", "x", "core")
ALL = ("half", *HALF)
SPLIT = (5, 3)


def params():
    return pltpu.CompilerParams(vmem_limit_bytes=VMEM_BYTES)


def sigmoid(x):
    grown = 1.0 + jnp.exp(-jnp.maximum(x, -80.0))
    guess = pl.reciprocal(grown, approx=True)
    return guess * (2.0 - grown * guess)


def spec_whole(shape):
    return pl.BlockSpec(shape, lambda r: (0,) * len(shape))


SMEM = pl.BlockSpec(memory_space=pltpu.SMEM)


def project_kernel(low, high, norm_first, write, mask_ref, col_ref, at_ref, x_ref, gate_ref, value_ref, gain_ref, *refs):
    *outs, held, w_ref = refs
    count = high - low
    step = pl.program_id(0)

    @pl.when(step == 0)
    def _():
        w_ref[:count] = gate_ref[...].astype(jnp.float32).T[low:high].astype(jnp.bfloat16)
        w_ref[count:] = value_ref[...].astype(jnp.float32).T[low:high].astype(jnp.bfloat16)

    first_row = at_ref[0] + step * ROWS
    col_valid = col_ref[at_ref[1]].astype(jnp.float32)
    if norm_first:
        normed_ref, *outs = outs

    def one_row(i, _):
        if norm_first:
            x = x_ref[i].astype(jnp.float32)
            centred = x - jnp.mean(x, axis=-1, keepdims=True)
            spread = jnp.mean(centred * centred, axis=-1, keepdims=True)
            normed = (centred * lax.rsqrt(spread + norm_eps) * gain_ref[...]).astype(jnp.bfloat16)
            normed_ref[i] = normed
        else:
            normed = x_ref[i]
        both = lax.dot_general(w_ref[...], normed, (((1,), (1,)), ((), ())), preferred_element_type=jnp.float32)
        valid = col_valid * mask_ref[first_row + i].astype(jnp.float32)
        gated = sigmoid(both[:count]) * both[count:] * valid
        for j in range(held.shape[0]):
            held[j, pl.ds(pl.multiple_of(i * count, 8), count), :] = gated[:, j * LANES:(j + 1) * LANES]
        return 0

    lax.fori_loop(0, ROWS, one_row, 0, unroll=2)

    def channel(j, c):
        return held[j, pl.ds(c, ROWS, stride=count), :].astype(jnp.bfloat16)

    write(outs, channel, at_ref)


def write_right(size, owners, outs, channel, at_ref):
    (out,) = outs

    def one_owner(o, _):
        for e in range(size):
            for j in range(out.shape[-1] // LANES):
                block = channel(j, o * size + e)
                for h in range(2):
                    out[h * owners + o, e, :, j * LANES:(j + 1) * LANES] = block
        return 0

    lax.fori_loop(0, owners, one_owner, 0, unroll=2)


def write_left(sizes, owners, outs, channel, at_ref):
    for d, out in enumerate(outs):
        owner = at_ref[2] ^ d
        first = 0
        for size in sizes:
            for e in range(size):
                for j in range(out.shape[-1] // LANES):
                    out[first + e, :, j * LANES:(j + 1) * LANES] = channel(j, first * owners + owner * size + e)
            first += size


def project(x, gate, value, gain, mask, col_mask, at, low, high, norm_first, write, out_blocks):
    rows, cols, width = x.shape
    count = high - low
    x_spec = pl.BlockSpec((ROWS, cols, width), lambda r: (r, 0, 0))
    out_shape = [jax.ShapeDtypeStruct((*lead, rows, cols), jnp.bfloat16) for lead in out_blocks]
    out_specs = [pl.BlockSpec((*lead, ROWS, cols), lambda r, n=len(lead): (0,) * n + (r, 0)) for lead in out_blocks]
    if norm_first:
        out_shape = [jax.ShapeDtypeStruct(x.shape, jnp.bfloat16), *out_shape]
        out_specs = [x_spec, *out_specs]
    return pl.pallas_call(
        functools.partial(project_kernel, low, high, norm_first, write),
        grid=(rows // ROWS,),
        in_specs=[SMEM, spec_whole(col_mask.shape), SMEM, x_spec]
        + [spec_whole(gate.shape)] * 2 + [spec_whole((1, width))],
        out_specs=out_specs,
        out_shape=out_shape,
        scratch_shapes=[
            pltpu.VMEM((cols // LANES, ROWS * count, LANES), jnp.float32),
            pltpu.VMEM((2 * count, width), jnp.bfloat16),
        ],
        compiler_params=params(),
        cost_estimate=pl.CostEstimate(
            flops=4 * rows * cols * width * count, bytes_accessed=8 * rows * cols * width, transcendentals=rows * cols * count
        ),
        name="project",
    )(mask, col_mask, at, x, gate, value, gain[None])


def contract_kernel(n, by_partner, rows, cols, at_ref, *refs):
    lefts, right = refs[:n], refs[n]
    outs = refs[n + 1:-3]
    left_all, right_all, sums = refs[-3:]
    for s in range(right.shape[0]):
        right_all[s % 2, (s // 2) * rows:(s // 2 + 1) * rows, :] = right[s, 0]
    for d, left in enumerate(lefts):
        source = at_ref[2] ^ d
        left_all[source & 1, pl.ds(pl.multiple_of((source >> 1) * rows, rows), rows), :] = left[0]
    dims = (((1,), (1,)), ((), ()))
    for k in range(2):
        total = sum(
            lax.dot_general(left_all[p], right_all[p, k * cols:(k + 1) * cols, :], dims, preferred_element_type=jnp.float32)
            for p in range(2)
        ).astype(jnp.bfloat16)
        if by_partner:
            sums[k] = total
        else:
            for b in range(n // 2):
                outs[0][2 * b + k, 0] = total[b * rows:(b + 1) * rows]
    if by_partner:
        for d, out in enumerate(outs):
            target = at_ref[2] ^ d
            out[0] = sums[target & 1, pl.ds(pl.multiple_of((target >> 1) * rows, rows), rows), :]


def contract(lefts, right, at, first, by_partner):
    everyone, size, rows, cols = right.shape
    n = len(lefts)
    out_shape = [jax.ShapeDtypeStruct((size, rows, cols), jnp.bfloat16)] * n
    out_specs = [pl.BlockSpec((1, rows, cols), lambda q: (q, 0, 0))] * n
    if not by_partner:
        out_shape = [jax.ShapeDtypeStruct((n, size, rows, cols), jnp.bfloat16)]
        out_specs = [pl.BlockSpec((n, 1, rows, cols), lambda q: (0, q, 0, 0))]
    return pl.pallas_call(
        functools.partial(contract_kernel, n, by_partner, rows, cols),
        grid=(size,),
        in_specs=[SMEM]
        + [pl.BlockSpec((1, rows, cols), lambda q: (first + q, 0, 0))] * n
        + [pl.BlockSpec((everyone, 1, rows, cols), lambda q: (0, q, 0, 0))],
        out_specs=out_specs,
        out_shape=out_shape,
        scratch_shapes=[
            pltpu.VMEM((2, n // 2 * rows, cols), jnp.bfloat16),
            pltpu.VMEM((2, everyone // 2 * rows, cols), jnp.bfloat16),
            pltpu.VMEM((2, n // 2 * rows, cols), jnp.bfloat16),
        ],
        compiler_params=params(),
        cost_estimate=pl.CostEstimate(
            flops=size * 2 * n * n * everyone // 4 * rows * rows * cols,
            bytes_accessed=size * (everyone + 2 * n) * rows * cols * 2,
            transcendentals=0,
        ),
        name="contract",
    )(at, *lefts, right)


def finish_kernel(plan, at_ref, gain_ref, normed_ref, proj_ref, gate_ref, *refs):
    blocks, out_ref, held = refs[:len(plan)], refs[-2], refs[-1]
    rows, cols = normed_ref.shape[:2]
    pieces = []
    for block, (first, size, partner) in zip(blocks, plan):
        if partner is None:
            pieces += [(block.at[o, e], first + o * size + e) for o in range(block.shape[0]) for e in range(size)]
        else:
            base = first + (at_ref[2] ^ partner) * size
            pieces += [(block.at[e], base + e) for e in range(size)]
    channels = len(pieces)
    total = jnp.zeros((rows, cols), jnp.float32)
    for piece, _ in pieces:
        total = total + piece[...].astype(jnp.float32)
    average = total * (1.0 / channels)
    spread = jnp.zeros((rows, cols), jnp.float32)
    for piece, _ in pieces:
        centred = piece[...].astype(jnp.float32) - average
        spread = spread + centred * centred
    scale = lax.rsqrt(spread * (1.0 / channels) + norm_eps)
    for piece, c in pieces:
        mixed = (piece[...].astype(jnp.float32) - average) * scale * gain_ref[c]
        for j in range(held.shape[0]):
            held[j, pl.ds(pl.multiple_of(c * rows, rows), rows), :] = mixed[:, j * LANES:(j + 1) * LANES]

    def one_row(i, _):
        mixed = jnp.concatenate(
            [held[j, pl.ds(i, channels, stride=rows), :] for j in range(held.shape[0])], axis=1
        ).astype(jnp.bfloat16)
        linear = lax.dot_general(mixed, proj_ref[...], (((0,), (0,)), ((), ())), preferred_element_type=jnp.float32)
        gate = jnp.dot(normed_ref[i], gate_ref[...], preferred_element_type=jnp.float32)
        out_ref[i] = (sigmoid(gate) * linear).astype(jnp.bfloat16)
        return 0

    lax.fori_loop(0, rows, one_row, 0, unroll=2)


def finish(blocks, plan, at, normed, gain, proj, out_gate):
    rows, cols, width = normed.shape
    pair = pl.BlockSpec((ROWS, cols, width), lambda r: (r, 0, 0))
    return pl.pallas_call(
        functools.partial(finish_kernel, plan),
        grid=(rows // ROWS,),
        in_specs=[SMEM, SMEM, pair, spec_whole(proj.shape), spec_whole(out_gate.shape)]
        + [pl.BlockSpec((*b.shape[:-2], ROWS, cols), lambda r, n=b.ndim - 2: (0,) * n + (r, 0)) for b in blocks],
        out_specs=pair,
        out_shape=jax.ShapeDtypeStruct(normed.shape, jnp.bfloat16),
        scratch_shapes=[pltpu.VMEM((cols // LANES, proj.shape[0] * ROWS, LANES), jnp.float32)],
        compiler_params=params(),
        name="finish",
    )(at, gain, normed, proj, out_gate, *blocks)


def exchange(x, axes):
    return lax.all_to_all(x, axes, split_axis=0, concat_axis=0, tiled=True)


def partners(blocks):
    n = len(blocks)
    return [blocks[0]] + [lax.ppermute(blocks[d], HALF, [(i, i ^ d) for i in range(n)]) for d in range(1, n)]


def after(x, *others):
    return lax.optimization_barrier((x, *others))[0]


def per_device(
    pair_input, token_mask, norm_gain, left_gate, left_value, right_gate, right_value, sum_gain, out_gate, out_proj
):
    rows, cols, _ = pair_input.shape
    hidden = left_gate.shape[1]
    owners = lax.axis_size(HALF)
    chip = lax.axis_index(("half", "near", "y", "x"))
    at = jnp.stack([chip * rows, lax.axis_index("core"), lax.axis_index(HALF)]).astype(jnp.int32)
    col_mask = token_mask.reshape(-1, 1, cols)
    own = hidden // owners
    share = own // sum(SPLIT)
    sizes = tuple(s * share for s in SPLIT)
    firsts = tuple(sum(sizes[:q]) for q in range(len(sizes)))

    def right_chunk(x, q, norm_first):
        return project(
            x, right_gate, right_value, norm_gain, token_mask, col_mask, at,
            firsts[q] * owners, (firsts[q] + sizes[q]) * owners, norm_first,
            functools.partial(write_right, sizes[q], owners), [(2 * owners, sizes[q])],
        )

    normed, right = right_chunk(pair_input, 0, True)
    rights = [exchange(right, ALL)]
    lefts = project(
        normed, left_gate, left_value, norm_gain, token_mask, col_mask, at, 0, hidden, False,
        functools.partial(write_left, sizes, owners), [(own,)] * owners,
    )
    lefts = partners(lefts)
    for q in range(1, len(sizes)):
        (right,) = right_chunk(normed, q, False)
        rights.append(exchange(after(right, rights[-1], *lefts), ALL))
    blocks, plan = [], []
    for q, size in enumerate(sizes):
        last = q == len(sizes) - 1
        outs = contract(lefts, rights[q] if q == 0 else after(rights[q], *blocks), at, firsts[q], not last)
        if last:
            blocks.append(exchange(outs[0], HALF))
            plan.append((firsts[q] * owners, size, None))
        else:
            blocks += partners(outs)
            plan += [(firsts[q] * owners, size, d) for d in range(owners)]
    return finish(blocks, tuple(plan), at, normed, sum_gain, out_proj, out_gate)


def solution(mesh):
    grid = mesh.devices
    fine = Mesh(
        grid.reshape(grid.shape[0], 2, grid.shape[1] // 8, 2, 2, grid.shape[2]), ("groups", *ALL)
    )
    pair = P(("groups", "half", "near", "y", "x"), "core", None)
    return jax.shard_map(
        per_device, mesh=fine, in_specs=(pair, P("groups")) + (P(),) * 8, out_specs=pair, check_vma=False
    )
```

time: 405 us -> 343 us (0.85)
  blocking collectives: 330 us -> 28.3 us
  waiting for transfers between devices: 0 us -> 170 us
  starting transfers between devices: 0 us -> 64 us
  Pallas kernels: 63.6 us -> 75.8 us
  other arithmetic: 5.27 us -> 0.64 us
    all_to_all x3 -> x1, blocking collectives: 330 us -> 28.3 us  [exchange(): return lax.all_to_all(x, axes, split_axis=0, concat_axis=0, tiled=True)]
    ppermute x0 -> x30, waiting for transfers between devices: none -> 170 us  [partners(): lax.ppermute(blocks[d], HALF, [(i, i ^ d) for i in range(n)])]
    ppermute x0 -> x30, starting transfers between devices: none -> 53.8 us  [partners(): lax.ppermute(blocks[d], HALF, [(i, i ^ d) for i in range(n)])]
    pallas_call x4 -> x6, Pallas kernels: 63.6 us -> 75.8 us  [the longest x3 43.8 us: project(): pl.pallas_call(functools.partial(project_kernel, low, high, norm_first, w...]
    all_to_all x0 -> x2, starting transfers between devices: none -> 10.2 us  [exchange(): return lax.all_to_all(x, axes, split_axis=0, concat_axis=0, tiled=True)]
  transfers between devices with their start and end apart: 0 -> 32, of which waited for: 0 -> 24; matrix products, arithmetic and copies ran while one was open for 0% -> 0% of each run, Pallas kernels for 0% -> 10%
where the time goes in v2:
time: 343 us; the launch traced here: 342 us
  waiting for transfers between devices  170 us (50%)
  Pallas kernels  75.8 us (22%)
  starting transfers between devices  64 us (19%)
  blocking collectives  28.3 us (8%)
  local copies, waits for them, and re-layouts  3.78 us (1%)
    ppermute x30, waiting for transfers between devices, partners(): lax.ppermute(blocks[d], HALF, [(i, i ^ d) for i in range(n)])  170 us
    ppermute x30, starting transfers between devices, partners(): lax.ppermute(blocks[d], HALF, [(i, i ^ d) for i in range(n)])  53.8 us
    pallas_call x3, Pallas kernels, project(): pl.pallas_call(functools.partial(project_kernel, low, high, norm_first, w...  43.8 us
    all_to_all x1, blocking collectives, exchange(): return lax.all_to_all(x, axes, split_axis=0, concat_axis=0, tiled=True)  28.3 us
    pallas_call x1, Pallas kernels, finish(): pl.pallas_call(functools.partial(finish_kernel, plan), grid=(rows // ROWS...  16.7 us
    pallas_call x2, Pallas kernels, contract(): pl.pallas_call(functools.partial(contract_kernel, n, by_partner, rows, co...  15.2 us
    all_to_all x2, starting transfers between devices, exchange(): return lax.all_to_all(x, axes, split_axis=0, concat_axis=0, tiled=True)  10.2 us
  transfers between devices with their start and end apart: 32, of which 24 were waited for; matrix products, arithmetic and copies ran while one was open for 0% of the time, Pallas kernels for 10%

profile of v2, /device:TPU:0, one launch (start us, length us, event | category | flops | bytes accessed | tf_op | source)
XLA Modules:
  0.0 342.3 jit_solution(17755910538907556623)
XLA Ops:
  1.9 17.5 %project.3 = (bf16[48,384,128]{2,1,0:T(8,128)(2,1)}, bf16[32,5,48,384]{3,2,1,0:T(8,128)(2,1)}) custom-call(s32[768]{0:T(1024)} %mask_ref.5, s32[2,1,384]{2,1,0:T(1,128)} %reshape.3.col_ref, s32[3]{0:T(128)} %pad_add_fusion.at_ref, bf16[48,384,128]{2,1,0:T(8,128)(2,1)} %x_ref.1, bf16[128,128]{1,0:T(8,128)(2,1)} %gate_ref.6, bf16[128,128]{1,0:T(8,128)(2,1)} %value_ref.5, ...), custom_call_target="tpu_custom_call" | custom-call | flops 754974720 | bytes 18874368 | tf_op jit(solution)/shard_map/project/pallas_call | solution.py:110
  19.4 7.4 %all-to-all-start = ((bf16[32,5,48,384]{3,2,1,0:T(8,128)(2,1)}), bf16[32,5,48,384]{3,2,1,0:T(8,128)(2,1)}, u32[]{:S(2)}, u32[]{:S(2)}) async-start(bf16[32,5,48,384]{3,2,1,0:T(8,128)(2,1)} %get-tuple-element.58), calls=%async_computation | async-start | bytes 11796480 | tf_op jit(solution)/shard_map/all_to_all | solution.py:240
  26.8 16.5 %project.4 = (bf16[8,48,384]{2,1,0:T(8,128)(2,1)}, bf16[8,48,384]{2,1,0:T(8,128)(2,1)}, bf16[8,48,384]{2,1,0:T(8,128)(2,1)}, bf16[8,48,384]{2,1,0:T(8,128)(2,1)}...) custom-call(s32[768]{0:T(1024)} %mask_ref.5, ...), custom_call_target="tpu_custom_call" | custom-call | flops 1207959552 | bytes 18874368 | tf_op jit(solution)/shard_map/project/pallas_call | solution.py:110
  43.6 1.7 collective-permute-start.1
  45.3 1.7 collective-permute-start.3
  47.1 2.6 collective-permute-start.5
  49.7 26.1 %collective-permute-done.1.refs_2_ = bf16[8,48,384]{2,1,0:T(8,128)(2,1)} collective-permute-done((bf16[8,48,384]{2,1,0:T(8,128)(2,1)}, bf16[8,48,384]{2,1,0:T(8,128)(2,1)}, u32[]{:S(2)}, u32[]{:S(2)}) %collective-permute-start.1) | collective-permute-done | bytes 294944 | tf_op jit(solution)/shard_map/ppermute | solution.py:245
  75.7 4.3 %collective-permute-start.6 = (bf16[8,48,384]{2,1,0:T(8,128)(2,1)}, bf16[8,48,384]{2,1,0:T(8,128)(2,1)}, u32[]{:S(2)}, u32[]{:S(2)}) collective-permute-start(bf16[8,48,384]{2,1,0:T(8,128)(2,1)} %get-tuple-element.49), channel_id=1, source_target_pairs={{0,7},{1,6},{2,5},{3,4},{4,3},{5,2},{6,1},{7,0},{8,15},{9,14},{10,... | collective-permute-start | bytes 884744 | tf_op jit(solution)/shard_map/ppermute | solution.py:245
  80.0 8.4 %collective-permute-done.2.refs_3_ = bf16[8,48,384]{2,1,0:T(8,128)(2,1)} collective-permute-done((bf16[8,48,384]{2,1,0:T(8,128)(2,1)}, bf16[8,48,384]{2,1,0:T(8,128)(2,1)}, u32[]{:S(2)}, u32[]{:S(2)}) %collective-permute-start.2) | collective-permute-done | bytes 294944 | tf_op jit(solution)/shard_map/ppermute | solution.py:245
  88.4 8.1 %collective-permute-start.8 = (bf16[8,48,384]{2,1,0:T(8,128)(2,1)}, bf16[8,48,384]{2,1,0:T(8,128)(2,1)}, u32[]{:S(2)}, u32[]{:S(2)}) collective-permute-start(bf16[8,48,384]{2,1,0:T(8,128)(2,1)} %get-tuple-element.51), channel_id=1, source_target_pairs={{0,9},{1,8},{2,11},{3,10},{4,13},{5,12},{6,15},{7,14},{8,1},{9,0},... | collective-permute-start | bytes 884744 | tf_op jit(solution)/shard_map/ppermute | solution.py:245
  96.5 9.7 %collective-permute-done.5.refs_6_ = bf16[8,48,384]{2,1,0:T(8,128)(2,1)} collective-permute-done((bf16[8,48,384]{2,1,0:T(8,128)(2,1)}, bf16[8,48,384]{2,1,0:T(8,128)(2,1)}, u32[]{:S(2)}, u32[]{:S(2)}) %collective-permute-start.5) | collective-permute-done | bytes 294944 | tf_op jit(solution)/shard_map/ppermute | solution.py:245
  106.3 7.5 %collective-permute-done.6.refs_7_ = bf16[8,48,384]{2,1,0:T(8,128)(2,1)} collective-permute-done((bf16[8,48,384]{2,1,0:T(8,128)(2,1)}, bf16[8,48,384]{2,1,0:T(8,128)(2,1)}, u32[]{:S(2)}, u32[]{:S(2)}) %collective-permute-start.6) | collective-permute-done | bytes 294944 | tf_op jit(solution)/shard_map/ppermute | solution.py:245
  113.7 2.0 collective-permute-start.11
  115.7 14.8 %collective-permute-done.7.refs_8_ = bf16[8,48,384]{2,1,0:T(8,128)(2,1)} collective-permute-done((bf16[8,48,384]{2,1,0:T(8,128)(2,1)}, bf16[8,48,384]{2,1,0:T(8,128)(2,1)}, u32[]{:S(2)}, u32[]{:S(2)}) %collective-permute-start.7) | collective-permute-done | bytes 294944 | tf_op jit(solution)/shard_map/ppermute | solution.py:245
  132.0 4.9 %collective-permute-done.8.refs_9_ = bf16[8,48,384]{2,1,0:T(8,128)(2,1)} collective-permute-done((bf16[8,48,384]{2,1,0:T(8,128)(2,1)}, bf16[8,48,384]{2,1,0:T(8,128)(2,1)}, u32[]{:S(2)}, u32[]{:S(2)}) %collective-permute-start.8) | collective-permute-done | bytes 294944 | tf_op jit(solution)/shard_map/ppermute | solution.py:245
  136.8 4.1 %collective-permute-start.13 = (bf16[8,48,384]{2,1,0:T(8,128)(2,1)}, bf16[8,48,384]{2,1,0:T(8,128)(2,1)}, u32[]{:S(2)}, u32[]{:S(2)}) collective-permute-start(bf16[8,48,384]{2,1,0:T(8,128)(2,1)} %get-tuple-element.56), channel_id=1, source_target_pairs={{0,14},{1,15},{2,12},{3,13},{4,10},{5,11},{6,8},{7,9},{8,6},{9,7},... | collective-permute-start | bytes 884744 | tf_op jit(solution)/shard_map/ppermute | solution.py:245
  141.0 2.7 collective-permute-done.9.refs_10_
  143.7 1.9 collective-permute-start.14
  145.5 9.8 %project.5 = bf16[32,3,48,384]{3,2,1,0:T(8,128)(2,1)} custom-call(s32[768]{0:T(1024)} %mask_ref.5, s32[2,1,384]{2,1,0:T(1,128)} %reshape.3.col_ref, s32[3]{0:T(128)} %pad_add_fusion.at_ref, bf16[48,384,128]{2,1,0:T(8,128)(2,1)} %get-tuple-element.41.x_ref.normed_ref, bf16[128,128]{1,0:T(8,128)(2,1)} %gate_ref.6, bf16[128,128]{1,0:T(8,128)(2,1)} %value_ref.5, ...), custom_call_target="tpu_custom_call" | custom-call | flops 452984832 | bytes 18874368 | tf_op jit(solution)/shard_map/project/pallas_call | solution.py:110
  155.4 6.3 %collective-permute-done.11.refs_12_ = bf16[8,48,384]{2,1,0:T(8,128)(2,1)} collective-permute-done((bf16[8,48,384]{2,1,0:T(8,128)(2,1)}, bf16[8,48,384]{2,1,0:T(8,128)(2,1)}, u32[]{:S(2)}, u32[]{:S(2)}) %collective-permute-start.11) | collective-permute-done | bytes 294944 | tf_op jit(solution)/shard_map/ppermute | solution.py:245
  161.7 6.3 %collective-permute-done.12.refs_13_ = bf16[8,48,384]{2,1,0:T(8,128)(2,1)} collective-permute-done((bf16[8,48,384]{2,1,0:T(8,128)(2,1)}, bf16[8,48,384]{2,1,0:T(8,128)(2,1)}, u32[]{:S(2)}, u32[]{:S(2)}) %collective-permute-start.12) | collective-permute-done | bytes 294944 | tf_op jit(solution)/shard_map/ppermute | solution.py:245
  168.0 13.4 %collective-permute-done.13.refs_14_ = bf16[8,48,384]{2,1,0:T(8,128)(2,1)} collective-permute-done((bf16[8,48,384]{2,1,0:T(8,128)(2,1)}, bf16[8,48,384]{2,1,0:T(8,128)(2,1)}, u32[]{:S(2)}, u32[]{:S(2)}) %collective-permute-start.13) | collective-permute-done | bytes 294944 | tf_op jit(solution)/shard_map/ppermute | solution.py:245
  181.4 6.4 %collective-permute-done.14.refs_15_ = bf16[8,48,384]{2,1,0:T(8,128)(2,1)} collective-permute-done((bf16[8,48,384]{2,1,0:T(8,128)(2,1)}, bf16[8,48,384]{2,1,0:T(8,128)(2,1)}, u32[]{:S(2)}, u32[]{:S(2)}) %collective-permute-start.14) | collective-permute-done | bytes 294944 | tf_op jit(solution)/shard_map/ppermute | solution.py:245
  187.7 2.8 all-to-all-start.1
  190.5 9.0 %contract.2 = (bf16[5,48,384]{2,1,0:T(8,128)(2,1)}, bf16[5,48,384]{2,1,0:T(8,128)(2,1)}, bf16[5,48,384]{2,1,0:T(8,128)(2,1)}, bf16[5,48,384]{2,1,0:T(8,128)(2,1)...) custom-call(s32[3]{0:T(128)} %pad_add_fusion.at_ref, ...), custom_call_target="tpu_custom_call" | custom-call | flops 18119393280 | bytes 11796480 | tf_op jit(solution)/shard_map/contract/pallas_call | solution.py:163
  199.7 1.7 collective-permute-start.16
  201.5 1.6 collective-permute-start.18
  203.2 2.6 collective-permute-start.20
  205.8 14.2 %collective-permute-done.16.refs_2_ = bf16[5,48,384]{2,1,0:T(8,128)(2,1)S(1)} collective-permute-done((bf16[5,48,384]{2,1,0:T(8,128)(2,1)}, bf16[5,48,384]{2,1,0:T(8,128)(2,1)S(1)}, u32[]{:S(2)}, u32[]{:S(2)}) %collective-permute-start.16) | collective-permute-done | bytes 184352 | tf_op jit(solution)/shard_map/ppermute | solution.py:245
  220.6 4.1 %collective-permute-done.17.refs_3_ = bf16[5,48,384]{2,1,0:T(8,128)(2,1)S(1)} collective-permute-done((bf16[5,48,384]{2,1,0:T(8,128)(2,1)}, bf16[5,48,384]{2,1,0:T(8,128)(2,1)S(1)}, u32[]{:S(2)}, u32[]{:S(2)}) %collective-permute-start.17) | collective-permute-done | bytes 184352 | tf_op jit(solution)/shard_map/ppermute | solution.py:245
  226.1 6.1 %collective-permute-start.24 = (bf16[5,48,384]{2,1,0:T(8,128)(2,1)}, bf16[5,48,384]{2,1,0:T(8,128)(2,1)S(1)}, u32[]{:S(2)}, u32[]{:S(2)}) collective-permute-start(bf16[5,48,384]{2,1,0:T(8,128)(2,1)} %get-tuple-element.69), channel_id=1, source_target_pairs={{0,10},{1,11},{2,8},{3,9},{4,14},{5,15},{6,12},{7,13},{8,2},{9,3},... | collective-permute-start | bytes 552968 | tf_op jit(solution)/shard_map/ppermute | solution.py:245
  232.2 7.2 %collective-permute-done.20.refs_6_ = bf16[5,48,384]{2,1,0:T(8,128)(2,1)S(1)} collective-permute-done((bf16[5,48,384]{2,1,0:T(8,128)(2,1)}, bf16[5,48,384]{2,1,0:T(8,128)(2,1)S(1)}, u32[]{:S(2)}, u32[]{:S(2)}) %collective-permute-start.20) | collective-permute-done | bytes 184352 | tf_op jit(solution)/shard_map/ppermute | solution.py:245
  239.4 4.2 %collective-permute-done.21.refs_7_ = bf16[5,48,384]{2,1,0:T(8,128)(2,1)S(1)} collective-permute-done((bf16[5,48,384]{2,1,0:T(8,128)(2,1)}, bf16[5,48,384]{2,1,0:T(8,128)(2,1)S(1)}, u32[]{:S(2)}, u32[]{:S(2)}) %collective-permute-start.21) | collective-permute-done | bytes 184352 | tf_op jit(solution)/shard_map/ppermute | solution.py:245
  243.7 3.1 collective-permute-start.26
  246.7 6.4 %collective-permute-done.22.refs_8_ = bf16[5,48,384]{2,1,0:T(8,128)(2,1)S(1)} collective-permute-done((bf16[5,48,384]{2,1,0:T(8,128)(2,1)}, bf16[5,48,384]{2,1,0:T(8,128)(2,1)S(1)}, u32[]{:S(2)}, u32[]{:S(2)}) %collective-permute-start.22) | collective-permute-done | bytes 184352 | tf_op jit(solution)/shard_map/ppermute | solution.py:245
  253.1 1.9 collective-permute-start.27
  255.0 2.0 collective-permute-done.23.refs_9_
  257.0 3.8 %collective-permute-start.28 = (bf16[5,48,384]{2,1,0:T(8,128)(2,1)}, bf16[5,48,384]{2,1,0:T(8,128)(2,1)S(1)}, u32[]{:S(2)}, u32[]{:S(2)}) collective-permute-start(bf16[5,48,384]{2,1,0:T(8,128)(2,1)} %get-tuple-element.73), channel_id=1, source_target_pairs={{0,14},{1,15},{2,12},{3,13},{4,10},{5,11},{6,8},{7,9},{8,6},{9,7},... | collective-permute-start | bytes 552968 | tf_op jit(solution)/shard_map/ppermute | solution.py:245
  261.0 2.8 collective-permute-start.29
  263.8 4.0 %collective-permute-done.25.refs_11_ = bf16[5,48,384]{2,1,0:T(8,128)(2,1)S(1)} collective-permute-done((bf16[5,48,384]{2,1,0:T(8,128)(2,1)}, bf16[5,48,384]{2,1,0:T(8,128)(2,1)S(1)}, u32[]{:S(2)}, u32[]{:S(2)}) %collective-permute-start.25) | collective-permute-done | bytes 184352 | tf_op jit(solution)/shard_map/ppermute | solution.py:245
  267.8 3.9 %collective-permute-done.26.refs_12_ = bf16[5,48,384]{2,1,0:T(8,128)(2,1)S(1)} collective-permute-done((bf16[5,48,384]{2,1,0:T(8,128)(2,1)}, bf16[5,48,384]{2,1,0:T(8,128)(2,1)S(1)}, u32[]{:S(2)}, u32[]{:S(2)}) %collective-permute-start.26) | collective-permute-done | bytes 184352 | tf_op jit(solution)/shard_map/ppermute | solution.py:245
  271.8 4.0 %collective-permute-done.27.refs_13_ = bf16[5,48,384]{2,1,0:T(8,128)(2,1)S(1)} collective-permute-done((bf16[5,48,384]{2,1,0:T(8,128)(2,1)}, bf16[5,48,384]{2,1,0:T(8,128)(2,1)S(1)}, u32[]{:S(2)}, u32[]{:S(2)}) %collective-permute-start.27) | collective-permute-done | bytes 184352 | tf_op jit(solution)/shard_map/ppermute | solution.py:245
  275.8 9.2 %collective-permute-done.28.refs_14_ = bf16[5,48,384]{2,1,0:T(8,128)(2,1)S(1)} collective-permute-done((bf16[5,48,384]{2,1,0:T(8,128)(2,1)}, bf16[5,48,384]{2,1,0:T(8,128)(2,1)S(1)}, u32[]{:S(2)}, u32[]{:S(2)}) %collective-permute-start.28) | collective-permute-done | bytes 184352 | tf_op jit(solution)/shard_map/ppermute | solution.py:245
  285.8 3.4 collective-permute-done.29.refs_15_
  289.2 1.8 copy-done
  291.0 6.2 %contract.3 = bf16[16,3,48,384]{3,2,1,0:T(8,128)(2,1)} custom-call(s32[3]{0:T(128)} %pad_add_fusion.at_ref, bf16[8,48,384]{2,1,0:T(8,128)(2,1)} %get-tuple-element.42.refs_0_, bf16[8,48,384]{2,1,0:T(8,128)(2,1)} %collective-permute-done.refs_1_, bf16[8,48,384]{2,1,0:T(8,128)(2,1)} %collective-permute-done.1.refs_2_, ...), custom_call_target="tpu_custom_call" | custom-call | flops 10871635968 | bytes 7077888 | tf_op jit(solution)/shard_map/contract/pallas_call | solution.py:163
  297.2 28.3 %all_to_all.15.refs_16_ = bf16[16,3,48,384]{3,2,1,0:T(8,128)(2,1)} all-to-all(bf16[16,3,48,384]{3,2,1,0:T(8,128)(2,1)} %contract.3), channel_id=1, replica_groups=mesh['groups'=1,'half'=2,'near'=2,'y'=2,'x'=2,'core'=2] {'near','y','x',..., dimensions={0} | all-to-all | bytes 3538944 | tf_op jit(solution)/shard_map/all_to_all | solution.py:240
  325.5 16.7 %finish.1 = bf16[48,384,128]{2,1,0:T(8,128)(2,1)} custom-call(s32[3]{0:T(128)} %pad_add_fusion.at_ref, f32[128]{0:T(128)} %gain_ref.1, bf16[48,384,128]{2,1,0:T(8,128)(2,1)} %get-tuple-element.41.x_ref.normed_ref, bf16[128,128]{1,0:T(8,128)(2,1)} %proj_ref.1, bf16[128,128]{1,0:T(8,128)(2,1)} %gate_ref.7, bf16[5,48,384]{2,1,0:T(8,128)(2,1)} %get-tuple-element.59.refs_0_, ...), custom_call_target="tpu_custom_call" | custom-call | tf_op jit(solution)/shard_map/finish/pallas_call | solution.py:226
  (55 shorter events, 7.0 us)
Async XLA Ops:
  19.4 168.3 %all-to-all-start = ((bf16[32,5,48,384]{3,2,1,0:T(8,128)(2,1)}), bf16[32,5,48,384]{3,2,1,0:T(8,128)(2,1)}, u32[]{:S(2)}, u32[]{:S(2)}) async-start(bf16[32,5,48,384]{3,2,1,0:T(8,128)(2,1)} %get-tuple-element.58), calls=%async_computation | async-start | bytes 11796480 | tf_op jit(solution)/shard_map/all_to_all | solution.py:240
  43.3 3.7 %collective-permute-start = (bf16[8,48,384]{2,1,0:T(8,128)(2,1)}, bf16[8,48,384]{2,1,0:T(8,128)(2,1)}, u32[]{:S(2)}, u32[]{:S(2)}) collective-permute-start(bf16[8,48,384]{2,1,0:T(8,128)(2,1)} %get-tuple-element.43), channel_id=1, source_target_pairs={{0,1},{1,0},{2,3},{3,2},{4,5},{5,4},{6,7},{7,6},{8,9},{9,8},{10,11... | collective-permute-start | bytes 884744 | tf_op jit(solution)/shard_map/ppermute | solution.py:245
  43.6 32.1 %collective-permute-start.1 = (bf16[8,48,384]{2,1,0:T(8,128)(2,1)}, bf16[8,48,384]{2,1,0:T(8,128)(2,1)}, u32[]{:S(2)}, u32[]{:S(2)}) collective-permute-start(bf16[8,48,384]{2,1,0:T(8,128)(2,1)} %get-tuple-element.44), channel_id=1, source_target_pairs={{0,2},{1,3},{2,0},{3,1},{4,6},{5,7},{6,4},{7,5},{8,10},{9,11},{10,... | collective-permute-start | bytes 884744 | tf_op jit(solution)/shard_map/ppermute | solution.py:245
  45.2 43.2 %collective-permute-start.2 = (bf16[8,48,384]{2,1,0:T(8,128)(2,1)}, bf16[8,48,384]{2,1,0:T(8,128)(2,1)}, u32[]{:S(2)}, u32[]{:S(2)}) collective-permute-start(bf16[8,48,384]{2,1,0:T(8,128)(2,1)} %get-tuple-element.45), channel_id=1, source_target_pairs={{0,3},{1,2},{2,1},{3,0},{4,7},{5,6},{6,5},{7,4},{8,11},{9,10},{10,... | collective-permute-start | bytes 884744 | tf_op jit(solution)/shard_map/ppermute | solution.py:245
  45.3 43.1 %collective-permute-start.3 = (bf16[8,48,384]{2,1,0:T(8,128)(2,1)}, bf16[8,48,384]{2,1,0:T(8,128)(2,1)}, u32[]{:S(2)}, u32[]{:S(2)}) collective-permute-start(bf16[8,48,384]{2,1,0:T(8,128)(2,1)} %get-tuple-element.46), channel_id=1, source_target_pairs={{0,4},{1,5},{2,6},{3,7},{4,0},{5,1},{6,2},{7,3},{8,12},{9,13},{10,... | collective-permute-start | bytes 884744 | tf_op jit(solution)/shard_map/ppermute | solution.py:245
  47.0 49.6 %collective-permute-start.4 = (bf16[8,48,384]{2,1,0:T(8,128)(2,1)}, bf16[8,48,384]{2,1,0:T(8,128)(2,1)}, u32[]{:S(2)}, u32[]{:S(2)}) collective-permute-start(bf16[8,48,384]{2,1,0:T(8,128)(2,1)} %get-tuple-element.47), channel_id=1, source_target_pairs={{0,5},{1,4},{2,7},{3,6},{4,1},{5,0},{6,3},{7,2},{8,13},{9,12},{10,... | collective-permute-start | bytes 884744 | tf_op jit(solution)/shard_map/ppermute | solution.py:245
  47.1 59.2 %collective-permute-start.5 = (bf16[8,48,384]{2,1,0:T(8,128)(2,1)}, bf16[8,48,384]{2,1,0:T(8,128)(2,1)}, u32[]{:S(2)}, u32[]{:S(2)}) collective-permute-start(bf16[8,48,384]{2,1,0:T(8,128)(2,1)} %get-tuple-element.48), channel_id=1, source_target_pairs={{0,6},{1,7},{2,4},{3,5},{4,2},{5,3},{6,0},{7,1},{8,14},{9,15},{10,... | collective-permute-start | bytes 884744 | tf_op jit(solution)/shard_map/ppermute | solution.py:245
  75.7 38.0 %collective-permute-start.6 = (bf16[8,48,384]{2,1,0:T(8,128)(2,1)}, bf16[8,48,384]{2,1,0:T(8,128)(2,1)}, u32[]{:S(2)}, u32[]{:S(2)}) collective-permute-start(bf16[8,48,384]{2,1,0:T(8,128)(2,1)} %get-tuple-element.49), channel_id=1, source_target_pairs={{0,7},{1,6},{2,5},{3,4},{4,3},{5,2},{6,1},{7,0},{8,15},{9,14},{10,... | collective-permute-start | bytes 884744 | tf_op jit(solution)/shard_map/ppermute | solution.py:245
  88.4 42.1 %collective-permute-start.7 = (bf16[8,48,384]{2,1,0:T(8,128)(2,1)}, bf16[8,48,384]{2,1,0:T(8,128)(2,1)}, u32[]{:S(2)}, u32[]{:S(2)}) collective-permute-start(bf16[8,48,384]{2,1,0:T(8,128)(2,1)} %get-tuple-element.50), channel_id=1, source_target_pairs={{0,8},{1,9},{2,10},{3,11},{4,12},{5,13},{6,14},{7,15},{8,0},{9,1},... | collective-permute-start | bytes 884744 | tf_op jit(solution)/shard_map/ppermute | solution.py:245
  88.4 48.4 %collective-permute-start.8 = (bf16[8,48,384]{2,1,0:T(8,128)(2,1)}, bf16[8,48,384]{2,1,0:T(8,128)(2,1)}, u32[]{:S(2)}, u32[]{:S(2)}) collective-permute-start(bf16[8,48,384]{2,1,0:T(8,128)(2,1)} %get-tuple-element.51), channel_id=1, source_target_pairs={{0,9},{1,8},{2,11},{3,10},{4,13},{5,12},{6,15},{7,14},{8,1},{9,0},... | collective-permute-start | bytes 884744 | tf_op jit(solution)/shard_map/ppermute | solution.py:245
  96.5 47.1 %collective-permute-start.9 = (bf16[8,48,384]{2,1,0:T(8,128)(2,1)}, bf16[8,48,384]{2,1,0:T(8,128)(2,1)}, u32[]{:S(2)}, u32[]{:S(2)}) collective-permute-start(bf16[8,48,384]{2,1,0:T(8,128)(2,1)} %get-tuple-element.52), channel_id=1, source_target_pairs={{0,10},{1,11},{2,8},{3,9},{4,14},{5,15},{6,12},{7,13},{8,2},{9,3},... | collective-permute-start | bytes 884744 | tf_op jit(solution)/shard_map/ppermute | solution.py:245
  106.2 49.1 %collective-permute-start.10 = (bf16[8,48,384]{2,1,0:T(8,128)(2,1)}, bf16[8,48,384]{2,1,0:T(8,128)(2,1)}, u32[]{:S(2)}, u32[]{:S(2)}) collective-permute-start(bf16[8,48,384]{2,1,0:T(8,128)(2,1)} %get-tuple-element.53), channel_id=1, source_target_pairs={{0,11},{1,10},{2,9},{3,8},{4,15},{5,14},{6,13},{7,12},{8,3},{9,2},... | collective-permute-start | bytes 884744 | tf_op jit(solution)/shard_map/ppermute | solution.py:245
  113.7 47.9 %collective-permute-start.11 = (bf16[8,48,384]{2,1,0:T(8,128)(2,1)}, bf16[8,48,384]{2,1,0:T(8,128)(2,1)}, u32[]{:S(2)}, u32[]{:S(2)}) collective-permute-start(bf16[8,48,384]{2,1,0:T(8,128)(2,1)} %get-tuple-element.54), channel_id=1, source_target_pairs={{0,12},{1,13},{2,14},{3,15},{4,8},{5,9},{6,10},{7,11},{8,4},{9,5},... | collective-permute-start | bytes 884744 | tf_op jit(solution)/shard_map/ppermute | solution.py:245
  130.5 37.5 %collective-permute-start.12 = (bf16[8,48,384]{2,1,0:T(8,128)(2,1)}, bf16[8,48,384]{2,1,0:T(8,128)(2,1)}, u32[]{:S(2)}, u32[]{:S(2)}) collective-permute-start(bf16[8,48,384]{2,1,0:T(8,128)(2,1)} %get-tuple-element.55), channel_id=1, source_target_pairs={{0,13},{1,12},{2,15},{3,14},{4,9},{5,8},{6,11},{7,10},{8,5},{9,4},... | collective-permute-start | bytes 884744 | tf_op jit(solution)/shard_map/ppermute | solution.py:245
  136.8 44.5 %collective-permute-start.13 = (bf16[8,48,384]{2,1,0:T(8,128)(2,1)}, bf16[8,48,384]{2,1,0:T(8,128)(2,1)}, u32[]{:S(2)}, u32[]{:S(2)}) collective-permute-start(bf16[8,48,384]{2,1,0:T(8,128)(2,1)} %get-tuple-element.56), channel_id=1, source_target_pairs={{0,14},{1,15},{2,12},{3,13},{4,10},{5,11},{6,8},{7,9},{8,6},{9,7},... | collective-permute-start | bytes 884744 | tf_op jit(solution)/shard_map/ppermute | solution.py:245
  143.7 44.0 %collective-permute-start.14 = (bf16[8,48,384]{2,1,0:T(8,128)(2,1)}, bf16[8,48,384]{2,1,0:T(8,128)(2,1)}, u32[]{:S(2)}, u32[]{:S(2)}) collective-permute-start(bf16[8,48,384]{2,1,0:T(8,128)(2,1)} %get-tuple-element.57), channel_id=1, source_target_pairs={{0,15},{1,14},{2,13},{3,12},{4,11},{5,10},{6,9},{7,8},{8,7},{9,6},... | collective-permute-start | bytes 884744 | tf_op jit(solution)/shard_map/ppermute | solution.py:245
  187.7 101.5 %all-to-all-start.1 = ((bf16[32,3,48,384]{3,2,1,0:T(8,128)(2,1)}), bf16[32,3,48,384]{3,2,1,0:T(8,128)(2,1)S(1)}, u32[]{:S(2)}, u32[]{:S(2)}) async-start(bf16[32,3,48,384]{3,2,1,0:T(8,128)(2,1)} %project.5), calls=%async_computation.1 | async-start | bytes 7077888 | tf_op jit(solution)/shard_map/all_to_all | solution.py:240
  199.5 3.7 %collective-permute-start.15 = (bf16[5,48,384]{2,1,0:T(8,128)(2,1)}, bf16[5,48,384]{2,1,0:T(8,128)(2,1)S(1)}, u32[]{:S(2)}, u32[]{:S(2)}) collective-permute-start(bf16[5,48,384]{2,1,0:T(8,128)(2,1)} %get-tuple-element.60), channel_id=1, source_target_pairs={{0,1},{1,0},{2,3},{3,2},{4,5},{5,4},{6,7},{7,6},{8,9},{9,8},{10,11... | collective-permute-start | bytes 552968 | tf_op jit(solution)/shard_map/ppermute | solution.py:245
  199.7 20.3 %collective-permute-start.16 = (bf16[5,48,384]{2,1,0:T(8,128)(2,1)}, bf16[5,48,384]{2,1,0:T(8,128)(2,1)S(1)}, u32[]{:S(2)}, u32[]{:S(2)}) collective-permute-start(bf16[5,48,384]{2,1,0:T(8,128)(2,1)} %get-tuple-element.61), channel_id=1, source_target_pairs={{0,2},{1,3},{2,0},{3,1},{4,6},{5,7},{6,4},{7,5},{8,10},{9,11},{10,... | collective-permute-start | bytes 552968 | tf_op jit(solution)/shard_map/ppermute | solution.py:245
  201.4 23.4 %collective-permute-start.17 = (bf16[5,48,384]{2,1,0:T(8,128)(2,1)}, bf16[5,48,384]{2,1,0:T(8,128)(2,1)S(1)}, u32[]{:S(2)}, u32[]{:S(2)}) collective-permute-start(bf16[5,48,384]{2,1,0:T(8,128)(2,1)} %get-tuple-element.62), channel_id=1, source_target_pairs={{0,3},{1,2},{2,1},{3,0},{4,7},{5,6},{6,5},{7,4},{8,11},{9,10},{10,... | collective-permute-start | bytes 552968 | tf_op jit(solution)/shard_map/ppermute | solution.py:245
  201.5 23.3 %collective-permute-start.18 = (bf16[5,48,384]{2,1,0:T(8,128)(2,1)}, bf16[5,48,384]{2,1,0:T(8,128)(2,1)S(1)}, u32[]{:S(2)}, u32[]{:S(2)}) collective-permute-start(bf16[5,48,384]{2,1,0:T(8,128)(2,1)} %get-tuple-element.63), channel_id=1, source_target_pairs={{0,4},{1,5},{2,6},{3,7},{4,0},{5,1},{6,2},{7,3},{8,12},{9,13},{10,... | collective-permute-start | bytes 552968 | tf_op jit(solution)/shard_map/ppermute | solution.py:245
  203.1 23.0 %collective-permute-start.19 = (bf16[5,48,384]{2,1,0:T(8,128)(2,1)}, bf16[5,48,384]{2,1,0:T(8,128)(2,1)S(1)}, u32[]{:S(2)}, u32[]{:S(2)}) collective-permute-start(bf16[5,48,384]{2,1,0:T(8,128)(2,1)} %get-tuple-element.64), channel_id=1, source_target_pairs={{0,5},{1,4},{2,7},{3,6},{4,1},{5,0},{6,3},{7,2},{8,13},{9,12},{10,... | collective-permute-start | bytes 552968 | tf_op jit(solution)/shard_map/ppermute | solution.py:245
  203.2 81.8 %copy-start.1 = (bf16[5,48,384]{2,1,0:T(8,128)(2,1)}, bf16[5,48,384]{2,1,0:T(8,128)(2,1)S(1)}, u32[]{:S(2)}) copy-start(bf16[5,48,384]{2,1,0:T(8,128)(2,1)S(1)} %collective-permute-done.15.refs_1_) | copy-start | bytes 552964
  203.2 36.2 %collective-permute-start.20 = (bf16[5,48,384]{2,1,0:T(8,128)(2,1)}, bf16[5,48,384]{2,1,0:T(8,128)(2,1)S(1)}, u32[]{:S(2)}, u32[]{:S(2)}) collective-permute-start(bf16[5,48,384]{2,1,0:T(8,128)(2,1)} %get-tuple-element.65), channel_id=1, source_target_pairs={{0,6},{1,7},{2,4},{3,5},{4,2},{5,3},{6,0},{7,1},{8,14},{9,15},{10,... | collective-permute-start | bytes 552968 | tf_op jit(solution)/shard_map/ppermute | solution.py:245
  220.0 65.0 %copy-start.2 = (bf16[5,48,384]{2,1,0:T(8,128)(2,1)}, bf16[5,48,384]{2,1,0:T(8,128)(2,1)S(1)}, u32[]{:S(2)}) copy-start(bf16[5,48,384]{2,1,0:T(8,128)(2,1)S(1)} %collective-permute-done.16.refs_2_) | copy-start | bytes 552964
  220.0 23.6 %collective-permute-start.21 = (bf16[5,48,384]{2,1,0:T(8,128)(2,1)}, bf16[5,48,384]{2,1,0:T(8,128)(2,1)S(1)}, u32[]{:S(2)}, u32[]{:S(2)}) collective-permute-start(bf16[5,48,384]{2,1,0:T(8,128)(2,1)} %get-tuple-element.66), channel_id=1, source_target_pairs={{0,7},{1,6},{2,5},{3,4},{4,3},{5,2},{6,1},{7,0},{8,15},{9,14},{10,... | collective-permute-start | bytes 552968 | tf_op jit(solution)/shard_map/ppermute | solution.py:245
  224.8 60.3 %copy-start.3 = (bf16[5,48,384]{2,1,0:T(8,128)(2,1)}, bf16[5,48,384]{2,1,0:T(8,128)(2,1)S(1)}, u32[]{:S(2)}) copy-start(bf16[5,48,384]{2,1,0:T(8,128)(2,1)S(1)} %collective-permute-done.17.refs_3_) | copy-start | bytes 552964
  224.8 28.3 %collective-permute-start.22 = (bf16[5,48,384]{2,1,0:T(8,128)(2,1)}, bf16[5,48,384]{2,1,0:T(8,128)(2,1)S(1)}, u32[]{:S(2)}, u32[]{:S(2)}) collective-permute-start(bf16[5,48,384]{2,1,0:T(8,128)(2,1)} %get-tuple-element.67), channel_id=1, source_target_pairs={{0,8},{1,9},{2,10},{3,11},{4,12},{5,13},{6,14},{7,15},{8,0},{9,1},... | collective-permute-start | bytes 552968 | tf_op jit(solution)/shard_map/ppermute | solution.py:245
  224.8 60.3 %copy-start.4 = (bf16[5,48,384]{2,1,0:T(8,128)(2,1)}, bf16[5,48,384]{2,1,0:T(8,128)(2,1)S(1)}, u32[]{:S(2)}) copy-start(bf16[5,48,384]{2,1,0:T(8,128)(2,1)S(1)} %collective-permute-done.18.refs_4_) | copy-start | bytes 552964
  224.8 32.3 %collective-permute-start.23 = (bf16[5,48,384]{2,1,0:T(8,128)(2,1)}, bf16[5,48,384]{2,1,0:T(8,128)(2,1)S(1)}, u32[]{:S(2)}, u32[]{:S(2)}) collective-permute-start(bf16[5,48,384]{2,1,0:T(8,128)(2,1)} %get-tuple-element.68), channel_id=1, source_target_pairs={{0,9},{1,8},{2,11},{3,10},{4,13},{5,12},{6,15},{7,14},{8,1},{9,0},... | collective-permute-start | bytes 552968 | tf_op jit(solution)/shard_map/ppermute | solution.py:245
  226.1 58.9 %copy-start.5 = (bf16[5,48,384]{2,1,0:T(8,128)(2,1)}, bf16[5,48,384]{2,1,0:T(8,128)(2,1)S(1)}, u32[]{:S(2)}) copy-start(bf16[5,48,384]{2,1,0:T(8,128)(2,1)S(1)} %collective-permute-done.19.refs_5_) | copy-start | bytes 552964
  226.1 34.9 %collective-permute-start.24 = (bf16[5,48,384]{2,1,0:T(8,128)(2,1)}, bf16[5,48,384]{2,1,0:T(8,128)(2,1)S(1)}, u32[]{:S(2)}, u32[]{:S(2)}) collective-permute-start(bf16[5,48,384]{2,1,0:T(8,128)(2,1)} %get-tuple-element.69), channel_id=1, source_target_pairs={{0,10},{1,11},{2,8},{3,9},{4,14},{5,15},{6,12},{7,13},{8,2},{9,3},... | collective-permute-start | bytes 552968 | tf_op jit(solution)/shard_map/ppermute | solution.py:245
  239.4 45.7 %copy-start.6 = (bf16[5,48,384]{2,1,0:T(8,128)(2,1)}, bf16[5,48,384]{2,1,0:T(8,128)(2,1)S(1)}, u32[]{:S(2)}) copy-start(bf16[5,48,384]{2,1,0:T(8,128)(2,1)S(1)} %collective-permute-done.20.refs_6_) | copy-start | bytes 552964
  239.4 28.4 %collective-permute-start.25 = (bf16[5,48,384]{2,1,0:T(8,128)(2,1)}, bf16[5,48,384]{2,1,0:T(8,128)(2,1)S(1)}, u32[]{:S(2)}, u32[]{:S(2)}) collective-permute-start(bf16[5,48,384]{2,1,0:T(8,128)(2,1)} %get-tuple-element.70), channel_id=1, source_target_pairs={{0,11},{1,10},{2,9},{3,8},{4,15},{5,14},{6,13},{7,12},{8,3},{9,2},... | collective-permute-start | bytes 552968 | tf_op jit(solution)/shard_map/ppermute | solution.py:245
  243.7 41.4 %copy-start.7 = (bf16[5,48,384]{2,1,0:T(8,128)(2,1)}, bf16[5,48,384]{2,1,0:T(8,128)(2,1)S(1)}, u32[]{:S(2)}) copy-start(bf16[5,48,384]{2,1,0:T(8,128)(2,1)S(1)} %collective-permute-done.21.refs_7_) | copy-start | bytes 552964
  243.7 28.1 %collective-permute-start.26 = (bf16[5,48,384]{2,1,0:T(8,128)(2,1)}, bf16[5,48,384]{2,1,0:T(8,128)(2,1)S(1)}, u32[]{:S(2)}, u32[]{:S(2)}) collective-permute-start(bf16[5,48,384]{2,1,0:T(8,128)(2,1)} %get-tuple-element.71), channel_id=1, source_target_pairs={{0,12},{1,13},{2,14},{3,15},{4,8},{5,9},{6,10},{7,11},{8,4},{9,5},... | collective-permute-start | bytes 552968 | tf_op jit(solution)/shard_map/ppermute | solution.py:245
  253.1 32.0 %copy-start.8 = (bf16[5,48,384]{2,1,0:T(8,128)(2,1)}, bf16[5,48,384]{2,1,0:T(8,128)(2,1)S(1)}, u32[]{:S(2)}) copy-start(bf16[5,48,384]{2,1,0:T(8,128)(2,1)S(1)} %collective-permute-done.22.refs_8_) | copy-start | bytes 552964
  253.1 22.7 %collective-permute-start.27 = (bf16[5,48,384]{2,1,0:T(8,128)(2,1)}, bf16[5,48,384]{2,1,0:T(8,128)(2,1)S(1)}, u32[]{:S(2)}, u32[]{:S(2)}) collective-permute-start(bf16[5,48,384]{2,1,0:T(8,128)(2,1)} %get-tuple-element.72), channel_id=1, source_target_pairs={{0,13},{1,12},{2,15},{3,14},{4,9},{5,8},{6,11},{7,10},{8,5},{9,4},... | collective-permute-start | bytes 552968 | tf_op jit(solution)/shard_map/ppermute | solution.py:245
  257.0 28.1 %copy-start.9 = (bf16[5,48,384]{2,1,0:T(8,128)(2,1)}, bf16[5,48,384]{2,1,0:T(8,128)(2,1)S(1)}, u32[]{:S(2)}) copy-start(bf16[5,48,384]{2,1,0:T(8,128)(2,1)S(1)} %collective-permute-done.23.refs_9_) | copy-start | bytes 552964
  257.0 28.0 %collective-permute-start.28 = (bf16[5,48,384]{2,1,0:T(8,128)(2,1)}, bf16[5,48,384]{2,1,0:T(8,128)(2,1)S(1)}, u32[]{:S(2)}, u32[]{:S(2)}) collective-permute-start(bf16[5,48,384]{2,1,0:T(8,128)(2,1)} %get-tuple-element.73), channel_id=1, source_target_pairs={{0,14},{1,15},{2,12},{3,13},{4,10},{5,11},{6,8},{7,9},{8,6},{9,7},... | collective-permute-start | bytes 552968 | tf_op jit(solution)/shard_map/ppermute | solution.py:245
  261.0 24.1 %copy-start.10 = (bf16[5,48,384]{2,1,0:T(8,128)(2,1)}, bf16[5,48,384]{2,1,0:T(8,128)(2,1)S(1)}, u32[]{:S(2)}) copy-start(bf16[5,48,384]{2,1,0:T(8,128)(2,1)S(1)} %collective-permute-done.24.refs_10_) | copy-start | bytes 552964
  261.0 28.2 %collective-permute-start.29 = (bf16[5,48,384]{2,1,0:T(8,128)(2,1)}, bf16[5,48,384]{2,1,0:T(8,128)(2,1)}, u32[]{:S(2)}, u32[]{:S(2)}) collective-permute-start(bf16[5,48,384]{2,1,0:T(8,128)(2,1)} %get-tuple-element.74), channel_id=1, source_target_pairs={{0,15},{1,14},{2,13},{3,12},{4,11},{5,10},{6,9},{7,8},{8,7},{9,6},... | collective-permute-start | bytes 552968 | tf_op jit(solution)/shard_map/ppermute | solution.py:245
  267.8 17.3 %copy-start.11 = (bf16[5,48,384]{2,1,0:T(8,128)(2,1)}, bf16[5,48,384]{2,1,0:T(8,128)(2,1)S(1)}, u32[]{:S(2)}) copy-start(bf16[5,48,384]{2,1,0:T(8,128)(2,1)S(1)} %collective-permute-done.25.refs_11_) | copy-start | bytes 552964
  271.8 13.4 %copy-start.12 = (bf16[5,48,384]{2,1,0:T(8,128)(2,1)}, bf16[5,48,384]{2,1,0:T(8,128)(2,1)S(1)}, u32[]{:S(2)}) copy-start(bf16[5,48,384]{2,1,0:T(8,128)(2,1)S(1)} %collective-permute-done.26.refs_12_) | copy-start | bytes 552964
  275.8 9.3 %copy-start.13 = (bf16[5,48,384]{2,1,0:T(8,128)(2,1)}, bf16[5,48,384]{2,1,0:T(8,128)(2,1)S(1)}, u32[]{:S(2)}) copy-start(bf16[5,48,384]{2,1,0:T(8,128)(2,1)S(1)} %collective-permute-done.27.refs_13_) | copy-start | bytes 552964
  285.2 0.7 copy-start.14
  289.2 1.8 copy-start

commit v3 on v2

--- a/solution.py
+++ b/solution.py
@@ -34,8 +34,12 @@
 SMEM = pl.BlockSpec(memory_space=pltpu.SMEM)
 
 
-def project_kernel(low, high, norm_first, write, mask_ref, col_ref, at_ref, x_ref, gate_ref, value_ref, gain_ref, *refs):
-    *outs, held, w_ref = refs
+def project_kernel(low, high, norm_first, keep, write, mask_ref, at_ref, x_ref, gate_ref, value_ref, gain_ref, *refs):
+    *outs, held, w_ref, gain_all = refs
+    col_valid = 1.0
+    if keep is not None:
+        col_ref, *outs = outs
+        col_valid = col_ref[at_ref[1]].astype(jnp.float32)
     count = high - low
     step = pl.program_id(0)
 
@@ -43,29 +47,31 @@
     def _():
         w_ref[:count] = gate_ref[...].astype(jnp.float32).T[low:high].astype(jnp.bfloat16)
         w_ref[count:] = value_ref[...].astype(jnp.float32).T[low:high].astype(jnp.bfloat16)
+        gain = jnp.broadcast_to(gain_ref[...], (gain_ref.shape[1], gain_ref.shape[1])).T
+        gain_all[...] = jnp.broadcast_to(gain[:, :1], gain_all.shape)
 
     first_row = at_ref[0] + step * ROWS
-    col_valid = col_ref[at_ref[1]].astype(jnp.float32)
-    if norm_first:
+    if keep:
         normed_ref, *outs = outs
 
     def one_row(i, _):
         if norm_first:
-            x = x_ref[i].astype(jnp.float32)
-            centred = x - jnp.mean(x, axis=-1, keepdims=True)
-            spread = jnp.mean(centred * centred, axis=-1, keepdims=True)
-            normed = (centred * lax.rsqrt(spread + norm_eps) * gain_ref[...]).astype(jnp.bfloat16)
-            normed_ref[i] = normed
+            x = x_ref[i].T.astype(jnp.float32)
+            centred = x - jnp.mean(x, axis=0, keepdims=True)
+            spread = jnp.mean(centred * centred, axis=0, keepdims=True)
+            normed = (centred * lax.rsqrt(spread + norm_eps) * gain_all[...]).astype(jnp.bfloat16)
+            if keep:
+                normed_ref[i] = normed
         else:
             normed = x_ref[i]
-        both = lax.dot_general(w_ref[...], normed, (((1,), (1,)), ((), ())), preferred_element_type=jnp.float32)
-        valid = col_valid * mask_ref[first_row + i].astype(jnp.float32)
+        both = jnp.dot(w_ref[...], normed, preferred_element_type=jnp.float32)
+        valid = mask_ref[first_row + i].astype(jnp.float32) * col_valid
         gated = sigmoid(both[:count]) * both[count:] * valid
         for j in range(held.shape[0]):
             held[j, pl.ds(pl.multiple_of(i * count, 8), count), :] = gated[:, j * LANES:(j + 1) * LANES]
         return 0
 
-    lax.fori_loop(0, ROWS, one_row, 0, unroll=2)
+    lax.fori_loop(0, ROWS, one_row, 0, unroll=ROWS)
 
     def channel(j, c):
         return held[j, pl.ds(c, ROWS, stride=count), :].astype(jnp.bfloat16)
@@ -98,32 +104,59 @@
             first += size
 
 
-def project(x, gate, value, gain, mask, col_mask, at, low, high, norm_first, write, out_blocks):
-    rows, cols, width = x.shape
+def project(x, gate, value, gain, mask, col_mask, at, low, high, norm_first, keep, write, out_blocks):
+    rows, cols, width = x.shape if norm_first else (x.shape[0], x.shape[2], x.shape[1])
     count = high - low
-    x_spec = pl.BlockSpec((ROWS, cols, width), lambda r: (r, 0, 0))
+    x_spec = pl.BlockSpec((ROWS, *x.shape[1:]), lambda r: (r, 0, 0))
     out_shape = [jax.ShapeDtypeStruct((*lead, rows, cols), jnp.bfloat16) for lead in out_blocks]
     out_specs = [pl.BlockSpec((*lead, ROWS, cols), lambda r, n=len(lead): (0,) * n + (r, 0)) for lead in out_blocks]
-    if norm_first:
-        out_shape = [jax.ShapeDtypeStruct(x.shape, jnp.bfloat16), *out_shape]
-        out_specs = [x_spec, *out_specs]
+    if keep:
+        out_shape = [jax.ShapeDtypeStruct((rows, width, cols), jnp.bfloat16), *out_shape]
+        out_specs = [pl.BlockSpec((ROWS, width, cols), lambda r: (r, 0, 0)), *out_specs]
+    extra = [] if keep is None else [col_mask]
     return pl.pallas_call(
-        functools.partial(project_kernel, low, high, norm_first, write),
+        functools.partial(project_kernel, low, high, norm_first, keep, write),
         grid=(rows // ROWS,),
-        in_specs=[SMEM, spec_whole(col_mask.shape), SMEM, x_spec]
-        + [spec_whole(gate.shape)] * 2 + [spec_whole((1, width))],
+        in_specs=[SMEM, SMEM, x_spec]
+        + [spec_whole(gate.shape)] * 2 + [spec_whole((1, width))] + [spec_whole(e.shape) for e in extra],
         out_specs=out_specs,
         out_shape=out_shape,
         scratch_shapes=[
             pltpu.VMEM((cols // LANES, ROWS * count, LANES), jnp.float32),
             pltpu.VMEM((2 * count, width), jnp.bfloat16),
+            pltpu.VMEM((width, cols), jnp.float32),
         ],
         compiler_params=params(),
         cost_estimate=pl.CostEstimate(
             flops=4 * rows * cols * width * count, bytes_accessed=8 * rows * cols * width, transcendentals=rows * cols * count
         ),
         name="project",
-    )(mask, col_mask, at, x, gate, value, gain[None])
+    )(mask, at, x, gate, value, gain[None], *extra)
+
+
+def gate_kernel(normed_ref, gate_ref, out_ref):
+    def one_row(i, _):
+        gate = lax.dot_general(normed_ref[i], gate_ref[...], (((0,), (0,)), ((), ())), preferred_element_type=jnp.float32)
+        out_ref[i] = sigmoid(gate).astype(out_ref.dtype)
+        return 0
+
+    lax.fori_loop(0, normed_ref.shape[0], one_row, 0, unroll=4)
+
+
+def output_gate(normed, out_gate):
+    rows, width, cols = normed.shape
+    return pl.pallas_call(
+        gate_kernel,
+        grid=(rows // ROWS,),
+        in_specs=[pl.BlockSpec((ROWS, width, cols), lambda r: (r, 0, 0)), spec_whole(out_gate.shape)],
+        out_specs=pl.BlockSpec((ROWS, cols, width), lambda r: (r, 0, 0)),
+        out_shape=jax.ShapeDtypeStruct((rows, cols, width), jnp.float32),
+        compiler_params=params(),
+        cost_estimate=pl.CostEstimate(
+            flops=2 * rows * cols * width * width, bytes_accessed=4 * rows * cols * width, transcendentals=rows * cols * width
+        ),
+        name="output_gate",
+    )(normed, out_gate)
 
 
 def contract_kernel(n, by_partner, rows, cols, at_ref, *refs):
@@ -183,57 +216,124 @@
     )(at, *lefts, right)
 
 
-def finish_kernel(plan, at_ref, gain_ref, normed_ref, proj_ref, gate_ref, *refs):
-    blocks, out_ref, held = refs[:len(plan)], refs[-2], refs[-1]
-    rows, cols = normed_ref.shape[:2]
-    pieces = []
-    for block, (first, size, partner) in zip(blocks, plan):
-        if partner is None:
-            pieces += [(block.at[o, e], first + o * size + e) for o in range(block.shape[0]) for e in range(size)]
-        else:
-            base = first + (at_ref[2] ^ partner) * size
-            pieces += [(block.at[e], base + e) for e in range(size)]
-    channels = len(pieces)
+def gather_kernel(size, at_ref, *refs):
+    blocks, turned_ref, stats_ref, held = refs[:-3], refs[-3], refs[-2], refs[-1]
+    rows, channels, cols = turned_ref.shape
+    pieces = [(b.at[e], (at_ref[2] ^ d) * size + e) for d, b in enumerate(blocks) for e in range(size)]
     total = jnp.zeros((rows, cols), jnp.float32)
     for piece, _ in pieces:
         total = total + piece[...].astype(jnp.float32)
     average = total * (1.0 / channels)
     spread = jnp.zeros((rows, cols), jnp.float32)
-    for piece, _ in pieces:
-        centred = piece[...].astype(jnp.float32) - average
+    for piece, c in pieces:
+        value = piece[...].astype(jnp.float32)
+        centred = value - average
         spread = spread + centred * centred
+        for j in range(held.shape[0]):
+            held[j, pl.ds(pl.multiple_of(c * rows, rows), rows), :] = value[:, j * LANES:(j + 1) * LANES]
+    stats_ref[0] = average
+    stats_ref[1] = spread
+    for i in range(rows):
+        for j in range(held.shape[0]):
+            turned_ref[i, :, j * LANES:(j + 1) * LANES] = held[j, pl.ds(i, channels, stride=rows), :].astype(jnp.bfloat16)
+
+
+def gather(blocks, at):
+    size, rows, cols = blocks[0].shape
+    channels = size * len(blocks)
+    return pl.pallas_call(
+        functools.partial(gather_kernel, size),
+        grid=(rows // ROWS,),
+        in_specs=[SMEM] + [pl.BlockSpec((size, ROWS, cols), lambda r: (0, r, 0))] * len(blocks),
+        out_specs=[
+            pl.BlockSpec((ROWS, channels, cols), lambda r: (r, 0, 0)),
+            pl.BlockSpec((2, ROWS, cols), lambda r: (0, r, 0)),
+        ],
+        out_shape=[
+            jax.ShapeDtypeStruct((rows, channels, cols), jnp.bfloat16),
+            jax.ShapeDtypeStruct((2, rows, cols), jnp.float32),
+        ],
+        scratch_shapes=[pltpu.VMEM((cols // LANES, channels * ROWS, LANES), jnp.float32)],
+        compiler_params=params(),
+        cost_estimate=pl.CostEstimate(
+            flops=4 * channels * rows * cols, bytes_accessed=4 * channels * rows * cols, transcendentals=0
+        ),
+        name="gather",
+    )(at, *blocks)
+
+
+def finish_kernel(gain_ref, column_ref, gate_ref, proj_ref, turned_ref, stats_ref, last_ref, out_ref, held, row_stats, gain_all):
+    rows, early, cols = turned_ref.shape
+    owners, size = last_ref.shape[:2]
+    late = owners * size
+    channels = early + late
+
+    @pl.when(pl.program_id(0) == 0)
+    def _():
+        gain = jnp.broadcast_to(column_ref[...], (channels, channels)).T
+        gain_all[...] = jnp.broadcast_to(gain[:, :1], gain_all.shape)
+
+    total = stats_ref[0] * float(early)
+    for o in range(owners):
+        for e in range(size):
+            total = total + last_ref[o, e].astype(jnp.float32)
+    average = total * (1.0 / channels)
+    shift = stats_ref[0] - average
+    spread = stats_ref[1] + shift * shift * float(early)
+    for o in range(owners):
+        for e in range(size):
+            centred = last_ref[o, e].astype(jnp.float32) - average
+            spread = spread + centred * centred
     scale = lax.rsqrt(spread * (1.0 / channels) + norm_eps)
-    for piece, c in pieces:
-        mixed = (piece[...].astype(jnp.float32) - average) * scale * gain_ref[c]
-        for j in range(held.shape[0]):
-            held[j, pl.ds(pl.multiple_of(c * rows, rows), rows), :] = mixed[:, j * LANES:(j + 1) * LANES]
+    row_stats[0] = average
+    row_stats[1] = scale
+    for o in range(owners):
+        for e in range(size):
+            c = o * size + e
+            mixed = (last_ref[o, e].astype(jnp.float32) - average) * scale * gain_ref[early + c]
+            for j in range(held.shape[0]):
+                held[j, c * rows:(c + 1) * rows, :] = mixed[:, j * LANES:(j + 1) * LANES]
 
     def one_row(i, _):
-        mixed = jnp.concatenate(
-            [held[j, pl.ds(i, channels, stride=rows), :] for j in range(held.shape[0])], axis=1
-        ).astype(jnp.bfloat16)
+        before = turned_ref[i].astype(jnp.float32) - row_stats[0, pl.ds(i, 1), :]
+        before = before * row_stats[1, pl.ds(i, 1), :] * gain_all[:early]
+        after_it = jnp.concatenate([held[j, pl.ds(i, late, stride=rows), :] for j in range(held.shape[0])], axis=1)
+        mixed = jnp.concatenate([before.astype(jnp.bfloat16), after_it.astype(jnp.bfloat16)], axis=0)
         linear = lax.dot_general(mixed, proj_ref[...], (((0,), (0,)), ((), ())), preferred_element_type=jnp.float32)
-        gate = jnp.dot(normed_ref[i], gate_ref[...], preferred_element_type=jnp.float32)
-        out_ref[i] = (sigmoid(gate) * linear).astype(jnp.bfloat16)
+        out_ref[i] = (gate_ref[i] * linear).astype(jnp.bfloat16)
         return 0
 
-    lax.fori_loop(0, rows, one_row, 0, unroll=2)
-
-
-def finish(blocks, plan, at, normed, gain, proj, out_gate):
-    rows, cols, width = normed.shape
+    lax.fori_loop(0, rows, one_row, 0, unroll=rows)
+
+
+def finish(turned, stats, last, gate, gain, proj):
+    rows, early, cols = turned.shape
+    owners, size = last.shape[:2]
+    channels = early + owners * size
+    width = gate.shape[2]
     pair = pl.BlockSpec((ROWS, cols, width), lambda r: (r, 0, 0))
     return pl.pallas_call(
-        functools.partial(finish_kernel, plan),
+        finish_kernel,
         grid=(rows // ROWS,),
-        in_specs=[SMEM, SMEM, pair, spec_whole(proj.shape), spec_whole(out_gate.shape)]
-        + [pl.BlockSpec((*b.shape[:-2], ROWS, cols), lambda r, n=b.ndim - 2: (0,) * n + (r, 0)) for b in blocks],
+        in_specs=[
+            SMEM,
+            spec_whole((1, channels)),
+            pair,
+            spec_whole(proj.shape),
+            pl.BlockSpec((ROWS, early, cols), lambda r: (r, 0, 0)),
+            pl.BlockSpec((2, ROWS, cols), lambda r: (0, r, 0)),
+            pl.BlockSpec((owners, size, ROWS, cols), lambda r: (0, 0, r, 0)),
+        ],
         out_specs=pair,
-        out_shape=jax.ShapeDtypeStruct(normed.shape, jnp.bfloat16),
-        scratch_shapes=[pltpu.VMEM((cols // LANES, proj.shape[0] * ROWS, LANES), jnp.float32)],
+        out_shape=jax.ShapeDtypeStruct((rows, cols, width), jnp.bfloat16),
+        scratch_shapes=[
+            pltpu.VMEM((cols // LANES, owners * size * ROWS, LANES), jnp.float32),
+            pltpu.VMEM((2, ROWS, cols), jnp.float32),
+            pltpu.VMEM((channels, cols), jnp.float32),
+        ],
         compiler_params=params(),
         name="finish",
-    )(at, gain, normed, proj, out_gate, *blocks)
+    )(gain, gain[None], gate, proj, turned, stats, last)
 
 
 def exchange(x, axes):
@@ -242,7 +342,11 @@
 
 def partners(blocks):
     n = len(blocks)
-    return [blocks[0]] + [lax.ppermute(blocks[d], HALF, [(i, i ^ d) for i in range(n)]) for d in range(1, n)]
+    moved = [blocks[0]]
+    for d in range(1, n):
+        block = blocks[d] if d <= 5 else after(blocks[d], moved[d - 5])
+        moved.append(lax.ppermute(block, HALF, [(i, i ^ d) for i in range(n)]))
+    return moved
 
 
 def after(x, *others):
@@ -265,32 +369,26 @@
 
     def right_chunk(x, q, norm_first):
         return project(
-            x, right_gate, right_value, norm_gain, token_mask, col_mask, at,
-            firsts[q] * owners, (firsts[q] + sizes[q]) * owners, norm_first,
+            x, right_gate, right_value, norm_gain, token_mask, None, at,
+            firsts[q] * owners, (firsts[q] + sizes[q]) * owners, norm_first, None,
             functools.partial(write_right, sizes[q], owners), [(2 * owners, sizes[q])],
         )
 
-    normed, right = right_chunk(pair_input, 0, True)
-    rights = [exchange(right, ALL)]
-    lefts = project(
-        normed, left_gate, left_value, norm_gain, token_mask, col_mask, at, 0, hidden, False,
+    (right,) = right_chunk(pair_input, 0, True)
+    first = exchange(right, ALL)
+    normed, *lefts = project(
+        pair_input, left_gate, left_value, norm_gain, token_mask, col_mask, at, 0, hidden, True, True,
         functools.partial(write_left, sizes, owners), [(own,)] * owners,
     )
     lefts = partners(lefts)
-    for q in range(1, len(sizes)):
-        (right,) = right_chunk(normed, q, False)
-        rights.append(exchange(after(right, rights[-1], *lefts), ALL))
-    blocks, plan = [], []
-    for q, size in enumerate(sizes):
-        last = q == len(sizes) - 1
-        outs = contract(lefts, rights[q] if q == 0 else after(rights[q], *blocks), at, firsts[q], not last)
-        if last:
-            blocks.append(exchange(outs[0], HALF))
-            plan.append((firsts[q] * owners, size, None))
-        else:
-            blocks += partners(outs)
-            plan += [(firsts[q] * owners, size, d) for d in range(owners)]
-    return finish(blocks, tuple(plan), at, normed, sum_gain, out_proj, out_gate)
+    (right,) = right_chunk(normed, 1, False)
+    second = exchange(after(right, first, *lefts), ALL)
+    blocks = partners(contract(lefts, first, at, 0, True))
+    (out,) = contract(lefts, after(second, *blocks), at, firsts[1], False)
+    last = exchange(out, HALF)
+    gate = output_gate(normed, out_gate)
+    turned, stats = gather(blocks, at)
+    return finish(turned, stats, last, gate, sum_gain, out_proj)
 
 
 def solution(mesh):

time: 343 us -> 324 us (0.945)
  blocking collectives: 28.3 us -> 0 us
  starting transfers between devices: 64 us -> 78.9 us
  waiting for transfers between devices: 170 us -> 164 us
    all_to_all x1 -> x0, blocking collectives: 28.3 us -> none  [exchange(): return lax.all_to_all(x, axes, split_axis=0, concat_axis=0, tiled=True)]
    ppermute x30, waiting for transfers between devices: 170 us -> 154 us  [partners(): moved.append(lax.ppermute(block, HALF, [(i, i ^ d) for i in range(n)]))]
    all_to_all x2 -> x3, waiting for transfers between devices: 0.01 us -> 9.69 us  [exchange(): return lax.all_to_all(x, axes, split_axis=0, concat_axis=0, tiled=True)]
    ppermute x30, starting transfers between devices: 53.8 us -> 61.5 us  [partners(): moved.append(lax.ppermute(block, HALF, [(i, i ^ d) for i in range(n)]))]
    all_to_all x2 -> x3, starting transfers between devices: 10.2 us -> 17.4 us  [exchange(): return lax.all_to_all(x, axes, split_axis=0, concat_axis=0, tiled=True)]
    pallas_call x4 -> x6, Pallas kernels: 60.6 us -> 60.4 us  [the longest x3 34.8 us: project(): pl.pallas_call(functools.partial(project_kernel, low, high, norm_first, k...]
  transfers between devices with their start and end apart: 32 -> 33, of which waited for: 24 -> 21; matrix products, arithmetic and copies ran while one was open for 0% -> 0% of each run, Pallas kernels for 10% -> 15%
where the time goes in v3:
time: 324 us
  waiting for transfers between devices  164 us (51%)
  starting transfers between devices  78.9 us (24%)
  Pallas kernels  75.7 us (23%)
  local copies, waits for them, and re-layouts  4.42 us (1%)
    ppermute x30, waiting for transfers between devices, partners(): moved.append(lax.ppermute(block, HALF, [(i, i ^ d) for i in range(n)]))  154 us
    ppermute x30, starting transfers between devices, partners(): moved.append(lax.ppermute(block, HALF, [(i, i ^ d) for i in range(n)]))  61.5 us
    pallas_call x3, Pallas kernels, project(): pl.pallas_call(functools.partial(project_kernel, low, high, norm_first, k...  34.8 us
    all_to_all x3, starting transfers between devices, exchange(): return lax.all_to_all(x, axes, split_axis=0, concat_axis=0, tiled=True)  17.4 us
    pallas_call x2, Pallas kernels, contract(): pl.pallas_call(functools.partial(contract_kernel, n, by_partner, rows, co...  15.3 us
    pallas_call x1, Pallas kernels, finish(): pl.pallas_call(finish_kernel, grid=(rows // ROWS,), in_specs=[SMEM, spec_...  10.1 us
    all_to_all x3, waiting for transfers between devices, exchange(): return lax.all_to_all(x, axes, split_axis=0, concat_axis=0, tiled=True)  9.69 us
    pallas_call x1, Pallas kernels, output_gate(): pl.pallas_call(gate_kernel, grid=(rows // ROWS,), in_specs=[pl.BlockSpec(...  9.19 us
  transfers between devices with their start and end apart: 33, of which 21 were waited for; matrix products, arithmetic and copies ran while one was open for 0% of the time, Pallas kernels for 15%

profile of v3, /device:TPU:0, one launch (start us, length us, event | category | flops | bytes accessed | tf_op | source)
XLA Modules:
  0.0 323.7 jit_solution(5236708250620923339)
XLA Ops:
  0.6 11.2 %project.4 = bf16[32,5,48,384]{3,2,1,0:T(8,128)(2,1)} custom-call(s32[768]{0:T(1024)} %mask_ref.5, s32[3]{0:T(128)} %pad_add_fusion.at_ref, bf16[48,384,128]{2,1,0:T(8,128)(2,1)} %x_ref.3, bf16[128,128]{1,0:T(8,128)(2,1)} %gate_ref.7, bf16[128,128]{1,0:T(8,128)(2,1)} %value_ref.5, f32[1,128]{1,0:T(1,128)} %bitcast.5), custom_call_target="tpu_custom_call" | custom-call | flops 754974720 | bytes 18874368 | tf_op jit(solution)/shard_map/project/pallas_call | solution.py:117
  11.8 7.4 %all-to-all-start = ((bf16[32,5,48,384]{3,2,1,0:T(8,128)(2,1)}), bf16[32,5,48,384]{3,2,1,0:T(8,128)(2,1)}, u32[]{:S(2)}, u32[]{:S(2)}) async-start(bf16[32,5,48,384]{3,2,1,0:T(8,128)(2,1)} %project.4), calls=%async_computation | async-start | bytes 11796480 | tf_op jit(solution)/shard_map/all_to_all | solution.py:340
  19.9 16.8 %project.3 = (bf16[48,128,384]{2,1,0:T(8,128)(2,1)}, bf16[8,48,384]{2,1,0:T(8,128)(2,1)}, bf16[8,48,384]{2,1,0:T(8,128)(2,1)}, bf16[8,48,384]{2,1,0:T(8,128)(2,1...) custom-call(s32[768]{0:T(1024)} %mask_ref.5, ...), custom_call_target="tpu_custom_call" | custom-call | flops 1207959552 | bytes 18874368 | tf_op jit(solution)/shard_map/project/pallas_call | solution.py:117
  36.7 1.5 collective-permute-start.4
  38.6 1.4 collective-permute-start.2
  40.4 27.5 %collective-permute-done.4.refs_5_ = bf16[8,48,384]{2,1,0:T(8,128)(2,1)} collective-permute-done((bf16[8,48,384]{2,1,0:T(8,128)(2,1)}, bf16[8,48,384]{2,1,0:T(8,128)(2,1)}, u32[]{:S(2)}, u32[]{:S(2)}) %collective-permute-start.4) | collective-permute-done | bytes 294944 | tf_op jit(solution)/shard_map/ppermute | solution.py:348
  68.0 6.5 %collective-permute-done.3.refs_4_ = bf16[8,48,384]{2,1,0:T(8,128)(2,1)} collective-permute-done((bf16[8,48,384]{2,1,0:T(8,128)(2,1)}, bf16[8,48,384]{2,1,0:T(8,128)(2,1)}, u32[]{:S(2)}, u32[]{:S(2)}) %collective-permute-start.3) | collective-permute-done | bytes 294944 | tf_op jit(solution)/shard_map/ppermute | solution.py:348
  75.5 4.9 %collective-permute-done.1.refs_2_ = bf16[8,48,384]{2,1,0:T(8,128)(2,1)} collective-permute-done((bf16[8,48,384]{2,1,0:T(8,128)(2,1)}, bf16[8,48,384]{2,1,0:T(8,128)(2,1)}, u32[]{:S(2)}, u32[]{:S(2)}) %collective-permute-start.1) | collective-permute-done | bytes 294944 | tf_op jit(solution)/shard_map/ppermute | solution.py:348
  80.4 14.3 %collective-permute-start.6 = (bf16[8,48,384]{2,1,0:T(8,128)(2,1)}, bf16[8,48,384]{2,1,0:T(8,128)(2,1)}, u32[]{:S(2)}, u32[]{:S(2)}) collective-permute-start(bf16[8,48,384]{2,1,0:T(8,128)(2,1)} %get-tuple-element.72), channel_id=1, source_target_pairs={{0,7},{1,6},{2,5},{3,4},{4,3},{5,2},{6,1},{7,0},{8,15},{9,14},{10,... | collective-permute-start | bytes 884744 | tf_op jit(solution)/shard_map/ppermute | solution.py:348
  94.7 1.8 collective-permute-start.5
  96.5 26.5 %collective-permute-done.9.refs_10_ = bf16[8,48,384]{2,1,0:T(8,128)(2,1)} collective-permute-done((bf16[8,48,384]{2,1,0:T(8,128)(2,1)}, bf16[8,48,384]{2,1,0:T(8,128)(2,1)}, u32[]{:S(2)}, u32[]{:S(2)}) %collective-permute-start.9) | collective-permute-done | bytes 294944 | tf_op jit(solution)/shard_map/ppermute | solution.py:348
  123.0 2.3 collective-permute-start.14
  125.3 4.0 %collective-permute-done.8.refs_9_ = bf16[8,48,384]{2,1,0:T(8,128)(2,1)} collective-permute-done((bf16[8,48,384]{2,1,0:T(8,128)(2,1)}, bf16[8,48,384]{2,1,0:T(8,128)(2,1)}, u32[]{:S(2)}, u32[]{:S(2)}) %collective-permute-start.8) | collective-permute-done | bytes 294944 | tf_op jit(solution)/shard_map/ppermute | solution.py:348
  129.3 4.1 %collective-permute-start.13 = (bf16[8,48,384]{2,1,0:T(8,128)(2,1)}, bf16[8,48,384]{2,1,0:T(8,128)(2,1)}, u32[]{:S(2)}, u32[]{:S(2)}) collective-permute-start(bf16[8,48,384]{2,1,0:T(8,128)(2,1)} %get-tuple-element.86), channel_id=1, source_target_pairs={{0,14},{1,15},{2,12},{3,13},{4,10},{5,11},{6,8},{7,9},{8,6},{9,7},... | collective-permute-start | bytes 884744 | tf_op jit(solution)/shard_map/ppermute | solution.py:348
  133.4 2.2 collective-permute-done.7.refs_8_
  135.6 1.4 collective-permute-start.12
  138.3 2.7 collective-permute-start.10
  141.0 6.7 %project.5 = bf16[32,3,48,384]{3,2,1,0:T(8,128)(2,1)} custom-call(s32[768]{0:T(1024)} %mask_ref.5, s32[3]{0:T(128)} %pad_add_fusion.at_ref, bf16[48,128,384]{2,1,0:T(8,128)(2,1)} %get-tuple-element.62.normed_ref.x_ref, bf16[128,128]{1,0:T(8,128)(2,1)} %gate_ref.7, bf16[128,128]{1,0:T(8,128)(2,1)} %value_ref.5, f32[1,128]{1,0:T(1,128)} %bitcast.7), custom_call_target="tpu_custom_call" | custom-call | flops 452984832 | bytes 18874368 | tf_op jit(solution)/shard_map/project/pallas_call | solution.py:117
  147.8 9.2 %collective-permute-done.13.refs_14_ = bf16[8,48,384]{2,1,0:T(8,128)(2,1)} collective-permute-done((bf16[8,48,384]{2,1,0:T(8,128)(2,1)}, bf16[8,48,384]{2,1,0:T(8,128)(2,1)}, u32[]{:S(2)}, u32[]{:S(2)}) %collective-permute-start.13) | collective-permute-done | bytes 294944 | tf_op jit(solution)/shard_map/ppermute | solution.py:348
  156.9 3.9 %collective-permute-done.12.refs_13_ = bf16[8,48,384]{2,1,0:T(8,128)(2,1)} collective-permute-done((bf16[8,48,384]{2,1,0:T(8,128)(2,1)}, bf16[8,48,384]{2,1,0:T(8,128)(2,1)}, u32[]{:S(2)}, u32[]{:S(2)}) %collective-permute-start.12) | collective-permute-done | bytes 294944 | tf_op jit(solution)/shard_map/ppermute | solution.py:348
  160.8 8.7 %collective-permute-done.11.refs_12_ = bf16[8,48,384]{2,1,0:T(8,128)(2,1)} collective-permute-done((bf16[8,48,384]{2,1,0:T(8,128)(2,1)}, bf16[8,48,384]{2,1,0:T(8,128)(2,1)}, u32[]{:S(2)}, u32[]{:S(2)}) %collective-permute-start.11) | collective-permute-done | bytes 294944 | tf_op jit(solution)/shard_map/ppermute | solution.py:348
  169.5 3.7 %collective-permute-done.10.refs_11_ = bf16[8,48,384]{2,1,0:T(8,128)(2,1)} collective-permute-done((bf16[8,48,384]{2,1,0:T(8,128)(2,1)}, bf16[8,48,384]{2,1,0:T(8,128)(2,1)}, u32[]{:S(2)}, u32[]{:S(2)}) %collective-permute-start.10) | collective-permute-done | bytes 294944 | tf_op jit(solution)/shard_map/ppermute | solution.py:348
  173.2 6.3 %all-to-all-start.1 = ((bf16[32,3,48,384]{3,2,1,0:T(8,128)(2,1)}), bf16[32,3,48,384]{3,2,1,0:T(8,128)(2,1)S(1)}, u32[]{:S(2)}, u32[]{:S(2)}) async-start(bf16[32,3,48,384]{3,2,1,0:T(8,128)(2,1)} %project.5), calls=%async_computation.1 | async-start | bytes 7077888 | tf_op jit(solution)/shard_map/all_to_all | solution.py:340
  179.5 9.0 %contract.2 = (bf16[5,48,384]{2,1,0:T(8,128)(2,1)}, bf16[5,48,384]{2,1,0:T(8,128)(2,1)}, bf16[5,48,384]{2,1,0:T(8,128)(2,1)}, bf16[5,48,384]{2,1,0:T(8,128)(2,1)...) custom-call(s32[3]{0:T(128)} %pad_add_fusion.at_ref, ...), custom_call_target="tpu_custom_call" | custom-call | flops 18119393280 | bytes 11796480 | tf_op jit(solution)/shard_map/contract/pallas_call | solution.py:196
  188.5 1.4 collective-permute-start.19
  190.3 1.4 collective-permute-start.17
  192.1 14.8 %collective-permute-done.19.refs_5_ = bf16[5,48,384]{2,1,0:T(8,128)(2,1)S(1)} collective-permute-done((bf16[5,48,384]{2,1,0:T(8,128)(2,1)}, bf16[5,48,384]{2,1,0:T(8,128)(2,1)S(1)}, u32[]{:S(2)}, u32[]{:S(2)}) %collective-permute-start.19) | collective-permute-done | bytes 184352 | tf_op jit(solution)/shard_map/ppermute | solution.py:348
  207.0 1.7 collective-permute-start.24
  208.6 4.7 %collective-permute-done.18.refs_4_ = bf16[5,48,384]{2,1,0:T(8,128)(2,1)S(1)} collective-permute-done((bf16[5,48,384]{2,1,0:T(8,128)(2,1)}, bf16[5,48,384]{2,1,0:T(8,128)(2,1)S(1)}, u32[]{:S(2)}, u32[]{:S(2)}) %collective-permute-start.18) | collective-permute-done | bytes 184352 | tf_op jit(solution)/shard_map/ppermute | solution.py:348
  214.2 8.7 %collective-permute-start.21 = (bf16[5,48,384]{2,1,0:T(8,128)(2,1)}, bf16[5,48,384]{2,1,0:T(8,128)(2,1)S(1)}, u32[]{:S(2)}, u32[]{:S(2)}) collective-permute-start(bf16[5,48,384]{2,1,0:T(8,128)(2,1)} %get-tuple-element.98), channel_id=1, source_target_pairs={{0,7},{1,6},{2,5},{3,4},{4,3},{5,2},{6,1},{7,0},{8,15},{9,14},{10,... | collective-permute-start | bytes 552968 | tf_op jit(solution)/shard_map/ppermute | solution.py:348
  222.8 1.3 collective-permute-start.20
  224.2 17.8 %collective-permute-done.24.refs_10_ = bf16[5,48,384]{2,1,0:T(8,128)(2,1)S(1)} collective-permute-done((bf16[5,48,384]{2,1,0:T(8,128)(2,1)}, bf16[5,48,384]{2,1,0:T(8,128)(2,1)S(1)}, u32[]{:S(2)}, u32[]{:S(2)}) %collective-permute-start.24) | collective-permute-done | bytes 184352 | tf_op jit(solution)/shard_map/ppermute | solution.py:348
  242.0 2.8 collective-permute-start.29
  245.9 3.8 %collective-permute-start.28 = (bf16[5,48,384]{2,1,0:T(8,128)(2,1)}, bf16[5,48,384]{2,1,0:T(8,128)(2,1)S(1)}, u32[]{:S(2)}, u32[]{:S(2)}) collective-permute-start(bf16[5,48,384]{2,1,0:T(8,128)(2,1)} %get-tuple-element.112), channel_id=1, source_target_pairs={{0,14},{1,15},{2,12},{3,13},{4,10},{5,11},{6,8},{7,9},{8,6},{9,7},... | collective-permute-start | bytes 552968 | tf_op jit(solution)/shard_map/ppermute | solution.py:348
  249.9 1.9 collective-permute-start.27
  251.8 1.3 collective-permute-start.26
  253.1 3.0 collective-permute-start.25
  256.6 5.5 %collective-permute-done.28.refs_14_ = bf16[5,48,384]{2,1,0:T(8,128)(2,1)S(1)} collective-permute-done((bf16[5,48,384]{2,1,0:T(8,128)(2,1)}, bf16[5,48,384]{2,1,0:T(8,128)(2,1)S(1)}, u32[]{:S(2)}, u32[]{:S(2)}) %collective-permute-start.28) | collective-permute-done | bytes 184352 | tf_op jit(solution)/shard_map/ppermute | solution.py:348
  262.1 4.9 %collective-permute-done.27.refs_13_ = bf16[5,48,384]{2,1,0:T(8,128)(2,1)S(1)} collective-permute-done((bf16[5,48,384]{2,1,0:T(8,128)(2,1)}, bf16[5,48,384]{2,1,0:T(8,128)(2,1)S(1)}, u32[]{:S(2)}, u32[]{:S(2)}) %collective-permute-start.27) | collective-permute-done | bytes 184352 | tf_op jit(solution)/shard_map/ppermute | solution.py:348
  267.0 4.9 %collective-permute-done.26.refs_12_ = bf16[5,48,384]{2,1,0:T(8,128)(2,1)S(1)} collective-permute-done((bf16[5,48,384]{2,1,0:T(8,128)(2,1)}, bf16[5,48,384]{2,1,0:T(8,128)(2,1)S(1)}, u32[]{:S(2)}, u32[]{:S(2)}) %collective-permute-start.26) | collective-permute-done | bytes 184352 | tf_op jit(solution)/shard_map/ppermute | solution.py:348
  272.8 2.5 collective-permute-done.25.refs_11_
  275.2 1.8 copy-done.1
  277.1 6.2 %contract.3 = bf16[16,3,48,384]{3,2,1,0:T(8,128)(2,1)} custom-call(s32[3]{0:T(128)} %pad_add_fusion.at_ref, bf16[8,48,384]{2,1,0:T(8,128)(2,1)} %get-tuple-element.63.refs_0_, bf16[8,48,384]{2,1,0:T(8,128)(2,1)} %collective-permute-done.refs_1_, bf16[8,48,384]{2,1,0:T(8,128)(2,1)} %collective-permute-done.1.refs_2_, ...), custom_call_target="tpu_custom_call" | custom-call | flops 10871635968 | bytes 7077888 | tf_op jit(solution)/shard_map/contract/pallas_call | solution.py:196
  283.3 3.7 %all-to-all-start.2 = ((bf16[16,3,48,384]{3,2,1,0:T(8,128)(2,1)}), bf16[16,3,48,384]{3,2,1,0:T(8,128)(2,1)S(1)}, u32[]{:S(2)}, u32[]{:S(2)}) async-start(bf16[16,3,48,384]{3,2,1,0:T(8,128)(2,1)} %contract.3), calls=%async_computation.2 | async-start | bytes 3538944 | tf_op jit(solution)/shard_map/all_to_all | solution.py:340
  287.0 9.2 %output_gate.1.gate_ref = f32[48,384,128]{2,1,0:T(8,128)} custom-call(bf16[48,128,384]{2,1,0:T(8,128)(2,1)} %get-tuple-element.62.normed_ref.x_ref, bf16[128,128]{1,0:T(8,128)(2,1)} %gate_ref.5), custom_call_target="tpu_custom_call" | custom-call | flops 603979776 | bytes 9437184 | tf_op jit(solution)/shard_map/output_gate/pallas_call | solution.py:148
  296.2 6.3 %gather.1 = (bf16[48,80,384]{2,1,0:T(8,128)(2,1)}, f32[2,48,384]{2,1,0:T(8,128)}) custom-call(s32[3]{0:T(128)} %pad_add_fusion.at_ref, bf16[5,48,384]{2,1,0:T(8,128)(2,1)} %get-tuple-element.89.refs_0_, bf16[5,48,384]{2,1,0:T(8,128)(2,1)} %copy-done.6, bf16[5,48,384]{2,1,0:T(8,128)(2,1)} %copy-done.5, bf16[5,48,384]{2,1,0:T(8,128)(2,1)} %copy-done.4, ...), custom_call_target="tpu_custom_call" | custom-call | flops 5898240 | bytes 5898240 | tf_op jit(solution)/shard_map/gather/pallas_call | solution.py:244
  302.6 9.7 %all-to-all-done.2.last_ref = bf16[16,3,48,384]{3,2,1,0:T(8,128)(2,1)S(1)} async-done(((bf16[16,3,48,384]{3,2,1,0:T(8,128)(2,1)}), bf16[16,3,48,384]{3,2,1,0:T(8,128)(2,1)S(1)}, u32[]{:S(2)}, u32[]{:S(2)}) %all-to-all-start.2) | async-done | bytes 1769504 | tf_op jit(solution)/shard_map/all_to_all | solution.py:340
  313.5 10.1 %finish.1 = bf16[48,384,128]{2,1,0:T(8,128)(2,1)} custom-call(f32[128]{0:T(128)} %gain_ref.1, f32[1,128]{1,0:T(1,128)} %bitcast.8, f32[48,384,128]{2,1,0:T(8,128)} %output_gate.1.gate_ref, bf16[128,128]{1,0:T(8,128)(2,1)} %proj_ref.1, bf16[48,80,384]{2,1,0:T(8,128)(2,1)} %get-tuple-element.115.turned_ref, f32[2,48,384]{2,1,0:T(8,128)} %get-tuple-element.116.stats_ref, ...), custom_call_target="tpu_custom_call" | custom-call | tf_op jit(solution)/shard_map/finish/pallas_call | solution.py:315
  (62 shorter events, 10.0 us)
Async XLA Ops:
  11.8 7.4 %copy-start.16 = (s32[768]{0:T(1024)S(1)}, s32[768]{0:T(1024)}, u32[]{:S(2)}) copy-start(s32[768]{0:T(1024)} %mask_ref.5) | copy-start | bytes 9220
  11.8 161.3 %all-to-all-start = ((bf16[32,5,48,384]{3,2,1,0:T(8,128)(2,1)}), bf16[32,5,48,384]{3,2,1,0:T(8,128)(2,1)}, u32[]{:S(2)}, u32[]{:S(2)}) async-start(bf16[32,5,48,384]{3,2,1,0:T(8,128)(2,1)} %project.4), calls=%async_computation | async-start | bytes 11796480 | tf_op jit(solution)/shard_map/all_to_all | solution.py:340
  36.7 31.3 %collective-permute-start.4 = (bf16[8,48,384]{2,1,0:T(8,128)(2,1)}, bf16[8,48,384]{2,1,0:T(8,128)(2,1)}, u32[]{:S(2)}, u32[]{:S(2)}) collective-permute-start(bf16[8,48,384]{2,1,0:T(8,128)(2,1)} %get-tuple-element.68), channel_id=1, source_target_pairs={{0,5},{1,4},{2,7},{3,6},{4,1},{5,0},{6,3},{7,2},{8,13},{9,12},{10,... | collective-permute-start | bytes 884744 | tf_op jit(solution)/shard_map/ppermute | solution.py:348
  38.2 36.2 %collective-permute-start.3 = (bf16[8,48,384]{2,1,0:T(8,128)(2,1)}, bf16[8,48,384]{2,1,0:T(8,128)(2,1)}, u32[]{:S(2)}, u32[]{:S(2)}) collective-permute-start(bf16[8,48,384]{2,1,0:T(8,128)(2,1)} %get-tuple-element.67), channel_id=1, source_target_pairs={{0,4},{1,5},{2,6},{3,7},{4,0},{5,1},{6,2},{7,3},{8,12},{9,13},{10,... | collective-permute-start | bytes 884744 | tf_op jit(solution)/shard_map/ppermute | solution.py:348
  38.6 35.9 %collective-permute-start.2 = (bf16[8,48,384]{2,1,0:T(8,128)(2,1)}, bf16[8,48,384]{2,1,0:T(8,128)(2,1)}, u32[]{:S(2)}, u32[]{:S(2)}) collective-permute-start(bf16[8,48,384]{2,1,0:T(8,128)(2,1)} %get-tuple-element.66), channel_id=1, source_target_pairs={{0,3},{1,2},{2,1},{3,0},{4,7},{5,6},{6,5},{7,4},{8,11},{9,10},{10,... | collective-permute-start | bytes 884744 | tf_op jit(solution)/shard_map/ppermute | solution.py:348
  39.9 40.4 %collective-permute-start.1 = (bf16[8,48,384]{2,1,0:T(8,128)(2,1)}, bf16[8,48,384]{2,1,0:T(8,128)(2,1)}, u32[]{:S(2)}, u32[]{:S(2)}) collective-permute-start(bf16[8,48,384]{2,1,0:T(8,128)(2,1)} %get-tuple-element.65), channel_id=1, source_target_pairs={{0,2},{1,3},{2,0},{3,1},{4,6},{5,7},{6,4},{7,5},{8,10},{9,11},{10,... | collective-permute-start | bytes 884744 | tf_op jit(solution)/shard_map/ppermute | solution.py:348
  40.3 54.4 %collective-permute-start = (bf16[8,48,384]{2,1,0:T(8,128)(2,1)}, bf16[8,48,384]{2,1,0:T(8,128)(2,1)}, u32[]{:S(2)}, u32[]{:S(2)}) collective-permute-start(bf16[8,48,384]{2,1,0:T(8,128)(2,1)} %get-tuple-element.64), channel_id=1, source_target_pairs={{0,1},{1,0},{2,3},{3,2},{4,5},{5,4},{6,7},{7,6},{8,9},{9,8},{10,11... | collective-permute-start | bytes 884744 | tf_op jit(solution)/shard_map/ppermute | solution.py:348
  68.0 55.0 %collective-permute-start.9 = (bf16[8,48,384]{2,1,0:T(8,128)(2,1)}, bf16[8,48,384]{2,1,0:T(8,128)(2,1)}, u32[]{:S(2)}, u32[]{:S(2)}) collective-permute-start(bf16[8,48,384]{2,1,0:T(8,128)(2,1)} %get-tuple-element.78), channel_id=1, source_target_pairs={{0,10},{1,11},{2,8},{3,9},{4,14},{5,15},{6,12},{7,13},{8,2},{9,3},... | collective-permute-start | bytes 884744 | tf_op jit(solution)/shard_map/ppermute | solution.py:348
  74.5 54.8 %collective-permute-start.8 = (bf16[8,48,384]{2,1,0:T(8,128)(2,1)}, bf16[8,48,384]{2,1,0:T(8,128)(2,1)}, u32[]{:S(2)}, u32[]{:S(2)}) collective-permute-start(bf16[8,48,384]{2,1,0:T(8,128)(2,1)} %get-tuple-element.76), channel_id=1, source_target_pairs={{0,9},{1,8},{2,11},{3,10},{4,13},{5,12},{6,15},{7,14},{8,1},{9,0},... | collective-permute-start | bytes 884744 | tf_op jit(solution)/shard_map/ppermute | solution.py:348
  74.5 61.2 %collective-permute-start.7 = (bf16[8,48,384]{2,1,0:T(8,128)(2,1)}, bf16[8,48,384]{2,1,0:T(8,128)(2,1)}, u32[]{:S(2)}, u32[]{:S(2)}) collective-permute-start(bf16[8,48,384]{2,1,0:T(8,128)(2,1)} %get-tuple-element.74), channel_id=1, source_target_pairs={{0,8},{1,9},{2,10},{3,11},{4,12},{5,13},{6,14},{7,15},{8,0},{9,1},... | collective-permute-start | bytes 884744 | tf_op jit(solution)/shard_map/ppermute | solution.py:348
  80.4 56.7 %collective-permute-start.6 = (bf16[8,48,384]{2,1,0:T(8,128)(2,1)}, bf16[8,48,384]{2,1,0:T(8,128)(2,1)}, u32[]{:S(2)}, u32[]{:S(2)}) collective-permute-start(bf16[8,48,384]{2,1,0:T(8,128)(2,1)} %get-tuple-element.72), channel_id=1, source_target_pairs={{0,7},{1,6},{2,5},{3,4},{4,3},{5,2},{6,1},{7,0},{8,15},{9,14},{10,... | collective-permute-start | bytes 884744 | tf_op jit(solution)/shard_map/ppermute | solution.py:348
  94.7 43.6 %collective-permute-start.5 = (bf16[8,48,384]{2,1,0:T(8,128)(2,1)}, bf16[8,48,384]{2,1,0:T(8,128)(2,1)}, u32[]{:S(2)}, u32[]{:S(2)}) collective-permute-start(bf16[8,48,384]{2,1,0:T(8,128)(2,1)} %get-tuple-element.70), channel_id=1, source_target_pairs={{0,6},{1,7},{2,4},{3,5},{4,2},{5,3},{6,0},{7,1},{8,14},{9,15},{10,... | collective-permute-start | bytes 884744 | tf_op jit(solution)/shard_map/ppermute | solution.py:348
  123.0 24.8 %collective-permute-start.14 = (bf16[8,48,384]{2,1,0:T(8,128)(2,1)}, bf16[8,48,384]{2,1,0:T(8,128)(2,1)}, u32[]{:S(2)}, u32[]{:S(2)}) collective-permute-start(bf16[8,48,384]{2,1,0:T(8,128)(2,1)} %get-tuple-element.88), channel_id=1, source_target_pairs={{0,15},{1,14},{2,13},{3,12},{4,11},{5,10},{6,9},{7,8},{8,7},{9,6},... | collective-permute-start | bytes 884744 | tf_op jit(solution)/shard_map/ppermute | solution.py:348
  129.3 27.6 %collective-permute-start.13 = (bf16[8,48,384]{2,1,0:T(8,128)(2,1)}, bf16[8,48,384]{2,1,0:T(8,128)(2,1)}, u32[]{:S(2)}, u32[]{:S(2)}) collective-permute-start(bf16[8,48,384]{2,1,0:T(8,128)(2,1)} %get-tuple-element.86), channel_id=1, source_target_pairs={{0,14},{1,15},{2,12},{3,13},{4,10},{5,11},{6,8},{7,9},{8,6},{9,7},... | collective-permute-start | bytes 884744 | tf_op jit(solution)/shard_map/ppermute | solution.py:348
  135.6 25.2 %collective-permute-start.12 = (bf16[8,48,384]{2,1,0:T(8,128)(2,1)}, bf16[8,48,384]{2,1,0:T(8,128)(2,1)}, u32[]{:S(2)}, u32[]{:S(2)}) collective-permute-start(bf16[8,48,384]{2,1,0:T(8,128)(2,1)} %get-tuple-element.84), channel_id=1, source_target_pairs={{0,13},{1,12},{2,15},{3,14},{4,9},{5,8},{6,11},{7,10},{8,5},{9,4},... | collective-permute-start | bytes 884744 | tf_op jit(solution)/shard_map/ppermute | solution.py:348
  137.0 32.5 %collective-permute-start.11 = (bf16[8,48,384]{2,1,0:T(8,128)(2,1)}, bf16[8,48,384]{2,1,0:T(8,128)(2,1)}, u32[]{:S(2)}, u32[]{:S(2)}) collective-permute-start(bf16[8,48,384]{2,1,0:T(8,128)(2,1)} %get-tuple-element.82), channel_id=1, source_target_pairs={{0,12},{1,13},{2,14},{3,15},{4,8},{5,9},{6,10},{7,11},{8,4},{9,5},... | collective-permute-start | bytes 884744 | tf_op jit(solution)/shard_map/ppermute | solution.py:348
  138.3 34.9 %collective-permute-start.10 = (bf16[8,48,384]{2,1,0:T(8,128)(2,1)}, bf16[8,48,384]{2,1,0:T(8,128)(2,1)}, u32[]{:S(2)}, u32[]{:S(2)}) collective-permute-start(bf16[8,48,384]{2,1,0:T(8,128)(2,1)} %get-tuple-element.80), channel_id=1, source_target_pairs={{0,11},{1,10},{2,9},{3,8},{4,15},{5,14},{6,13},{7,12},{8,3},{9,2},... | collective-permute-start | bytes 884744 | tf_op jit(solution)/shard_map/ppermute | solution.py:348
  173.2 102.1 %all-to-all-start.1 = ((bf16[32,3,48,384]{3,2,1,0:T(8,128)(2,1)}), bf16[32,3,48,384]{3,2,1,0:T(8,128)(2,1)S(1)}, u32[]{:S(2)}, u32[]{:S(2)}) async-start(bf16[32,3,48,384]{3,2,1,0:T(8,128)(2,1)} %project.5), calls=%async_computation.1 | async-start | bytes 7077888 | tf_op jit(solution)/shard_map/all_to_all | solution.py:340
  188.5 18.5 %collective-permute-start.19 = (bf16[5,48,384]{2,1,0:T(8,128)(2,1)}, bf16[5,48,384]{2,1,0:T(8,128)(2,1)S(1)}, u32[]{:S(2)}, u32[]{:S(2)}) collective-permute-start(bf16[5,48,384]{2,1,0:T(8,128)(2,1)} %get-tuple-element.94), channel_id=1, source_target_pairs={{0,5},{1,4},{2,7},{3,6},{4,1},{5,0},{6,3},{7,2},{8,13},{9,12},{10,... | collective-permute-start | bytes 552968 | tf_op jit(solution)/shard_map/ppermute | solution.py:348
  189.9 23.4 %collective-permute-start.18 = (bf16[5,48,384]{2,1,0:T(8,128)(2,1)}, bf16[5,48,384]{2,1,0:T(8,128)(2,1)S(1)}, u32[]{:S(2)}, u32[]{:S(2)}) collective-permute-start(bf16[5,48,384]{2,1,0:T(8,128)(2,1)} %get-tuple-element.93), channel_id=1, source_target_pairs={{0,4},{1,5},{2,6},{3,7},{4,0},{5,1},{6,2},{7,3},{8,12},{9,13},{10,... | collective-permute-start | bytes 552968 | tf_op jit(solution)/shard_map/ppermute | solution.py:348
  190.3 23.1 %collective-permute-start.17 = (bf16[5,48,384]{2,1,0:T(8,128)(2,1)}, bf16[5,48,384]{2,1,0:T(8,128)(2,1)S(1)}, u32[]{:S(2)}, u32[]{:S(2)}) collective-permute-start(bf16[5,48,384]{2,1,0:T(8,128)(2,1)} %get-tuple-element.92), channel_id=1, source_target_pairs={{0,3},{1,2},{2,1},{3,0},{4,7},{5,6},{6,5},{7,4},{8,11},{9,10},{10,... | collective-permute-start | bytes 552968 | tf_op jit(solution)/shard_map/ppermute | solution.py:348
  191.6 22.6 %collective-permute-start.16 = (bf16[5,48,384]{2,1,0:T(8,128)(2,1)}, bf16[5,48,384]{2,1,0:T(8,128)(2,1)S(1)}, u32[]{:S(2)}, u32[]{:S(2)}) collective-permute-start(bf16[5,48,384]{2,1,0:T(8,128)(2,1)} %get-tuple-element.91), channel_id=1, source_target_pairs={{0,2},{1,3},{2,0},{3,1},{4,6},{5,7},{6,4},{7,5},{8,10},{9,11},{10,... | collective-permute-start | bytes 552968 | tf_op jit(solution)/shard_map/ppermute | solution.py:348
  192.1 30.8 %collective-permute-start.15 = (bf16[5,48,384]{2,1,0:T(8,128)(2,1)}, bf16[5,48,384]{2,1,0:T(8,128)(2,1)S(1)}, u32[]{:S(2)}, u32[]{:S(2)}) collective-permute-start(bf16[5,48,384]{2,1,0:T(8,128)(2,1)} %get-tuple-element.90), channel_id=1, source_target_pairs={{0,1},{1,0},{2,3},{3,2},{4,5},{5,4},{6,7},{7,6},{8,9},{9,8},{10,11... | collective-permute-start | bytes 552968 | tf_op jit(solution)/shard_map/ppermute | solution.py:348
  207.0 65.0 %copy-start.2 = (bf16[5,48,384]{2,1,0:T(8,128)(2,1)}, bf16[5,48,384]{2,1,0:T(8,128)(2,1)S(1)}, u32[]{:S(2)}) copy-start(bf16[5,48,384]{2,1,0:T(8,128)(2,1)S(1)} %collective-permute-done.19.refs_5_) | copy-start | bytes 552964
  207.0 35.0 %collective-permute-start.24 = (bf16[5,48,384]{2,1,0:T(8,128)(2,1)}, bf16[5,48,384]{2,1,0:T(8,128)(2,1)S(1)}, u32[]{:S(2)}, u32[]{:S(2)}) collective-permute-start(bf16[5,48,384]{2,1,0:T(8,128)(2,1)} %get-tuple-element.104), channel_id=1, source_target_pairs={{0,10},{1,11},{2,8},{3,9},{4,14},{5,15},{6,12},{7,13},{8,2},{9,3},... | collective-permute-start | bytes 552968 | tf_op jit(solution)/shard_map/ppermute | solution.py:348
  213.3 58.6 %copy-start.3 = (bf16[5,48,384]{2,1,0:T(8,128)(2,1)}, bf16[5,48,384]{2,1,0:T(8,128)(2,1)S(1)}, u32[]{:S(2)}) copy-start(bf16[5,48,384]{2,1,0:T(8,128)(2,1)S(1)} %collective-permute-done.18.refs_4_) | copy-start | bytes 552964
  213.3 32.6 %collective-permute-start.23 = (bf16[5,48,384]{2,1,0:T(8,128)(2,1)}, bf16[5,48,384]{2,1,0:T(8,128)(2,1)S(1)}, u32[]{:S(2)}, u32[]{:S(2)}) collective-permute-start(bf16[5,48,384]{2,1,0:T(8,128)(2,1)} %get-tuple-element.102), channel_id=1, source_target_pairs={{0,9},{1,8},{2,11},{3,10},{4,13},{5,12},{6,15},{7,14},{8,1},{9,0},... | collective-permute-start | bytes 552968 | tf_op jit(solution)/shard_map/ppermute | solution.py:348
  213.4 58.6 %copy-start.4 = (bf16[5,48,384]{2,1,0:T(8,128)(2,1)}, bf16[5,48,384]{2,1,0:T(8,128)(2,1)S(1)}, u32[]{:S(2)}) copy-start(bf16[5,48,384]{2,1,0:T(8,128)(2,1)S(1)} %collective-permute-done.17.refs_3_) | copy-start | bytes 552964
  213.4 36.5 %collective-permute-start.22 = (bf16[5,48,384]{2,1,0:T(8,128)(2,1)}, bf16[5,48,384]{2,1,0:T(8,128)(2,1)S(1)}, u32[]{:S(2)}, u32[]{:S(2)}) collective-permute-start(bf16[5,48,384]{2,1,0:T(8,128)(2,1)} %get-tuple-element.100), channel_id=1, source_target_pairs={{0,8},{1,9},{2,10},{3,11},{4,12},{5,13},{6,14},{7,15},{8,0},{9,1},... | collective-permute-start | bytes 552968 | tf_op jit(solution)/shard_map/ppermute | solution.py:348
  214.2 57.8 %copy-start.5 = (bf16[5,48,384]{2,1,0:T(8,128)(2,1)}, bf16[5,48,384]{2,1,0:T(8,128)(2,1)S(1)}, u32[]{:S(2)}) copy-start(bf16[5,48,384]{2,1,0:T(8,128)(2,1)S(1)} %collective-permute-done.16.refs_2_) | copy-start | bytes 552964
  214.2 37.6 %collective-permute-start.21 = (bf16[5,48,384]{2,1,0:T(8,128)(2,1)}, bf16[5,48,384]{2,1,0:T(8,128)(2,1)S(1)}, u32[]{:S(2)}, u32[]{:S(2)}) collective-permute-start(bf16[5,48,384]{2,1,0:T(8,128)(2,1)} %get-tuple-element.98), channel_id=1, source_target_pairs={{0,7},{1,6},{2,5},{3,4},{4,3},{5,2},{6,1},{7,0},{8,15},{9,14},{10,... | collective-permute-start | bytes 552968 | tf_op jit(solution)/shard_map/ppermute | solution.py:348
  222.8 49.1 %copy-start.6 = (bf16[5,48,384]{2,1,0:T(8,128)(2,1)}, bf16[5,48,384]{2,1,0:T(8,128)(2,1)S(1)}, u32[]{:S(2)}) copy-start(bf16[5,48,384]{2,1,0:T(8,128)(2,1)S(1)} %collective-permute-done.15.refs_1_) | copy-start | bytes 552964
  222.8 30.3 %collective-permute-start.20 = (bf16[5,48,384]{2,1,0:T(8,128)(2,1)}, bf16[5,48,384]{2,1,0:T(8,128)(2,1)S(1)}, u32[]{:S(2)}, u32[]{:S(2)}) collective-permute-start(bf16[5,48,384]{2,1,0:T(8,128)(2,1)} %get-tuple-element.96), channel_id=1, source_target_pairs={{0,6},{1,7},{2,4},{3,5},{4,2},{5,3},{6,0},{7,1},{8,14},{9,15},{10,... | collective-permute-start | bytes 552968 | tf_op jit(solution)/shard_map/ppermute | solution.py:348
  242.0 30.0 %copy-start.7 = (bf16[5,48,384]{2,1,0:T(8,128)(2,1)}, bf16[5,48,384]{2,1,0:T(8,128)(2,1)S(1)}, u32[]{:S(2)}) copy-start(bf16[5,48,384]{2,1,0:T(8,128)(2,1)S(1)} %collective-permute-done.24.refs_10_) | copy-start | bytes 552964
  242.0 14.6 %collective-permute-start.29 = (bf16[5,48,384]{2,1,0:T(8,128)(2,1)}, bf16[5,48,384]{2,1,0:T(8,128)(2,1)S(1)}, u32[]{:S(2)}, u32[]{:S(2)}) collective-permute-start(bf16[5,48,384]{2,1,0:T(8,128)(2,1)} %get-tuple-element.114), channel_id=1, source_target_pairs={{0,15},{1,14},{2,13},{3,12},{4,11},{5,10},{6,9},{7,8},{8,7},{9,6},... | collective-permute-start | bytes 552968 | tf_op jit(solution)/shard_map/ppermute | solution.py:348
  245.9 26.1 %copy-start.8 = (bf16[5,48,384]{2,1,0:T(8,128)(2,1)}, bf16[5,48,384]{2,1,0:T(8,128)(2,1)S(1)}, u32[]{:S(2)}) copy-start(bf16[5,48,384]{2,1,0:T(8,128)(2,1)S(1)} %collective-permute-done.23.refs_9_) | copy-start | bytes 552964
  245.9 16.2 %collective-permute-start.28 = (bf16[5,48,384]{2,1,0:T(8,128)(2,1)}, bf16[5,48,384]{2,1,0:T(8,128)(2,1)S(1)}, u32[]{:S(2)}, u32[]{:S(2)}) collective-permute-start(bf16[5,48,384]{2,1,0:T(8,128)(2,1)} %get-tuple-element.112), channel_id=1, source_target_pairs={{0,14},{1,15},{2,12},{3,13},{4,10},{5,11},{6,8},{7,9},{8,6},{9,7},... | collective-permute-start | bytes 552968 | tf_op jit(solution)/shard_map/ppermute | solution.py:348
  249.9 22.1 %copy-start.9 = (bf16[5,48,384]{2,1,0:T(8,128)(2,1)}, bf16[5,48,384]{2,1,0:T(8,128)(2,1)S(1)}, u32[]{:S(2)}) copy-start(bf16[5,48,384]{2,1,0:T(8,128)(2,1)S(1)} %collective-permute-done.22.refs_8_) | copy-start | bytes 552964
  249.9 17.1 %collective-permute-start.27 = (bf16[5,48,384]{2,1,0:T(8,128)(2,1)}, bf16[5,48,384]{2,1,0:T(8,128)(2,1)S(1)}, u32[]{:S(2)}, u32[]{:S(2)}) collective-permute-start(bf16[5,48,384]{2,1,0:T(8,128)(2,1)} %get-tuple-element.110), channel_id=1, source_target_pairs={{0,13},{1,12},{2,15},{3,14},{4,9},{5,8},{6,11},{7,10},{8,5},{9,4},... | collective-permute-start | bytes 552968 | tf_op jit(solution)/shard_map/ppermute | solution.py:348
  251.8 20.2 %copy-start.10 = (bf16[5,48,384]{2,1,0:T(8,128)(2,1)}, bf16[5,48,384]{2,1,0:T(8,128)(2,1)S(1)}, u32[]{:S(2)}) copy-start(bf16[5,48,384]{2,1,0:T(8,128)(2,1)S(1)} %collective-permute-done.21.refs_7_) | copy-start | bytes 552964
  251.8 20.2 %collective-permute-start.26 = (bf16[5,48,384]{2,1,0:T(8,128)(2,1)}, bf16[5,48,384]{2,1,0:T(8,128)(2,1)S(1)}, u32[]{:S(2)}, u32[]{:S(2)}) collective-permute-start(bf16[5,48,384]{2,1,0:T(8,128)(2,1)} %get-tuple-element.108), channel_id=1, source_target_pairs={{0,12},{1,13},{2,14},{3,15},{4,8},{5,9},{6,10},{7,11},{8,4},{9,5},... | collective-permute-start | bytes 552968 | tf_op jit(solution)/shard_map/ppermute | solution.py:348
  253.1 18.9 %copy-start.11 = (bf16[5,48,384]{2,1,0:T(8,128)(2,1)}, bf16[5,48,384]{2,1,0:T(8,128)(2,1)S(1)}, u32[]{:S(2)}) copy-start(bf16[5,48,384]{2,1,0:T(8,128)(2,1)S(1)} %collective-permute-done.20.refs_6_) | copy-start | bytes 552964
  253.1 22.1 %collective-permute-start.25 = (bf16[5,48,384]{2,1,0:T(8,128)(2,1)}, bf16[5,48,384]{2,1,0:T(8,128)(2,1)}, u32[]{:S(2)}, u32[]{:S(2)}) collective-permute-start(bf16[5,48,384]{2,1,0:T(8,128)(2,1)} %get-tuple-element.106), channel_id=1, source_target_pairs={{0,11},{1,10},{2,9},{3,8},{4,15},{5,14},{6,13},{7,12},{8,3},{9,2},... | collective-permute-start | bytes 552968 | tf_op jit(solution)/shard_map/ppermute | solution.py:348
  256.6 15.4 %copy-start.12 = (bf16[5,48,384]{2,1,0:T(8,128)(2,1)}, bf16[5,48,384]{2,1,0:T(8,128)(2,1)S(1)}, u32[]{:S(2)}) copy-start(bf16[5,48,384]{2,1,0:T(8,128)(2,1)S(1)} %collective-permute-done.29.refs_15_) | copy-start | bytes 552964
  262.1 9.9 %copy-start.13 = (bf16[5,48,384]{2,1,0:T(8,128)(2,1)}, bf16[5,48,384]{2,1,0:T(8,128)(2,1)S(1)}, u32[]{:S(2)}) copy-start(bf16[5,48,384]{2,1,0:T(8,128)(2,1)S(1)} %collective-permute-done.28.refs_14_) | copy-start | bytes 552964
  267.0 5.0 %copy-start.14 = (bf16[5,48,384]{2,1,0:T(8,128)(2,1)}, bf16[5,48,384]{2,1,0:T(8,128)(2,1)S(1)}, u32[]{:S(2)}) copy-start(bf16[5,48,384]{2,1,0:T(8,128)(2,1)S(1)} %collective-permute-done.27.refs_13_) | copy-start | bytes 552964
  275.2 1.8 copy-start.1
  283.3 28.9 %all-to-all-start.2 = ((bf16[16,3,48,384]{3,2,1,0:T(8,128)(2,1)}), bf16[16,3,48,384]{3,2,1,0:T(8,128)(2,1)S(1)}, u32[]{:S(2)}, u32[]{:S(2)}) async-start(bf16[16,3,48,384]{3,2,1,0:T(8,128)(2,1)} %contract.3), calls=%async_computation.2 | async-start | bytes 3538944 | tf_op jit(solution)/shard_map/all_to_all | solution.py:340
  (2 other events, 2.0 us)

commit v4 on v3

--- a/solution.py
+++ b/solution.py
@@ -11,14 +11,14 @@
 norm_eps = 1e-05
 ROWS = 16
 LANES = 128
-VMEM_BYTES = 56 * 1024 * 1024
+VMEM_BYTES = 63 * 1024 * 1024 + 256 * 1024
 HALF = ("near", "y", "x", "core")
 ALL = ("half", *HALF)
 SPLIT = (5, 3)
 
 
-def params():
-    return pltpu.CompilerParams(vmem_limit_bytes=VMEM_BYTES)
+def params(vmem=VMEM_BYTES):
+    return pltpu.CompilerParams(vmem_limit_bytes=vmem)
 
 
 def sigmoid(x):
@@ -150,7 +150,7 @@
         grid=(rows // ROWS,),
         in_specs=[pl.BlockSpec((ROWS, width, cols), lambda r: (r, 0, 0)), spec_whole(out_gate.shape)],
         out_specs=pl.BlockSpec((ROWS, cols, width), lambda r: (r, 0, 0)),
-        out_shape=jax.ShapeDtypeStruct((rows, cols, width), jnp.float32),
+        out_shape=jax.ShapeDtypeStruct((rows, cols, width), jnp.bfloat16),
         compiler_params=params(),
         cost_estimate=pl.CostEstimate(
             flops=2 * rows * cols * width * width, bytes_accessed=4 * rows * cols * width, transcendentals=rows * cols * width
@@ -300,7 +300,7 @@
         after_it = jnp.concatenate([held[j, pl.ds(i, late, stride=rows), :] for j in range(held.shape[0])], axis=1)
         mixed = jnp.concatenate([before.astype(jnp.bfloat16), after_it.astype(jnp.bfloat16)], axis=0)
         linear = lax.dot_general(mixed, proj_ref[...], (((0,), (0,)), ((), ())), preferred_element_type=jnp.float32)
-        out_ref[i] = (gate_ref[i] * linear).astype(jnp.bfloat16)
+        out_ref[i] = (gate_ref[i].astype(jnp.float32) * linear).astype(jnp.bfloat16)
         return 0
 
     lax.fori_loop(0, rows, one_row, 0, unroll=rows)
@@ -340,11 +340,11 @@
     return lax.all_to_all(x, axes, split_axis=0, concat_axis=0, tiled=True)
 
 
-def partners(blocks):
+def partners(blocks, abreast):
     n = len(blocks)
     moved = [blocks[0]]
     for d in range(1, n):
-        block = blocks[d] if d <= 5 else after(blocks[d], moved[d - 5])
+        block = blocks[d] if d <= abreast else after(blocks[d], moved[d - abreast])
         moved.append(lax.ppermute(block, HALF, [(i, i ^ d) for i in range(n)]))
     return moved
 
@@ -380,10 +380,10 @@
         pair_input, left_gate, left_value, norm_gain, token_mask, col_mask, at, 0, hidden, True, True,
         functools.partial(write_left, sizes, owners), [(own,)] * owners,
     )
-    lefts = partners(lefts)
+    lefts = partners(lefts, 6)
     (right,) = right_chunk(normed, 1, False)
     second = exchange(after(right, first, *lefts), ALL)
-    blocks = partners(contract(lefts, first, at, 0, True))
+    blocks = partners(contract(lefts, first, at, 0, True), 5)
     (out,) = contract(lefts, after(second, *blocks), at, firsts[1], False)
     last = exchange(out, HALF)
     gate = output_gate(normed, out_gate)

time: 324 us -> 320 us (0.988)
  waiting for transfers between devices: 164 us -> 176 us
  starting transfers between devices: 78.9 us -> 68.3 us
  local copies, waits for them, and re-layouts: 4.42 us -> 0.61 us
    ppermute x30, waiting for transfers between devices: 154 us -> 165 us  [partners(): moved.append(lax.ppermute(block, HALF, [(i, i ^ d) for i in range(n)]))]
    ppermute x30, starting transfers between devices: 61.5 us -> 52.7 us  [partners(): moved.append(lax.ppermute(block, HALF, [(i, i ^ d) for i in range(n)]))]
    unnamed x34 -> x12, local copies, waits for them, and re-layouts: 3.82 us -> 0.02 us
  transfers between devices with their start and end apart: 33 -> 33, of which waited for: 21 -> 23; matrix products, arithmetic and copies ran while one was open for 0% -> 0% of each run, Pallas kernels for 15% -> 15%
where the time goes in v4:
time: 320 us; the launch traced here: 319 us
  waiting for transfers between devices  176 us (55%)
  Pallas kernels  73.2 us (23%)
  starting transfers between devices  68.3 us (21%)
    ppermute x30, waiting for transfers between devices, partners(): moved.append(lax.ppermute(block, HALF, [(i, i ^ d) for i in range(n)]))  165 us
    ppermute x30, starting transfers between devices, partners(): moved.append(lax.ppermute(block, HALF, [(i, i ^ d) for i in range(n)]))  52.7 us
    pallas_call x3, Pallas kernels, project(): pl.pallas_call(functools.partial(project_kernel, low, high, norm_first, k...  34.8 us
    all_to_all x3, starting transfers between devices, exchange(): return lax.all_to_all(x, axes, split_axis=0, concat_axis=0, tiled=True)  15.6 us
    pallas_call x2, Pallas kernels, contract(): pl.pallas_call(functools.partial(contract_kernel, n, by_partner, rows, co...  15.2 us
    all_to_all x3, waiting for transfers between devices, exchange(): return lax.all_to_all(x, axes, split_axis=0, concat_axis=0, tiled=True)  10.7 us
    pallas_call x1, Pallas kernels, finish(): pl.pallas_call(finish_kernel, grid=(rows // ROWS,), in_specs=[SMEM, spec_...  8.64 us
    pallas_call x1, Pallas kernels, output_gate(): pl.pallas_call(gate_kernel, grid=(rows // ROWS,), in_specs=[pl.BlockSpec(...  8.23 us
  transfers between devices with their start and end apart: 33, of which 23 were waited for; matrix products, arithmetic and copies ran while one was open for 0% of the time, Pallas kernels for 15%

profile of v4, /device:TPU:0, one launch (start us, length us, event | category | flops | bytes accessed | tf_op | source)
XLA Modules:
  0.0 319.0 jit_solution(12921152026393606023)
XLA Ops:
  0.6 11.2 %project.4 = bf16[32,5,48,384]{3,2,1,0:T(8,128)(2,1)} custom-call(s32[768]{0:T(1024)} %mask_ref.5, s32[3]{0:T(128)} %pad_add_fusion.at_ref, bf16[48,384,128]{2,1,0:T(8,128)(2,1)} %x_ref.3, bf16[128,128]{1,0:T(8,128)(2,1)} %gate_ref.7, bf16[128,128]{1,0:T(8,128)(2,1)} %value_ref.5, f32[1,128]{1,0:T(1,128)} %bitcast.5), custom_call_target="tpu_custom_call" | custom-call | flops 754974720 | bytes 18874368 | tf_op jit(solution)/shard_map/project/pallas_call | solution.py:117
  11.8 7.4 %all-to-all-start = ((bf16[32,5,48,384]{3,2,1,0:T(8,128)(2,1)}), bf16[32,5,48,384]{3,2,1,0:T(8,128)(2,1)}, u32[]{:S(2)}, u32[]{:S(2)}) async-start(bf16[32,5,48,384]{3,2,1,0:T(8,128)(2,1)} %project.4), calls=%async_computation | async-start | bytes 11796480 | tf_op jit(solution)/shard_map/all_to_all | solution.py:340
  19.8 16.8 %project.3 = (bf16[48,128,384]{2,1,0:T(8,128)(2,1)}, bf16[8,48,384]{2,1,0:T(8,128)(2,1)}, bf16[8,48,384]{2,1,0:T(8,128)(2,1)}, bf16[8,48,384]{2,1,0:T(8,128)(2,1...) custom-call(s32[768]{0:T(1024)} %mask_ref.5, ...), custom_call_target="tpu_custom_call" | custom-call | flops 1207959552 | bytes 18874368 | tf_op jit(solution)/shard_map/project/pallas_call | solution.py:117
  36.7 1.5 collective-permute-start.2
  38.6 2.6 collective-permute-start.5
  41.6 25.5 %collective-permute-done.2.refs_3_ = bf16[8,48,384]{2,1,0:T(8,128)(2,1)S(1)} collective-permute-done((bf16[8,48,384]{2,1,0:T(8,128)(2,1)}, bf16[8,48,384]{2,1,0:T(8,128)(2,1)S(1)}, u32[]{:S(2)}, u32[]{:S(2)}) %collective-permute-start.2) | collective-permute-done | bytes 294944 | tf_op jit(solution)/shard_map/ppermute | solution.py:348
  67.1 5.3 %collective-permute-start.3 = (bf16[8,48,384]{2,1,0:T(8,128)(2,1)}, bf16[8,48,384]{2,1,0:T(8,128)(2,1)}, u32[]{:S(2)}, u32[]{:S(2)}) collective-permute-start(bf16[8,48,384]{2,1,0:T(8,128)(2,1)} %get-tuple-element.66), channel_id=1, source_target_pairs={{0,4},{1,5},{2,6},{3,7},{4,0},{5,1},{6,2},{7,3},{8,12},{9,13},{10,... | collective-permute-start | bytes 884744 | tf_op jit(solution)/shard_map/ppermute | solution.py:348
  72.4 15.2 %collective-permute-done.1.refs_2_ = bf16[8,48,384]{2,1,0:T(8,128)(2,1)S(1)} collective-permute-done((bf16[8,48,384]{2,1,0:T(8,128)(2,1)}, bf16[8,48,384]{2,1,0:T(8,128)(2,1)S(1)}, u32[]{:S(2)}, u32[]{:S(2)}) %collective-permute-start.1) | collective-permute-done | bytes 294944 | tf_op jit(solution)/shard_map/ppermute | solution.py:348
  87.7 10.4 %collective-permute-done.5.refs_6_ = bf16[8,48,384]{2,1,0:T(8,128)(2,1)} collective-permute-done((bf16[8,48,384]{2,1,0:T(8,128)(2,1)}, bf16[8,48,384]{2,1,0:T(8,128)(2,1)}, u32[]{:S(2)}, u32[]{:S(2)}) %collective-permute-start.5) | collective-permute-done | bytes 294944 | tf_op jit(solution)/shard_map/ppermute | solution.py:348
  99.0 3.0 collective-permute-start.10
  102.0 20.9 %collective-permute-done.8.refs_9_ = bf16[8,48,384]{2,1,0:T(8,128)(2,1)} collective-permute-done((bf16[8,48,384]{2,1,0:T(8,128)(2,1)}, bf16[8,48,384]{2,1,0:T(8,128)(2,1)}, u32[]{:S(2)}, u32[]{:S(2)}) %collective-permute-start.8) | collective-permute-done | bytes 294944 | tf_op jit(solution)/shard_map/ppermute | solution.py:348
  122.9 2.1 collective-permute-start.9
  125.1 4.2 %collective-permute-done.7.refs_8_ = bf16[8,48,384]{2,1,0:T(8,128)(2,1)} collective-permute-done((bf16[8,48,384]{2,1,0:T(8,128)(2,1)}, bf16[8,48,384]{2,1,0:T(8,128)(2,1)}, u32[]{:S(2)}, u32[]{:S(2)}) %collective-permute-start.7) | collective-permute-done | bytes 294944 | tf_op jit(solution)/shard_map/ppermute | solution.py:348
  129.3 3.9 %collective-permute-start.14 = (bf16[8,48,384]{2,1,0:T(8,128)(2,1)}, bf16[8,48,384]{2,1,0:T(8,128)(2,1)}, u32[]{:S(2)}, u32[]{:S(2)}) collective-permute-start(bf16[8,48,384]{2,1,0:T(8,128)(2,1)} %get-tuple-element.86), channel_id=1, source_target_pairs={{0,15},{1,14},{2,13},{3,12},{4,11},{5,10},{6,9},{7,8},{8,7},{9,6},... | collective-permute-start | bytes 884744 | tf_op jit(solution)/shard_map/ppermute | solution.py:348
  133.1 1.3 collective-permute-start.13
  134.4 1.2 collective-permute-done.11.refs_12_
  135.6 2.5 collective-permute-start.12
  138.1 6.7 %project.5 = bf16[32,3,48,384]{3,2,1,0:T(8,128)(2,1)} custom-call(s32[768]{0:T(1024)} %mask_ref.5, s32[3]{0:T(128)} %pad_add_fusion.at_ref, bf16[48,128,384]{2,1,0:T(8,128)(2,1)} %get-tuple-element.61.normed_ref.x_ref, bf16[128,128]{1,0:T(8,128)(2,1)} %gate_ref.7, bf16[128,128]{1,0:T(8,128)(2,1)} %value_ref.5, f32[1,128]{1,0:T(1,128)} %bitcast.7), custom_call_target="tpu_custom_call" | custom-call | flops 452984832 | bytes 18874368 | tf_op jit(solution)/shard_map/project/pallas_call | solution.py:117
  144.8 2.0 collective-permute-done.10.refs_11_
  146.8 6.3 %collective-permute-done.9.refs_10_ = bf16[8,48,384]{2,1,0:T(8,128)(2,1)} collective-permute-done((bf16[8,48,384]{2,1,0:T(8,128)(2,1)}, bf16[8,48,384]{2,1,0:T(8,128)(2,1)}, u32[]{:S(2)}, u32[]{:S(2)}) %collective-permute-start.9) | collective-permute-done | bytes 294944 | tf_op jit(solution)/shard_map/ppermute | solution.py:348
  153.1 9.7 %collective-permute-done.14.refs_15_ = bf16[8,48,384]{2,1,0:T(8,128)(2,1)} collective-permute-done((bf16[8,48,384]{2,1,0:T(8,128)(2,1)}, bf16[8,48,384]{2,1,0:T(8,128)(2,1)}, u32[]{:S(2)}, u32[]{:S(2)}) %collective-permute-start.14) | collective-permute-done | bytes 294944 | tf_op jit(solution)/shard_map/ppermute | solution.py:348
  162.8 10.3 %collective-permute-done.13.refs_14_ = bf16[8,48,384]{2,1,0:T(8,128)(2,1)} collective-permute-done((bf16[8,48,384]{2,1,0:T(8,128)(2,1)}, bf16[8,48,384]{2,1,0:T(8,128)(2,1)}, u32[]{:S(2)}, u32[]{:S(2)}) %collective-permute-start.13) | collective-permute-done | bytes 294944 | tf_op jit(solution)/shard_map/ppermute | solution.py:348
  173.0 2.3 collective-permute-done.12.refs_13_
  175.3 3.7 %all-to-all-start.1 = ((bf16[32,3,48,384]{3,2,1,0:T(8,128)(2,1)}), bf16[32,3,48,384]{3,2,1,0:T(8,128)(2,1)}, u32[]{:S(2)}, u32[]{:S(2)}) async-start(bf16[32,3,48,384]{3,2,1,0:T(8,128)(2,1)} %project.5), calls=%async_computation.1 | async-start | bytes 7077888 | tf_op jit(solution)/shard_map/all_to_all | solution.py:340
  179.1 9.0 %contract.2 = (bf16[5,48,384]{2,1,0:T(8,128)(2,1)}, bf16[5,48,384]{2,1,0:T(8,128)(2,1)}, bf16[5,48,384]{2,1,0:T(8,128)(2,1)}, bf16[5,48,384]{2,1,0:T(8,128)(2,1)...) custom-call(s32[3]{0:T(128)} %pad_add_fusion.at_ref, ...), custom_call_target="tpu_custom_call" | custom-call | flops 18119393280 | bytes 11796480 | tf_op jit(solution)/shard_map/contract/pallas_call | solution.py:196
  188.1 1.2 collective-permute-start.19
  189.7 2.6 collective-permute-start.17
  192.7 13.9 %collective-permute-done.19.refs_5_ = bf16[5,48,384]{2,1,0:T(8,128)(2,1)S(1)} collective-permute-done((bf16[5,48,384]{2,1,0:T(8,128)(2,1)}, bf16[5,48,384]{2,1,0:T(8,128)(2,1)S(1)}, u32[]{:S(2)}, u32[]{:S(2)}) %collective-permute-start.19) | collective-permute-done | bytes 184352 | tf_op jit(solution)/shard_map/ppermute | solution.py:348
  207.7 5.1 %collective-permute-done.18.refs_4_ = bf16[5,48,384]{2,1,0:T(8,128)(2,1)S(1)} collective-permute-done((bf16[5,48,384]{2,1,0:T(8,128)(2,1)}, bf16[5,48,384]{2,1,0:T(8,128)(2,1)S(1)}, u32[]{:S(2)}, u32[]{:S(2)}) %collective-permute-start.18) | collective-permute-done | bytes 184352 | tf_op jit(solution)/shard_map/ppermute | solution.py:348
  213.9 8.4 %collective-permute-start.21 = (bf16[5,48,384]{2,1,0:T(8,128)(2,1)}, bf16[5,48,384]{2,1,0:T(8,128)(2,1)}, u32[]{:S(2)}, u32[]{:S(2)}) collective-permute-start(bf16[5,48,384]{2,1,0:T(8,128)(2,1)} %get-tuple-element.96), channel_id=1, source_target_pairs={{0,7},{1,6},{2,5},{3,4},{4,3},{5,2},{6,1},{7,0},{8,15},{9,14},{10,... | collective-permute-start | bytes 552968 | tf_op jit(solution)/shard_map/ppermute | solution.py:348
  222.3 1.3 collective-permute-start.20
  223.6 17.9 %collective-permute-done.24.refs_10_ = bf16[5,48,384]{2,1,0:T(8,128)(2,1)} collective-permute-done((bf16[5,48,384]{2,1,0:T(8,128)(2,1)}, bf16[5,48,384]{2,1,0:T(8,128)(2,1)}, u32[]{:S(2)}, u32[]{:S(2)}) %collective-permute-start.24) | collective-permute-done | bytes 184352 | tf_op jit(solution)/shard_map/ppermute | solution.py:348
  241.5 2.8 collective-permute-start.29
  244.3 1.1 collective-permute-done.23.refs_9_
  245.4 3.7 %collective-permute-start.28 = (bf16[5,48,384]{2,1,0:T(8,128)(2,1)}, bf16[5,48,384]{2,1,0:T(8,128)(2,1)}, u32[]{:S(2)}, u32[]{:S(2)}) collective-permute-start(bf16[5,48,384]{2,1,0:T(8,128)(2,1)} %get-tuple-element.110), channel_id=1, source_target_pairs={{0,14},{1,15},{2,12},{3,13},{4,10},{5,11},{6,8},{7,9},{8,6},{9,7},... | collective-permute-start | bytes 552968 | tf_op jit(solution)/shard_map/ppermute | solution.py:348
  249.4 1.9 collective-permute-start.27
  251.3 1.3 collective-permute-start.26
  252.6 4.0 %collective-permute-start.25 = (bf16[5,48,384]{2,1,0:T(8,128)(2,1)}, bf16[5,48,384]{2,1,0:T(8,128)(2,1)}, u32[]{:S(2)}, u32[]{:S(2)}) collective-permute-start(bf16[5,48,384]{2,1,0:T(8,128)(2,1)} %get-tuple-element.104), channel_id=1, source_target_pairs={{0,11},{1,10},{2,9},{3,8},{4,15},{5,14},{6,13},{7,12},{8,3},{9,2},... | collective-permute-start | bytes 552968 | tf_op jit(solution)/shard_map/ppermute | solution.py:348
  256.5 5.2 %collective-permute-done.28.refs_14_ = bf16[5,48,384]{2,1,0:T(8,128)(2,1)} collective-permute-done((bf16[5,48,384]{2,1,0:T(8,128)(2,1)}, bf16[5,48,384]{2,1,0:T(8,128)(2,1)}, u32[]{:S(2)}, u32[]{:S(2)}) %collective-permute-start.28) | collective-permute-done | bytes 184352 | tf_op jit(solution)/shard_map/ppermute | solution.py:348
  261.7 6.0 %collective-permute-done.27.refs_13_ = bf16[5,48,384]{2,1,0:T(8,128)(2,1)} collective-permute-done((bf16[5,48,384]{2,1,0:T(8,128)(2,1)}, bf16[5,48,384]{2,1,0:T(8,128)(2,1)}, u32[]{:S(2)}, u32[]{:S(2)}) %collective-permute-start.27) | collective-permute-done | bytes 184352 | tf_op jit(solution)/shard_map/ppermute | solution.py:348
  267.7 4.0 %collective-permute-done.26.refs_12_ = bf16[5,48,384]{2,1,0:T(8,128)(2,1)} collective-permute-done((bf16[5,48,384]{2,1,0:T(8,128)(2,1)}, bf16[5,48,384]{2,1,0:T(8,128)(2,1)}, u32[]{:S(2)}, u32[]{:S(2)}) %collective-permute-start.26) | collective-permute-done | bytes 184352 | tf_op jit(solution)/shard_map/ppermute | solution.py:348
  271.7 2.7 collective-permute-done.25.refs_11_
  274.4 6.2 %contract.3 = bf16[16,3,48,384]{3,2,1,0:T(8,128)(2,1)} custom-call(s32[3]{0:T(128)} %pad_add_fusion.at_ref, bf16[8,48,384]{2,1,0:T(8,128)(2,1)} %get-tuple-element.62.refs_0_, bf16[8,48,384]{2,1,0:T(8,128)(2,1)} %collective-permute-done.refs_1_, bf16[8,48,384]{2,1,0:T(8,128)(2,1)} %copy-done.5, bf16[8,48,384]{2,1,0:T(8,128)(2,1)} %copy-done.4, ...), custom_call_target="tpu_custom_call" | custom-call | flops 10871635968 | bytes 7077888 | tf_op jit(solution)/shard_map/contract/pallas_call | solution.py:196
  280.6 4.4 %all-to-all-start.2 = ((bf16[16,3,48,384]{3,2,1,0:T(8,128)(2,1)}), bf16[16,3,48,384]{3,2,1,0:T(8,128)(2,1)}, u32[]{:S(2)}, u32[]{:S(2)}) async-start(bf16[16,3,48,384]{3,2,1,0:T(8,128)(2,1)} %contract.3), calls=%async_computation.2 | async-start | bytes 3538944 | tf_op jit(solution)/shard_map/all_to_all | solution.py:340
  285.1 8.2 %output_gate.1.gate_ref = bf16[48,384,128]{2,1,0:T(8,128)(2,1)} custom-call(bf16[48,128,384]{2,1,0:T(8,128)(2,1)} %get-tuple-element.61.normed_ref.x_ref, bf16[128,128]{1,0:T(8,128)(2,1)} %gate_ref.5), custom_call_target="tpu_custom_call" | custom-call | flops 603979776 | bytes 9437184 | tf_op jit(solution)/shard_map/output_gate/pallas_call | solution.py:148
  293.3 6.3 %gather.1 = (bf16[48,80,384]{2,1,0:T(8,128)(2,1)}, f32[2,48,384]{2,1,0:T(8,128)}) custom-call(s32[3]{0:T(128)} %pad_add_fusion.at_ref, bf16[5,48,384]{2,1,0:T(8,128)(2,1)} %get-tuple-element.87.refs_0_, bf16[5,48,384]{2,1,0:T(8,128)(2,1)} %collective-permute-done.15.refs_1_, bf16[5,48,384]{2,1,0:T(8,128)(2,1)} %collective-permute-done.16.refs_2_, ...), custom_call_target="tpu_custom_call" | custom-call | flops 5898240 | bytes 5898240 | tf_op jit(solution)/shard_map/gather/pallas_call | solution.py:244
  299.6 10.7 %all-to-all-done.2.last_ref = bf16[16,3,48,384]{3,2,1,0:T(8,128)(2,1)} async-done(((bf16[16,3,48,384]{3,2,1,0:T(8,128)(2,1)}), bf16[16,3,48,384]{3,2,1,0:T(8,128)(2,1)}, u32[]{:S(2)}, u32[]{:S(2)}) %all-to-all-start.2) | async-done | bytes 1769504 | tf_op jit(solution)/shard_map/all_to_all | solution.py:340
  310.3 8.6 %finish.1 = bf16[48,384,128]{2,1,0:T(8,128)(2,1)} custom-call(f32[128]{0:T(128)} %gain_ref.1, f32[1,128]{1,0:T(1,128)} %bitcast.8, bf16[48,384,128]{2,1,0:T(8,128)(2,1)} %output_gate.1.gate_ref, bf16[128,128]{1,0:T(8,128)(2,1)} %proj_ref.1, bf16[48,80,384]{2,1,0:T(8,128)(2,1)} %get-tuple-element.113.turned_ref, f32[2,48,384]{2,1,0:T(8,128)} %get-tuple-element.114.stats_ref, ...), custom_call_target="tpu_custom_call" | custom-call | tf_op jit(solution)/shard_map/finish/pallas_call | solution.py:315
  (40 shorter events, 5.9 us)
Async XLA Ops:
  11.8 7.4 %copy-start.3 = (s32[768]{0:T(1024)S(1)}, s32[768]{0:T(1024)}, u32[]{:S(2)}) copy-start(s32[768]{0:T(1024)} %mask_ref.5) | copy-start | bytes 9220
  11.8 163.5 %all-to-all-start = ((bf16[32,5,48,384]{3,2,1,0:T(8,128)(2,1)}), bf16[32,5,48,384]{3,2,1,0:T(8,128)(2,1)}, u32[]{:S(2)}, u32[]{:S(2)}) async-start(bf16[32,5,48,384]{3,2,1,0:T(8,128)(2,1)} %project.4), calls=%async_computation | async-start | bytes 11796480 | tf_op jit(solution)/shard_map/all_to_all | solution.py:340
  36.7 30.4 %collective-permute-start.2 = (bf16[8,48,384]{2,1,0:T(8,128)(2,1)}, bf16[8,48,384]{2,1,0:T(8,128)(2,1)S(1)}, u32[]{:S(2)}, u32[]{:S(2)}) collective-permute-start(bf16[8,48,384]{2,1,0:T(8,128)(2,1)} %get-tuple-element.65), channel_id=1, source_target_pairs={{0,3},{1,2},{2,1},{3,0},{4,7},{5,6},{6,5},{7,4},{8,11},{9,10},{10,... | collective-permute-start | bytes 884744 | tf_op jit(solution)/shard_map/ppermute | solution.py:348
  38.2 49.4 %collective-permute-start.1 = (bf16[8,48,384]{2,1,0:T(8,128)(2,1)}, bf16[8,48,384]{2,1,0:T(8,128)(2,1)S(1)}, u32[]{:S(2)}, u32[]{:S(2)}) collective-permute-start(bf16[8,48,384]{2,1,0:T(8,128)(2,1)} %get-tuple-element.64), channel_id=1, source_target_pairs={{0,2},{1,3},{2,0},{3,1},{4,6},{5,7},{6,4},{7,5},{8,10},{9,11},{10,... | collective-permute-start | bytes 884744 | tf_op jit(solution)/shard_map/ppermute | solution.py:348
  38.6 49.1 %collective-permute-start = (bf16[8,48,384]{2,1,0:T(8,128)(2,1)}, bf16[8,48,384]{2,1,0:T(8,128)(2,1)}, u32[]{:S(2)}, u32[]{:S(2)}) collective-permute-start(bf16[8,48,384]{2,1,0:T(8,128)(2,1)} %get-tuple-element.63), channel_id=1, source_target_pairs={{0,1},{1,0},{2,3},{3,2},{4,5},{5,4},{6,7},{7,6},{8,9},{9,8},{10,11... | collective-permute-start | bytes 884744 | tf_op jit(solution)/shard_map/ppermute | solution.py:348
  38.6 59.5 %collective-permute-start.5 = (bf16[8,48,384]{2,1,0:T(8,128)(2,1)}, bf16[8,48,384]{2,1,0:T(8,128)(2,1)}, u32[]{:S(2)}, u32[]{:S(2)}) collective-permute-start(bf16[8,48,384]{2,1,0:T(8,128)(2,1)} %get-tuple-element.68), channel_id=1, source_target_pairs={{0,6},{1,7},{2,4},{3,5},{4,2},{5,3},{6,0},{7,1},{8,14},{9,15},{10,... | collective-permute-start | bytes 884744 | tf_op jit(solution)/shard_map/ppermute | solution.py:348
  41.2 56.9 %collective-permute-start.4 = (bf16[8,48,384]{2,1,0:T(8,128)(2,1)}, bf16[8,48,384]{2,1,0:T(8,128)(2,1)}, u32[]{:S(2)}, u32[]{:S(2)}) collective-permute-start(bf16[8,48,384]{2,1,0:T(8,128)(2,1)} %get-tuple-element.67), channel_id=1, source_target_pairs={{0,5},{1,4},{2,7},{3,6},{4,1},{5,0},{6,3},{7,2},{8,13},{9,12},{10,... | collective-permute-start | bytes 884744 | tf_op jit(solution)/shard_map/ppermute | solution.py:348
  67.1 108.3 %copy-start.4 = (bf16[8,48,384]{2,1,0:T(8,128)(2,1)}, bf16[8,48,384]{2,1,0:T(8,128)(2,1)S(1)}, u32[]{:S(2)}) copy-start(bf16[8,48,384]{2,1,0:T(8,128)(2,1)S(1)} %collective-permute-done.2.refs_3_) | copy-start | bytes 884740
  67.1 31.9 %collective-permute-start.3 = (bf16[8,48,384]{2,1,0:T(8,128)(2,1)}, bf16[8,48,384]{2,1,0:T(8,128)(2,1)}, u32[]{:S(2)}, u32[]{:S(2)}) collective-permute-start(bf16[8,48,384]{2,1,0:T(8,128)(2,1)} %get-tuple-element.66), channel_id=1, source_target_pairs={{0,4},{1,5},{2,6},{3,7},{4,0},{5,1},{6,2},{7,3},{8,12},{9,13},{10,... | collective-permute-start | bytes 884744 | tf_op jit(solution)/shard_map/ppermute | solution.py:348
  87.6 87.7 %copy-start.5 = (bf16[8,48,384]{2,1,0:T(8,128)(2,1)}, bf16[8,48,384]{2,1,0:T(8,128)(2,1)S(1)}, u32[]{:S(2)}) copy-start(bf16[8,48,384]{2,1,0:T(8,128)(2,1)S(1)} %collective-permute-done.1.refs_2_) | copy-start | bytes 884740
  87.6 35.3 %collective-permute-start.8 = (bf16[8,48,384]{2,1,0:T(8,128)(2,1)}, bf16[8,48,384]{2,1,0:T(8,128)(2,1)}, u32[]{:S(2)}, u32[]{:S(2)}) collective-permute-start(bf16[8,48,384]{2,1,0:T(8,128)(2,1)} %get-tuple-element.74), channel_id=1, source_target_pairs={{0,9},{1,8},{2,11},{3,10},{4,13},{5,12},{6,15},{7,14},{8,1},{9,0},... | collective-permute-start | bytes 884744 | tf_op jit(solution)/shard_map/ppermute | solution.py:348
  87.7 41.6 %collective-permute-start.7 = (bf16[8,48,384]{2,1,0:T(8,128)(2,1)}, bf16[8,48,384]{2,1,0:T(8,128)(2,1)}, u32[]{:S(2)}, u32[]{:S(2)}) collective-permute-start(bf16[8,48,384]{2,1,0:T(8,128)(2,1)} %get-tuple-element.72), channel_id=1, source_target_pairs={{0,8},{1,9},{2,10},{3,11},{4,12},{5,13},{6,14},{7,15},{8,0},{9,1},... | collective-permute-start | bytes 884744 | tf_op jit(solution)/shard_map/ppermute | solution.py:348
  98.2 35.0 %collective-permute-start.6 = (bf16[8,48,384]{2,1,0:T(8,128)(2,1)}, bf16[8,48,384]{2,1,0:T(8,128)(2,1)}, u32[]{:S(2)}, u32[]{:S(2)}) collective-permute-start(bf16[8,48,384]{2,1,0:T(8,128)(2,1)} %get-tuple-element.70), channel_id=1, source_target_pairs={{0,7},{1,6},{2,5},{3,4},{4,3},{5,2},{6,1},{7,0},{8,15},{9,14},{10,... | collective-permute-start | bytes 884744 | tf_op jit(solution)/shard_map/ppermute | solution.py:348
  98.2 37.4 %collective-permute-start.11 = (bf16[8,48,384]{2,1,0:T(8,128)(2,1)}, bf16[8,48,384]{2,1,0:T(8,128)(2,1)}, u32[]{:S(2)}, u32[]{:S(2)}) collective-permute-start(bf16[8,48,384]{2,1,0:T(8,128)(2,1)} %get-tuple-element.80), channel_id=1, source_target_pairs={{0,12},{1,13},{2,14},{3,15},{4,8},{5,9},{6,10},{7,11},{8,4},{9,5},... | collective-permute-start | bytes 884744 | tf_op jit(solution)/shard_map/ppermute | solution.py:348
  99.0 47.8 %collective-permute-start.10 = (bf16[8,48,384]{2,1,0:T(8,128)(2,1)}, bf16[8,48,384]{2,1,0:T(8,128)(2,1)}, u32[]{:S(2)}, u32[]{:S(2)}) collective-permute-start(bf16[8,48,384]{2,1,0:T(8,128)(2,1)} %get-tuple-element.78), channel_id=1, source_target_pairs={{0,11},{1,10},{2,9},{3,8},{4,15},{5,14},{6,13},{7,12},{8,3},{9,2},... | collective-permute-start | bytes 884744 | tf_op jit(solution)/shard_map/ppermute | solution.py:348
  122.9 30.1 %collective-permute-start.9 = (bf16[8,48,384]{2,1,0:T(8,128)(2,1)}, bf16[8,48,384]{2,1,0:T(8,128)(2,1)}, u32[]{:S(2)}, u32[]{:S(2)}) collective-permute-start(bf16[8,48,384]{2,1,0:T(8,128)(2,1)} %get-tuple-element.76), channel_id=1, source_target_pairs={{0,10},{1,11},{2,8},{3,9},{4,14},{5,15},{6,12},{7,13},{8,2},{9,3},... | collective-permute-start | bytes 884744 | tf_op jit(solution)/shard_map/ppermute | solution.py:348
  129.3 33.5 %collective-permute-start.14 = (bf16[8,48,384]{2,1,0:T(8,128)(2,1)}, bf16[8,48,384]{2,1,0:T(8,128)(2,1)}, u32[]{:S(2)}, u32[]{:S(2)}) collective-permute-start(bf16[8,48,384]{2,1,0:T(8,128)(2,1)} %get-tuple-element.86), channel_id=1, source_target_pairs={{0,15},{1,14},{2,13},{3,12},{4,11},{5,10},{6,9},{7,8},{8,7},{9,6},... | collective-permute-start | bytes 884744 | tf_op jit(solution)/shard_map/ppermute | solution.py:348
  133.1 39.9 %collective-permute-start.13 = (bf16[8,48,384]{2,1,0:T(8,128)(2,1)}, bf16[8,48,384]{2,1,0:T(8,128)(2,1)}, u32[]{:S(2)}, u32[]{:S(2)}) collective-permute-start(bf16[8,48,384]{2,1,0:T(8,128)(2,1)} %get-tuple-element.84), channel_id=1, source_target_pairs={{0,14},{1,15},{2,12},{3,13},{4,10},{5,11},{6,8},{7,9},{8,6},{9,7},... | collective-permute-start | bytes 884744 | tf_op jit(solution)/shard_map/ppermute | solution.py:348
  135.6 39.8 %collective-permute-start.12 = (bf16[8,48,384]{2,1,0:T(8,128)(2,1)}, bf16[8,48,384]{2,1,0:T(8,128)(2,1)}, u32[]{:S(2)}, u32[]{:S(2)}) collective-permute-start(bf16[8,48,384]{2,1,0:T(8,128)(2,1)} %get-tuple-element.82), channel_id=1, source_target_pairs={{0,13},{1,12},{2,15},{3,14},{4,9},{5,8},{6,11},{7,10},{8,5},{9,4},... | collective-permute-start | bytes 884744 | tf_op jit(solution)/shard_map/ppermute | solution.py:348
  175.3 99.0 %all-to-all-start.1 = ((bf16[32,3,48,384]{3,2,1,0:T(8,128)(2,1)}), bf16[32,3,48,384]{3,2,1,0:T(8,128)(2,1)}, u32[]{:S(2)}, u32[]{:S(2)}) async-start(bf16[32,3,48,384]{3,2,1,0:T(8,128)(2,1)} %project.5), calls=%async_computation.1 | async-start | bytes 7077888 | tf_op jit(solution)/shard_map/all_to_all | solution.py:340
  188.1 18.4 %collective-permute-start.19 = (bf16[5,48,384]{2,1,0:T(8,128)(2,1)}, bf16[5,48,384]{2,1,0:T(8,128)(2,1)S(1)}, u32[]{:S(2)}, u32[]{:S(2)}) collective-permute-start(bf16[5,48,384]{2,1,0:T(8,128)(2,1)} %get-tuple-element.92), channel_id=1, source_target_pairs={{0,5},{1,4},{2,7},{3,6},{4,1},{5,0},{6,3},{7,2},{8,13},{9,12},{10,... | collective-permute-start | bytes 552968 | tf_op jit(solution)/shard_map/ppermute | solution.py:348
  189.4 23.4 %collective-permute-start.18 = (bf16[5,48,384]{2,1,0:T(8,128)(2,1)}, bf16[5,48,384]{2,1,0:T(8,128)(2,1)S(1)}, u32[]{:S(2)}, u32[]{:S(2)}) collective-permute-start(bf16[5,48,384]{2,1,0:T(8,128)(2,1)} %get-tuple-element.91), channel_id=1, source_target_pairs={{0,4},{1,5},{2,6},{3,7},{4,0},{5,1},{6,2},{7,3},{8,12},{9,13},{10,... | collective-permute-start | bytes 552968 | tf_op jit(solution)/shard_map/ppermute | solution.py:348
  189.7 23.2 %collective-permute-start.17 = (bf16[5,48,384]{2,1,0:T(8,128)(2,1)}, bf16[5,48,384]{2,1,0:T(8,128)(2,1)S(1)}, u32[]{:S(2)}, u32[]{:S(2)}) collective-permute-start(bf16[5,48,384]{2,1,0:T(8,128)(2,1)} %get-tuple-element.90), channel_id=1, source_target_pairs={{0,3},{1,2},{2,1},{3,0},{4,7},{5,6},{6,5},{7,4},{8,11},{9,10},{10,... | collective-permute-start | bytes 552968 | tf_op jit(solution)/shard_map/ppermute | solution.py:348
  192.4 21.5 %collective-permute-start.16 = (bf16[5,48,384]{2,1,0:T(8,128)(2,1)}, bf16[5,48,384]{2,1,0:T(8,128)(2,1)}, u32[]{:S(2)}, u32[]{:S(2)}) collective-permute-start(bf16[5,48,384]{2,1,0:T(8,128)(2,1)} %get-tuple-element.89), channel_id=1, source_target_pairs={{0,2},{1,3},{2,0},{3,1},{4,6},{5,7},{6,4},{7,5},{8,10},{9,11},{10,... | collective-permute-start | bytes 552968 | tf_op jit(solution)/shard_map/ppermute | solution.py:348
  192.6 29.7 %collective-permute-start.15 = (bf16[5,48,384]{2,1,0:T(8,128)(2,1)}, bf16[5,48,384]{2,1,0:T(8,128)(2,1)}, u32[]{:S(2)}, u32[]{:S(2)}) collective-permute-start(bf16[5,48,384]{2,1,0:T(8,128)(2,1)} %get-tuple-element.88), channel_id=1, source_target_pairs={{0,1},{1,0},{2,3},{3,2},{4,5},{5,4},{6,7},{7,6},{8,9},{9,8},{10,11... | collective-permute-start | bytes 552968 | tf_op jit(solution)/shard_map/ppermute | solution.py:348
  206.6 74.0 %copy-start = (bf16[5,48,384]{2,1,0:T(8,128)(2,1)}, bf16[5,48,384]{2,1,0:T(8,128)(2,1)S(1)}, u32[]{:S(2)}) copy-start(bf16[5,48,384]{2,1,0:T(8,128)(2,1)S(1)} %collective-permute-done.19.refs_5_) | copy-start | bytes 552964
  206.6 34.9 %collective-permute-start.24 = (bf16[5,48,384]{2,1,0:T(8,128)(2,1)}, bf16[5,48,384]{2,1,0:T(8,128)(2,1)}, u32[]{:S(2)}, u32[]{:S(2)}) collective-permute-start(bf16[5,48,384]{2,1,0:T(8,128)(2,1)} %get-tuple-element.102), channel_id=1, source_target_pairs={{0,10},{1,11},{2,8},{3,9},{4,14},{5,15},{6,12},{7,13},{8,2},{9,3},... | collective-permute-start | bytes 552968 | tf_op jit(solution)/shard_map/ppermute | solution.py:348
  212.8 67.9 %copy-start.1 = (bf16[5,48,384]{2,1,0:T(8,128)(2,1)}, bf16[5,48,384]{2,1,0:T(8,128)(2,1)S(1)}, u32[]{:S(2)}) copy-start(bf16[5,48,384]{2,1,0:T(8,128)(2,1)S(1)} %collective-permute-done.18.refs_4_) | copy-start | bytes 552964
  212.8 32.7 %collective-permute-start.23 = (bf16[5,48,384]{2,1,0:T(8,128)(2,1)}, bf16[5,48,384]{2,1,0:T(8,128)(2,1)}, u32[]{:S(2)}, u32[]{:S(2)}) collective-permute-start(bf16[5,48,384]{2,1,0:T(8,128)(2,1)} %get-tuple-element.100), channel_id=1, source_target_pairs={{0,9},{1,8},{2,11},{3,10},{4,13},{5,12},{6,15},{7,14},{8,1},{9,0},... | collective-permute-start | bytes 552968 | tf_op jit(solution)/shard_map/ppermute | solution.py:348
  212.9 67.7 %copy-start.2 = (bf16[5,48,384]{2,1,0:T(8,128)(2,1)}, bf16[5,48,384]{2,1,0:T(8,128)(2,1)S(1)}, u32[]{:S(2)}) copy-start(bf16[5,48,384]{2,1,0:T(8,128)(2,1)S(1)} %collective-permute-done.17.refs_3_) | copy-start | bytes 552964
  212.9 36.5 %collective-permute-start.22 = (bf16[5,48,384]{2,1,0:T(8,128)(2,1)}, bf16[5,48,384]{2,1,0:T(8,128)(2,1)}, u32[]{:S(2)}, u32[]{:S(2)}) collective-permute-start(bf16[5,48,384]{2,1,0:T(8,128)(2,1)} %get-tuple-element.98), channel_id=1, source_target_pairs={{0,8},{1,9},{2,10},{3,11},{4,12},{5,13},{6,14},{7,15},{8,0},{9,1},... | collective-permute-start | bytes 552968 | tf_op jit(solution)/shard_map/ppermute | solution.py:348
  213.9 37.4 %collective-permute-start.21 = (bf16[5,48,384]{2,1,0:T(8,128)(2,1)}, bf16[5,48,384]{2,1,0:T(8,128)(2,1)}, u32[]{:S(2)}, u32[]{:S(2)}) collective-permute-start(bf16[5,48,384]{2,1,0:T(8,128)(2,1)} %get-tuple-element.96), channel_id=1, source_target_pairs={{0,7},{1,6},{2,5},{3,4},{4,3},{5,2},{6,1},{7,0},{8,15},{9,14},{10,... | collective-permute-start | bytes 552968 | tf_op jit(solution)/shard_map/ppermute | solution.py:348
  222.3 30.3 %collective-permute-start.20 = (bf16[5,48,384]{2,1,0:T(8,128)(2,1)}, bf16[5,48,384]{2,1,0:T(8,128)(2,1)}, u32[]{:S(2)}, u32[]{:S(2)}) collective-permute-start(bf16[5,48,384]{2,1,0:T(8,128)(2,1)} %get-tuple-element.94), channel_id=1, source_target_pairs={{0,6},{1,7},{2,4},{3,5},{4,2},{5,3},{6,0},{7,1},{8,14},{9,15},{10,... | collective-permute-start | bytes 552968 | tf_op jit(solution)/shard_map/ppermute | solution.py:348
  241.5 15.0 %collective-permute-start.29 = (bf16[5,48,384]{2,1,0:T(8,128)(2,1)}, bf16[5,48,384]{2,1,0:T(8,128)(2,1)}, u32[]{:S(2)}, u32[]{:S(2)}) collective-permute-start(bf16[5,48,384]{2,1,0:T(8,128)(2,1)} %get-tuple-element.112), channel_id=1, source_target_pairs={{0,15},{1,14},{2,13},{3,12},{4,11},{5,10},{6,9},{7,8},{8,7},{9,6},... | collective-permute-start | bytes 552968 | tf_op jit(solution)/shard_map/ppermute | solution.py:348
  245.4 16.3 %collective-permute-start.28 = (bf16[5,48,384]{2,1,0:T(8,128)(2,1)}, bf16[5,48,384]{2,1,0:T(8,128)(2,1)}, u32[]{:S(2)}, u32[]{:S(2)}) collective-permute-start(bf16[5,48,384]{2,1,0:T(8,128)(2,1)} %get-tuple-element.110), channel_id=1, source_target_pairs={{0,14},{1,15},{2,12},{3,13},{4,10},{5,11},{6,8},{7,9},{8,6},{9,7},... | collective-permute-start | bytes 552968 | tf_op jit(solution)/shard_map/ppermute | solution.py:348
  249.4 18.3 %collective-permute-start.27 = (bf16[5,48,384]{2,1,0:T(8,128)(2,1)}, bf16[5,48,384]{2,1,0:T(8,128)(2,1)}, u32[]{:S(2)}, u32[]{:S(2)}) collective-permute-start(bf16[5,48,384]{2,1,0:T(8,128)(2,1)} %get-tuple-element.108), channel_id=1, source_target_pairs={{0,13},{1,12},{2,15},{3,14},{4,9},{5,8},{6,11},{7,10},{8,5},{9,4},... | collective-permute-start | bytes 552968 | tf_op jit(solution)/shard_map/ppermute | solution.py:348
  251.3 20.4 %collective-permute-start.26 = (bf16[5,48,384]{2,1,0:T(8,128)(2,1)}, bf16[5,48,384]{2,1,0:T(8,128)(2,1)}, u32[]{:S(2)}, u32[]{:S(2)}) collective-permute-start(bf16[5,48,384]{2,1,0:T(8,128)(2,1)} %get-tuple-element.106), channel_id=1, source_target_pairs={{0,12},{1,13},{2,14},{3,15},{4,8},{5,9},{6,10},{7,11},{8,4},{9,5},... | collective-permute-start | bytes 552968 | tf_op jit(solution)/shard_map/ppermute | solution.py:348
  252.6 21.8 %collective-permute-start.25 = (bf16[5,48,384]{2,1,0:T(8,128)(2,1)}, bf16[5,48,384]{2,1,0:T(8,128)(2,1)}, u32[]{:S(2)}, u32[]{:S(2)}) collective-permute-start(bf16[5,48,384]{2,1,0:T(8,128)(2,1)} %get-tuple-element.104), channel_id=1, source_target_pairs={{0,11},{1,10},{2,9},{3,8},{4,15},{5,14},{6,13},{7,12},{8,3},{9,2},... | collective-permute-start | bytes 552968 | tf_op jit(solution)/shard_map/ppermute | solution.py:348
  280.6 29.7 %all-to-all-start.2 = ((bf16[16,3,48,384]{3,2,1,0:T(8,128)(2,1)}), bf16[16,3,48,384]{3,2,1,0:T(8,128)(2,1)}, u32[]{:S(2)}, u32[]{:S(2)}) async-start(bf16[16,3,48,384]{3,2,1,0:T(8,128)(2,1)} %contract.3), calls=%async_computation.2 | async-start | bytes 3538944 | tf_op jit(solution)/shard_map/all_to_all | solution.py:340

commit v5 on v4

--- a/solution.py
+++ b/solution.py
@@ -50,7 +50,7 @@
         gain = jnp.broadcast_to(gain_ref[...], (gain_ref.shape[1], gain_ref.shape[1])).T
         gain_all[...] = jnp.broadcast_to(gain[:, :1], gain_all.shape)
 
-    first_row = at_ref[0] + step * ROWS
+    first_row = (lax.axis_index(("half", "near", "y", "x")) * x_ref.shape[0] * pl.num_programs(0)) + step * ROWS
     if keep:
         normed_ref, *outs = outs
 
@@ -131,7 +131,7 @@
             flops=4 * rows * cols * width * count, bytes_accessed=8 * rows * cols * width, transcendentals=rows * cols * count
         ),
         name="project",
-    )(mask, at, x, gate, value, gain[None], *extra)
+    )(mask, mask if at is None else at, x, gate, value, gain[None], *extra)
 
 
 def gate_kernel(normed_ref, gate_ref, out_ref):
@@ -342,11 +342,12 @@
 
 def partners(blocks, abreast):
     n = len(blocks)
-    moved = [blocks[0]]
-    for d in range(1, n):
-        block = blocks[d] if d <= abreast else after(blocks[d], moved[d - abreast])
-        moved.append(lax.ppermute(block, HALF, [(i, i ^ d) for i in range(n)]))
-    return moved
+    moved = {0: blocks[0]}
+    order = [*range(1, n // 2), *(d ^ 1 for d in range(n // 2, n))]
+    for t, d in enumerate(order):
+        block = blocks[d] if t < abreast else after(blocks[d], moved[order[t - abreast]])
+        moved[d] = lax.ppermute(block, HALF, [(i, i ^ d) for i in range(n)])
+    return [moved[d] for d in range(n)]
 
 
 def after(x, *others):
@@ -369,7 +370,7 @@
 
     def right_chunk(x, q, norm_first):
         return project(
-            x, right_gate, right_value, norm_gain, token_mask, None, at,
+            x, right_gate, right_value, norm_gain, token_mask, None, None,
             firsts[q] * owners, (firsts[q] + sizes[q]) * owners, norm_first, None,
             functools.partial(write_right, sizes[q], owners), [(2 * owners, sizes[q])],
         )

time: 320 us -> 319 us (level)
  waiting for transfers between devices: 176 us -> 172 us
  starting transfers between devices: 68.3 us -> 71.5 us
    ppermute x30, waiting for transfers between devices: 165 us -> 161 us  [partners(): moved[d] = lax.ppermute(block, HALF, [(i, i ^ d) for i in range(n)])]
  transfers between devices with their start and end apart: 33 -> 33, of which waited for: 23 -> 21; matrix products, arithmetic and copies ran while one was open for 0% -> 0% of each run, Pallas kernels for 15% -> 15%
where the time goes in v5:
time: 319 us; the launch traced here: 318 us
  waiting for transfers between devices  172 us (54%)
  Pallas kernels  73.2 us (23%)
  starting transfers between devices  71.5 us (22%)
    ppermute x30, waiting for transfers between devices, partners(): moved[d] = lax.ppermute(block, HALF, [(i, i ^ d) for i in range(n)])  161 us
    ppermute x30, starting transfers between devices, partners(): moved[d] = lax.ppermute(block, HALF, [(i, i ^ d) for i in range(n)])  55.4 us
    pallas_call x3, Pallas kernels, project(): pl.pallas_call(functools.partial(project_kernel, low, high, norm_first, k...  34.7 us
    all_to_all x3, starting transfers between devices, exchange(): return lax.all_to_all(x, axes, split_axis=0, concat_axis=0, tiled=True)  16.1 us
    pallas_call x2, Pallas kernels, contract(): pl.pallas_call(functools.partial(contract_kernel, n, by_partner, rows, co...  15.3 us
    all_to_all x3, waiting for transfers between devices, exchange(): return lax.all_to_all(x, axes, split_axis=0, concat_axis=0, tiled=True)  10.7 us
    pallas_call x1, Pallas kernels, finish(): pl.pallas_call(finish_kernel, grid=(rows // ROWS,), in_specs=[SMEM, spec_...  8.64 us
    pallas_call x1, Pallas kernels, output_gate(): pl.pallas_call(gate_kernel, grid=(rows // ROWS,), in_specs=[pl.BlockSpec(...  8.2 us
  transfers between devices with their start and end apart: 33, of which 21 were waited for; matrix products, arithmetic and copies ran while one was open for 0% of the time, Pallas kernels for 15%

profile of v5, /device:TPU:0, one launch (start us, length us, event | category | flops | bytes accessed | tf_op | source)
XLA Modules:
  0.0 318.0 jit_solution(8952613794859221737)
XLA Ops:
  0.0 11.2 %project.4 = bf16[32,5,48,384]{3,2,1,0:T(8,128)(2,1)} custom-call(s32[768]{0:T(1024)} %at_ref.3, s32[768]{0:T(1024)} %at_ref.3, bf16[48,384,128]{2,1,0:T(8,128)(2,1)} %x_ref.3, bf16[128,128]{1,0:T(8,128)(2,1)} %gate_ref.7, bf16[128,128]{1,0:T(8,128)(2,1)} %value_ref.5, f32[1,128]{1,0:T(1,128)} %bitcast.5), custom_call_target="tpu_custom_call" | custom-call | flops 754974720 | bytes 18874368 | tf_op jit(solution)/shard_map/project/pallas_call | solution.py:117
  11.2 7.4 %all-to-all-start = ((bf16[32,5,48,384]{3,2,1,0:T(8,128)(2,1)}), bf16[32,5,48,384]{3,2,1,0:T(8,128)(2,1)}, u32[]{:S(2)}, u32[]{:S(2)}) async-start(bf16[32,5,48,384]{3,2,1,0:T(8,128)(2,1)} %project.4), calls=%async_computation | async-start | bytes 11796480 | tf_op jit(solution)/shard_map/all_to_all | solution.py:340
  19.9 16.8 %project.3 = (bf16[48,128,384]{2,1,0:T(8,128)(2,1)}, bf16[8,48,384]{2,1,0:T(8,128)(2,1)}, bf16[8,48,384]{2,1,0:T(8,128)(2,1)}, bf16[8,48,384]{2,1,0:T(8,128)(2,1...) custom-call(s32[768]{0:T(1024)} %at_ref.3, ...), custom_call_target="tpu_custom_call" | custom-call | flops 1207959552 | bytes 18874368 | tf_op jit(solution)/shard_map/project/pallas_call | solution.py:117
  36.7 1.8 collective-permute-start.1
  38.9 2.6 collective-permute-start.5
  42.1 25.3 %collective-permute-done.1.refs_2_ = bf16[8,48,384]{2,1,0:T(8,128)(2,1)S(1)} collective-permute-done((bf16[8,48,384]{2,1,0:T(8,128)(2,1)}, bf16[8,48,384]{2,1,0:T(8,128)(2,1)S(1)}, u32[]{:S(2)}, u32[]{:S(2)}) %collective-permute-start.1) | collective-permute-done | bytes 294944 | tf_op jit(solution)/shard_map/ppermute | solution.py:349
  67.4 2.0 collective-permute-start.4
  69.4 10.8 %collective-permute-done.2.refs_3_ = bf16[8,48,384]{2,1,0:T(8,128)(2,1)S(1)} collective-permute-done((bf16[8,48,384]{2,1,0:T(8,128)(2,1)}, bf16[8,48,384]{2,1,0:T(8,128)(2,1)S(1)}, u32[]{:S(2)}, u32[]{:S(2)}) %collective-permute-start.2) | collective-permute-done | bytes 294944 | tf_op jit(solution)/shard_map/ppermute | solution.py:349
  80.2 8.3 %collective-permute-start.7 = (bf16[8,48,384]{2,1,0:T(8,128)(2,1)}, bf16[8,48,384]{2,1,0:T(8,128)(2,1)}, u32[]{:S(2)}, u32[]{:S(2)}) collective-permute-start(bf16[8,48,384]{2,1,0:T(8,128)(2,1)} %get-tuple-element.72), channel_id=1, source_target_pairs={{0,8},{1,9},{2,10},{3,11},{4,12},{5,13},{6,14},{7,15},{8,0},{9,1},... | collective-permute-start | bytes 884744 | tf_op jit(solution)/shard_map/ppermute | solution.py:349
  88.5 9.1 %collective-permute-done.5.refs_6_ = bf16[8,48,384]{2,1,0:T(8,128)(2,1)} collective-permute-done((bf16[8,48,384]{2,1,0:T(8,128)(2,1)}, bf16[8,48,384]{2,1,0:T(8,128)(2,1)}, u32[]{:S(2)}, u32[]{:S(2)}) %collective-permute-start.5) | collective-permute-done | bytes 294944 | tf_op jit(solution)/shard_map/ppermute | solution.py:349
  97.6 2.8 collective-permute-start.10
  100.4 21.9 %collective-permute-done.8.refs_9_ = bf16[8,48,384]{2,1,0:T(8,128)(2,1)} collective-permute-done((bf16[8,48,384]{2,1,0:T(8,128)(2,1)}, bf16[8,48,384]{2,1,0:T(8,128)(2,1)}, u32[]{:S(2)}, u32[]{:S(2)}) %collective-permute-start.8) | collective-permute-done | bytes 294944 | tf_op jit(solution)/shard_map/ppermute | solution.py:349
  122.3 2.1 collective-permute-start.9
  124.5 4.2 %collective-permute-done.7.refs_8_ = bf16[8,48,384]{2,1,0:T(8,128)(2,1)} collective-permute-done((bf16[8,48,384]{2,1,0:T(8,128)(2,1)}, bf16[8,48,384]{2,1,0:T(8,128)(2,1)}, u32[]{:S(2)}, u32[]{:S(2)}) %collective-permute-start.7) | collective-permute-done | bytes 294944 | tf_op jit(solution)/shard_map/ppermute | solution.py:349
  128.7 3.9 %collective-permute-start.14 = (bf16[8,48,384]{2,1,0:T(8,128)(2,1)}, bf16[8,48,384]{2,1,0:T(8,128)(2,1)}, u32[]{:S(2)}, u32[]{:S(2)}) collective-permute-start(bf16[8,48,384]{2,1,0:T(8,128)(2,1)} %get-tuple-element.86), channel_id=1, source_target_pairs={{0,15},{1,14},{2,13},{3,12},{4,11},{5,10},{6,9},{7,8},{8,7},{9,6},... | collective-permute-start | bytes 884744 | tf_op jit(solution)/shard_map/ppermute | solution.py:349
  132.5 1.3 collective-permute-start.13
  135.0 2.8 collective-permute-start.11
  137.7 6.7 %project.5 = bf16[32,3,48,384]{3,2,1,0:T(8,128)(2,1)} custom-call(s32[768]{0:T(1024)} %at_ref.3, s32[768]{0:T(1024)} %at_ref.3, bf16[48,128,384]{2,1,0:T(8,128)(2,1)} %get-tuple-element.61.normed_ref.x_ref, bf16[128,128]{1,0:T(8,128)(2,1)} %gate_ref.7, bf16[128,128]{1,0:T(8,128)(2,1)} %value_ref.5, f32[1,128]{1,0:T(1,128)} %bitcast.7), custom_call_target="tpu_custom_call" | custom-call | flops 452984832 | bytes 18874368 | tf_op jit(solution)/shard_map/project/pallas_call | solution.py:117
  144.4 1.7 collective-permute-done.10.refs_11_
  146.2 6.3 %collective-permute-done.9.refs_10_ = bf16[8,48,384]{2,1,0:T(8,128)(2,1)} collective-permute-done((bf16[8,48,384]{2,1,0:T(8,128)(2,1)}, bf16[8,48,384]{2,1,0:T(8,128)(2,1)}, u32[]{:S(2)}, u32[]{:S(2)}) %collective-permute-start.9) | collective-permute-done | bytes 294944 | tf_op jit(solution)/shard_map/ppermute | solution.py:349
  152.5 9.5 %collective-permute-done.14.refs_15_ = bf16[8,48,384]{2,1,0:T(8,128)(2,1)} collective-permute-done((bf16[8,48,384]{2,1,0:T(8,128)(2,1)}, bf16[8,48,384]{2,1,0:T(8,128)(2,1)}, u32[]{:S(2)}, u32[]{:S(2)}) %collective-permute-start.14) | collective-permute-done | bytes 294944 | tf_op jit(solution)/shard_map/ppermute | solution.py:349
  162.0 10.6 %collective-permute-done.13.refs_14_ = bf16[8,48,384]{2,1,0:T(8,128)(2,1)} collective-permute-done((bf16[8,48,384]{2,1,0:T(8,128)(2,1)}, bf16[8,48,384]{2,1,0:T(8,128)(2,1)}, u32[]{:S(2)}, u32[]{:S(2)}) %collective-permute-start.13) | collective-permute-done | bytes 294944 | tf_op jit(solution)/shard_map/ppermute | solution.py:349
  172.6 1.5 collective-permute-done.11.refs_12_
  174.1 4.3 %all-to-all-start.1 = ((bf16[32,3,48,384]{3,2,1,0:T(8,128)(2,1)}), bf16[32,3,48,384]{3,2,1,0:T(8,128)(2,1)}, u32[]{:S(2)}, u32[]{:S(2)}) async-start(bf16[32,3,48,384]{3,2,1,0:T(8,128)(2,1)} %project.5), calls=%async_computation.1 | async-start | bytes 7077888 | tf_op jit(solution)/shard_map/all_to_all | solution.py:340
  178.3 9.1 %contract.2 = (bf16[5,48,384]{2,1,0:T(8,128)(2,1)}, bf16[5,48,384]{2,1,0:T(8,128)(2,1)}, bf16[5,48,384]{2,1,0:T(8,128)(2,1)}, bf16[5,48,384]{2,1,0:T(8,128)(2,1)...) custom-call(s32[3]{0:T(128)} %pad_add_fusion.at_ref, ...), custom_call_target="tpu_custom_call" | custom-call | flops 18119393280 | bytes 11796480 | tf_op jit(solution)/shard_map/contract/pallas_call | solution.py:196
  187.4 1.6 collective-permute-start.18
  189.0 2.6 collective-permute-start.16
  192.2 14.1 %collective-permute-done.18.refs_4_ = bf16[5,48,384]{2,1,0:T(8,128)(2,1)S(1)} collective-permute-done((bf16[5,48,384]{2,1,0:T(8,128)(2,1)}, bf16[5,48,384]{2,1,0:T(8,128)(2,1)S(1)}, u32[]{:S(2)}, u32[]{:S(2)}) %collective-permute-start.18) | collective-permute-done | bytes 184352 | tf_op jit(solution)/shard_map/ppermute | solution.py:349
  207.2 4.9 %collective-permute-done.19.refs_5_ = bf16[5,48,384]{2,1,0:T(8,128)(2,1)S(1)} collective-permute-done((bf16[5,48,384]{2,1,0:T(8,128)(2,1)}, bf16[5,48,384]{2,1,0:T(8,128)(2,1)S(1)}, u32[]{:S(2)}, u32[]{:S(2)}) %collective-permute-start.19) | collective-permute-done | bytes 184352 | tf_op jit(solution)/shard_map/ppermute | solution.py:349
  212.1 3.7 %collective-permute-start.25 = (bf16[5,48,384]{2,1,0:T(8,128)(2,1)}, bf16[5,48,384]{2,1,0:T(8,128)(2,1)}, u32[]{:S(2)}, u32[]{:S(2)}) collective-permute-start(bf16[5,48,384]{2,1,0:T(8,128)(2,1)} %get-tuple-element.104), channel_id=1, source_target_pairs={{0,11},{1,10},{2,9},{3,8},{4,15},{5,14},{6,13},{7,12},{8,3},{9,2},... | collective-permute-start | bytes 552968 | tf_op jit(solution)/shard_map/ppermute | solution.py:349
  215.8 3.8 %collective-permute-start.21 = (bf16[5,48,384]{2,1,0:T(8,128)(2,1)}, bf16[5,48,384]{2,1,0:T(8,128)(2,1)}, u32[]{:S(2)}, u32[]{:S(2)}) collective-permute-start(bf16[5,48,384]{2,1,0:T(8,128)(2,1)} %get-tuple-element.96), channel_id=1, source_target_pairs={{0,7},{1,6},{2,5},{3,4},{4,3},{5,2},{6,1},{7,0},{8,15},{9,14},{10,... | collective-permute-start | bytes 552968 | tf_op jit(solution)/shard_map/ppermute | solution.py:349
  219.6 1.9 collective-permute-start.20
  221.5 19.2 %collective-permute-done.22.refs_8_ = bf16[5,48,384]{2,1,0:T(8,128)(2,1)} collective-permute-done((bf16[5,48,384]{2,1,0:T(8,128)(2,1)}, bf16[5,48,384]{2,1,0:T(8,128)(2,1)}, u32[]{:S(2)}, u32[]{:S(2)}) %collective-permute-start.22) | collective-permute-done | bytes 184352 | tf_op jit(solution)/shard_map/ppermute | solution.py:349
  240.7 3.6 %collective-permute-start.29 = (bf16[5,48,384]{2,1,0:T(8,128)(2,1)}, bf16[5,48,384]{2,1,0:T(8,128)(2,1)}, u32[]{:S(2)}, u32[]{:S(2)}) collective-permute-start(bf16[5,48,384]{2,1,0:T(8,128)(2,1)} %get-tuple-element.112), channel_id=1, source_target_pairs={{0,15},{1,14},{2,13},{3,12},{4,11},{5,10},{6,9},{7,8},{8,7},{9,6},... | collective-permute-start | bytes 552968 | tf_op jit(solution)/shard_map/ppermute | solution.py:349
  244.7 4.0 %collective-permute-start.28 = (bf16[5,48,384]{2,1,0:T(8,128)(2,1)}, bf16[5,48,384]{2,1,0:T(8,128)(2,1)}, u32[]{:S(2)}, u32[]{:S(2)}) collective-permute-start(bf16[5,48,384]{2,1,0:T(8,128)(2,1)} %get-tuple-element.110), channel_id=1, source_target_pairs={{0,14},{1,15},{2,12},{3,13},{4,10},{5,11},{6,8},{7,9},{8,6},{9,7},... | collective-permute-start | bytes 552968 | tf_op jit(solution)/shard_map/ppermute | solution.py:349
  249.0 2.7 collective-permute-start.26
  251.6 1.4 collective-permute-start.24
  253.0 2.4 collective-permute-done.29.refs_15_
  255.4 5.7 %collective-permute-done.28.refs_14_ = bf16[5,48,384]{2,1,0:T(8,128)(2,1)} collective-permute-done((bf16[5,48,384]{2,1,0:T(8,128)(2,1)}, bf16[5,48,384]{2,1,0:T(8,128)(2,1)}, u32[]{:S(2)}, u32[]{:S(2)}) %collective-permute-start.28) | collective-permute-done | bytes 184352 | tf_op jit(solution)/shard_map/ppermute | solution.py:349
  261.1 5.7 %collective-permute-done.27.refs_13_ = bf16[5,48,384]{2,1,0:T(8,128)(2,1)} collective-permute-done((bf16[5,48,384]{2,1,0:T(8,128)(2,1)}, bf16[5,48,384]{2,1,0:T(8,128)(2,1)}, u32[]{:S(2)}, u32[]{:S(2)}) %collective-permute-start.27) | collective-permute-done | bytes 184352 | tf_op jit(solution)/shard_map/ppermute | solution.py:349
  266.8 2.9 collective-permute-done.26.refs_12_
  269.7 3.6 %collective-permute-done.24.refs_10_ = bf16[5,48,384]{2,1,0:T(8,128)(2,1)} collective-permute-done((bf16[5,48,384]{2,1,0:T(8,128)(2,1)}, bf16[5,48,384]{2,1,0:T(8,128)(2,1)}, u32[]{:S(2)}, u32[]{:S(2)}) %collective-permute-start.24) | collective-permute-done | bytes 184352 | tf_op jit(solution)/shard_map/ppermute | solution.py:349
  273.4 6.2 %contract.3 = bf16[16,3,48,384]{3,2,1,0:T(8,128)(2,1)} custom-call(s32[3]{0:T(128)} %pad_add_fusion.at_ref, bf16[8,48,384]{2,1,0:T(8,128)(2,1)} %get-tuple-element.62.refs_0_, bf16[8,48,384]{2,1,0:T(8,128)(2,1)} %collective-permute-done.refs_1_, bf16[8,48,384]{2,1,0:T(8,128)(2,1)} %copy-done.4, bf16[8,48,384]{2,1,0:T(8,128)(2,1)} %copy-done.5, ...), custom_call_target="tpu_custom_call" | custom-call | flops 10871635968 | bytes 7077888 | tf_op jit(solution)/shard_map/contract/pallas_call | solution.py:196
  279.6 4.5 %all-to-all-start.2 = ((bf16[16,3,48,384]{3,2,1,0:T(8,128)(2,1)}), bf16[16,3,48,384]{3,2,1,0:T(8,128)(2,1)}, u32[]{:S(2)}, u32[]{:S(2)}) async-start(bf16[16,3,48,384]{3,2,1,0:T(8,128)(2,1)} %contract.3), calls=%async_computation.2 | async-start | bytes 3538944 | tf_op jit(solution)/shard_map/all_to_all | solution.py:340
  284.1 8.2 %output_gate.1.gate_ref = bf16[48,384,128]{2,1,0:T(8,128)(2,1)} custom-call(bf16[48,128,384]{2,1,0:T(8,128)(2,1)} %get-tuple-element.61.normed_ref.x_ref, bf16[128,128]{1,0:T(8,128)(2,1)} %gate_ref.5), custom_call_target="tpu_custom_call" | custom-call | flops 603979776 | bytes 9437184 | tf_op jit(solution)/shard_map/output_gate/pallas_call | solution.py:148
  292.3 6.3 %gather.1 = (bf16[48,80,384]{2,1,0:T(8,128)(2,1)}, f32[2,48,384]{2,1,0:T(8,128)}) custom-call(s32[3]{0:T(128)} %pad_add_fusion.at_ref, bf16[5,48,384]{2,1,0:T(8,128)(2,1)} %get-tuple-element.87.refs_0_, bf16[5,48,384]{2,1,0:T(8,128)(2,1)} %collective-permute-done.15.refs_1_, bf16[5,48,384]{2,1,0:T(8,128)(2,1)} %copy-done.2, ...), custom_call_target="tpu_custom_call" | custom-call | flops 5898240 | bytes 5898240 | tf_op jit(solution)/shard_map/gather/pallas_call | solution.py:244
  298.6 10.7 %all-to-all-done.2.last_ref = bf16[16,3,48,384]{3,2,1,0:T(8,128)(2,1)} async-done(((bf16[16,3,48,384]{3,2,1,0:T(8,128)(2,1)}), bf16[16,3,48,384]{3,2,1,0:T(8,128)(2,1)}, u32[]{:S(2)}, u32[]{:S(2)}) %all-to-all-start.2) | async-done | bytes 1769504 | tf_op jit(solution)/shard_map/all_to_all | solution.py:340
  309.3 8.6 %finish.1 = bf16[48,384,128]{2,1,0:T(8,128)(2,1)} custom-call(f32[128]{0:T(128)} %gain_ref.1, f32[1,128]{1,0:T(1,128)} %bitcast.8, bf16[48,384,128]{2,1,0:T(8,128)(2,1)} %output_gate.1.gate_ref, bf16[128,128]{1,0:T(8,128)(2,1)} %proj_ref.1, bf16[48,80,384]{2,1,0:T(8,128)(2,1)} %get-tuple-element.113.turned_ref, f32[2,48,384]{2,1,0:T(8,128)} %get-tuple-element.114.stats_ref, ...), custom_call_target="tpu_custom_call" | custom-call | tf_op jit(solution)/shard_map/finish/pallas_call | solution.py:315
  (40 shorter events, 5.4 us)
Async XLA Ops:
  11.2 7.4 %copy-start.3 = (s32[768]{0:T(1024)S(1)}, s32[768]{0:T(1024)}, u32[]{:S(2)}) copy-start(s32[768]{0:T(1024)} %at_ref.3) | copy-start | bytes 9220
  11.2 162.8 %all-to-all-start = ((bf16[32,5,48,384]{3,2,1,0:T(8,128)(2,1)}), bf16[32,5,48,384]{3,2,1,0:T(8,128)(2,1)}, u32[]{:S(2)}, u32[]{:S(2)}) async-start(bf16[32,5,48,384]{3,2,1,0:T(8,128)(2,1)} %project.4), calls=%async_computation | async-start | bytes 11796480 | tf_op jit(solution)/shard_map/all_to_all | solution.py:340
  36.7 30.7 %collective-permute-start.1 = (bf16[8,48,384]{2,1,0:T(8,128)(2,1)}, bf16[8,48,384]{2,1,0:T(8,128)(2,1)S(1)}, u32[]{:S(2)}, u32[]{:S(2)}) collective-permute-start(bf16[8,48,384]{2,1,0:T(8,128)(2,1)} %get-tuple-element.64), channel_id=1, source_target_pairs={{0,2},{1,3},{2,0},{3,1},{4,6},{5,7},{6,4},{7,5},{8,10},{9,11},{10,... | collective-permute-start | bytes 884744 | tf_op jit(solution)/shard_map/ppermute | solution.py:349
  38.5 41.7 %collective-permute-start.2 = (bf16[8,48,384]{2,1,0:T(8,128)(2,1)}, bf16[8,48,384]{2,1,0:T(8,128)(2,1)S(1)}, u32[]{:S(2)}, u32[]{:S(2)}) collective-permute-start(bf16[8,48,384]{2,1,0:T(8,128)(2,1)} %get-tuple-element.65), channel_id=1, source_target_pairs={{0,3},{1,2},{2,1},{3,0},{4,7},{5,6},{6,5},{7,4},{8,11},{9,10},{10,... | collective-permute-start | bytes 884744 | tf_op jit(solution)/shard_map/ppermute | solution.py:349
  38.5 41.7 %collective-permute-start = (bf16[8,48,384]{2,1,0:T(8,128)(2,1)}, bf16[8,48,384]{2,1,0:T(8,128)(2,1)}, u32[]{:S(2)}, u32[]{:S(2)}) collective-permute-start(bf16[8,48,384]{2,1,0:T(8,128)(2,1)} %get-tuple-element.63), channel_id=1, source_target_pairs={{0,1},{1,0},{2,3},{3,2},{4,5},{5,4},{6,7},{7,6},{8,9},{9,8},{10,11... | collective-permute-start | bytes 884744 | tf_op jit(solution)/shard_map/ppermute | solution.py:349
  38.9 58.7 %collective-permute-start.5 = (bf16[8,48,384]{2,1,0:T(8,128)(2,1)}, bf16[8,48,384]{2,1,0:T(8,128)(2,1)}, u32[]{:S(2)}, u32[]{:S(2)}) collective-permute-start(bf16[8,48,384]{2,1,0:T(8,128)(2,1)} %get-tuple-element.68), channel_id=1, source_target_pairs={{0,6},{1,7},{2,4},{3,5},{4,2},{5,3},{6,0},{7,1},{8,14},{9,15},{10,... | collective-permute-start | bytes 884744 | tf_op jit(solution)/shard_map/ppermute | solution.py:349
  41.5 56.1 %collective-permute-start.3 = (bf16[8,48,384]{2,1,0:T(8,128)(2,1)}, bf16[8,48,384]{2,1,0:T(8,128)(2,1)}, u32[]{:S(2)}, u32[]{:S(2)}) collective-permute-start(bf16[8,48,384]{2,1,0:T(8,128)(2,1)} %get-tuple-element.66), channel_id=1, source_target_pairs={{0,4},{1,5},{2,6},{3,7},{4,0},{5,1},{6,2},{7,3},{8,12},{9,13},{10,... | collective-permute-start | bytes 884744 | tf_op jit(solution)/shard_map/ppermute | solution.py:349
  67.4 106.7 %copy-start.4 = (bf16[8,48,384]{2,1,0:T(8,128)(2,1)}, bf16[8,48,384]{2,1,0:T(8,128)(2,1)S(1)}, u32[]{:S(2)}) copy-start(bf16[8,48,384]{2,1,0:T(8,128)(2,1)S(1)} %collective-permute-done.1.refs_2_) | copy-start | bytes 884740
  67.4 30.2 %collective-permute-start.4 = (bf16[8,48,384]{2,1,0:T(8,128)(2,1)}, bf16[8,48,384]{2,1,0:T(8,128)(2,1)}, u32[]{:S(2)}, u32[]{:S(2)}) collective-permute-start(bf16[8,48,384]{2,1,0:T(8,128)(2,1)} %get-tuple-element.67), channel_id=1, source_target_pairs={{0,5},{1,4},{2,7},{3,6},{4,1},{5,0},{6,3},{7,2},{8,13},{9,12},{10,... | collective-permute-start | bytes 884744 | tf_op jit(solution)/shard_map/ppermute | solution.py:349
  80.2 93.9 %copy-start.5 = (bf16[8,48,384]{2,1,0:T(8,128)(2,1)}, bf16[8,48,384]{2,1,0:T(8,128)(2,1)S(1)}, u32[]{:S(2)}) copy-start(bf16[8,48,384]{2,1,0:T(8,128)(2,1)S(1)} %collective-permute-done.2.refs_3_) | copy-start | bytes 884740
  80.2 42.1 %collective-permute-start.8 = (bf16[8,48,384]{2,1,0:T(8,128)(2,1)}, bf16[8,48,384]{2,1,0:T(8,128)(2,1)}, u32[]{:S(2)}, u32[]{:S(2)}) collective-permute-start(bf16[8,48,384]{2,1,0:T(8,128)(2,1)} %get-tuple-element.74), channel_id=1, source_target_pairs={{0,9},{1,8},{2,11},{3,10},{4,13},{5,12},{6,15},{7,14},{8,1},{9,0},... | collective-permute-start | bytes 884744 | tf_op jit(solution)/shard_map/ppermute | solution.py:349
  80.2 48.4 %collective-permute-start.7 = (bf16[8,48,384]{2,1,0:T(8,128)(2,1)}, bf16[8,48,384]{2,1,0:T(8,128)(2,1)}, u32[]{:S(2)}, u32[]{:S(2)}) collective-permute-start(bf16[8,48,384]{2,1,0:T(8,128)(2,1)} %get-tuple-element.72), channel_id=1, source_target_pairs={{0,8},{1,9},{2,10},{3,11},{4,12},{5,13},{6,14},{7,15},{8,0},{9,1},... | collective-permute-start | bytes 884744 | tf_op jit(solution)/shard_map/ppermute | solution.py:349
  97.6 35.0 %collective-permute-start.6 = (bf16[8,48,384]{2,1,0:T(8,128)(2,1)}, bf16[8,48,384]{2,1,0:T(8,128)(2,1)}, u32[]{:S(2)}, u32[]{:S(2)}) collective-permute-start(bf16[8,48,384]{2,1,0:T(8,128)(2,1)} %get-tuple-element.70), channel_id=1, source_target_pairs={{0,7},{1,6},{2,5},{3,4},{4,3},{5,2},{6,1},{7,0},{8,15},{9,14},{10,... | collective-permute-start | bytes 884744 | tf_op jit(solution)/shard_map/ppermute | solution.py:349
  97.6 37.4 %collective-permute-start.12 = (bf16[8,48,384]{2,1,0:T(8,128)(2,1)}, bf16[8,48,384]{2,1,0:T(8,128)(2,1)}, u32[]{:S(2)}, u32[]{:S(2)}) collective-permute-start(bf16[8,48,384]{2,1,0:T(8,128)(2,1)} %get-tuple-element.82), channel_id=1, source_target_pairs={{0,13},{1,12},{2,15},{3,14},{4,9},{5,8},{6,11},{7,10},{8,5},{9,4},... | collective-permute-start | bytes 884744 | tf_op jit(solution)/shard_map/ppermute | solution.py:349
  97.6 48.6 %collective-permute-start.10 = (bf16[8,48,384]{2,1,0:T(8,128)(2,1)}, bf16[8,48,384]{2,1,0:T(8,128)(2,1)}, u32[]{:S(2)}, u32[]{:S(2)}) collective-permute-start(bf16[8,48,384]{2,1,0:T(8,128)(2,1)} %get-tuple-element.78), channel_id=1, source_target_pairs={{0,11},{1,10},{2,9},{3,8},{4,15},{5,14},{6,13},{7,12},{8,3},{9,2},... | collective-permute-start | bytes 884744 | tf_op jit(solution)/shard_map/ppermute | solution.py:349
  122.3 30.1 %collective-permute-start.9 = (bf16[8,48,384]{2,1,0:T(8,128)(2,1)}, bf16[8,48,384]{2,1,0:T(8,128)(2,1)}, u32[]{:S(2)}, u32[]{:S(2)}) collective-permute-start(bf16[8,48,384]{2,1,0:T(8,128)(2,1)} %get-tuple-element.76), channel_id=1, source_target_pairs={{0,10},{1,11},{2,8},{3,9},{4,14},{5,15},{6,12},{7,13},{8,2},{9,3},... | collective-permute-start | bytes 884744 | tf_op jit(solution)/shard_map/ppermute | solution.py:349
  128.7 33.3 %collective-permute-start.14 = (bf16[8,48,384]{2,1,0:T(8,128)(2,1)}, bf16[8,48,384]{2,1,0:T(8,128)(2,1)}, u32[]{:S(2)}, u32[]{:S(2)}) collective-permute-start(bf16[8,48,384]{2,1,0:T(8,128)(2,1)} %get-tuple-element.86), channel_id=1, source_target_pairs={{0,15},{1,14},{2,13},{3,12},{4,11},{5,10},{6,9},{7,8},{8,7},{9,6},... | collective-permute-start | bytes 884744 | tf_op jit(solution)/shard_map/ppermute | solution.py:349
  132.5 40.0 %collective-permute-start.13 = (bf16[8,48,384]{2,1,0:T(8,128)(2,1)}, bf16[8,48,384]{2,1,0:T(8,128)(2,1)}, u32[]{:S(2)}, u32[]{:S(2)}) collective-permute-start(bf16[8,48,384]{2,1,0:T(8,128)(2,1)} %get-tuple-element.84), channel_id=1, source_target_pairs={{0,14},{1,15},{2,12},{3,13},{4,10},{5,11},{6,8},{7,9},{8,6},{9,7},... | collective-permute-start | bytes 884744 | tf_op jit(solution)/shard_map/ppermute | solution.py:349
  135.0 39.1 %collective-permute-start.11 = (bf16[8,48,384]{2,1,0:T(8,128)(2,1)}, bf16[8,48,384]{2,1,0:T(8,128)(2,1)}, u32[]{:S(2)}, u32[]{:S(2)}) collective-permute-start(bf16[8,48,384]{2,1,0:T(8,128)(2,1)} %get-tuple-element.80), channel_id=1, source_target_pairs={{0,12},{1,13},{2,14},{3,15},{4,8},{5,9},{6,10},{7,11},{8,4},{9,5},... | collective-permute-start | bytes 884744 | tf_op jit(solution)/shard_map/ppermute | solution.py:349
  174.1 99.3 %all-to-all-start.1 = ((bf16[32,3,48,384]{3,2,1,0:T(8,128)(2,1)}), bf16[32,3,48,384]{3,2,1,0:T(8,128)(2,1)}, u32[]{:S(2)}, u32[]{:S(2)}) async-start(bf16[32,3,48,384]{3,2,1,0:T(8,128)(2,1)} %project.5), calls=%async_computation.1 | async-start | bytes 7077888 | tf_op jit(solution)/shard_map/all_to_all | solution.py:340
  187.4 18.9 %collective-permute-start.18 = (bf16[5,48,384]{2,1,0:T(8,128)(2,1)}, bf16[5,48,384]{2,1,0:T(8,128)(2,1)S(1)}, u32[]{:S(2)}, u32[]{:S(2)}) collective-permute-start(bf16[5,48,384]{2,1,0:T(8,128)(2,1)} %get-tuple-element.91), channel_id=1, source_target_pairs={{0,4},{1,5},{2,6},{3,7},{4,0},{5,1},{6,2},{7,3},{8,12},{9,13},{10,... | collective-permute-start | bytes 552968 | tf_op jit(solution)/shard_map/ppermute | solution.py:349
  189.0 23.1 %collective-permute-start.19 = (bf16[5,48,384]{2,1,0:T(8,128)(2,1)}, bf16[5,48,384]{2,1,0:T(8,128)(2,1)S(1)}, u32[]{:S(2)}, u32[]{:S(2)}) collective-permute-start(bf16[5,48,384]{2,1,0:T(8,128)(2,1)} %get-tuple-element.92), channel_id=1, source_target_pairs={{0,5},{1,4},{2,7},{3,6},{4,1},{5,0},{6,3},{7,2},{8,13},{9,12},{10,... | collective-permute-start | bytes 552968 | tf_op jit(solution)/shard_map/ppermute | solution.py:349
  189.0 26.8 %collective-permute-start.16 = (bf16[5,48,384]{2,1,0:T(8,128)(2,1)}, bf16[5,48,384]{2,1,0:T(8,128)(2,1)S(1)}, u32[]{:S(2)}, u32[]{:S(2)}) collective-permute-start(bf16[5,48,384]{2,1,0:T(8,128)(2,1)} %get-tuple-element.89), channel_id=1, source_target_pairs={{0,2},{1,3},{2,0},{3,1},{4,6},{5,7},{6,4},{7,5},{8,10},{9,11},{10,... | collective-permute-start | bytes 552968 | tf_op jit(solution)/shard_map/ppermute | solution.py:349
  191.7 28.0 %collective-permute-start.17 = (bf16[5,48,384]{2,1,0:T(8,128)(2,1)}, bf16[5,48,384]{2,1,0:T(8,128)(2,1)}, u32[]{:S(2)}, u32[]{:S(2)}) collective-permute-start(bf16[5,48,384]{2,1,0:T(8,128)(2,1)} %get-tuple-element.90), channel_id=1, source_target_pairs={{0,3},{1,2},{2,1},{3,0},{4,7},{5,6},{6,5},{7,4},{8,11},{9,10},{10,... | collective-permute-start | bytes 552968 | tf_op jit(solution)/shard_map/ppermute | solution.py:349
  192.1 27.5 %collective-permute-start.15 = (bf16[5,48,384]{2,1,0:T(8,128)(2,1)}, bf16[5,48,384]{2,1,0:T(8,128)(2,1)}, u32[]{:S(2)}, u32[]{:S(2)}) collective-permute-start(bf16[5,48,384]{2,1,0:T(8,128)(2,1)} %get-tuple-element.88), channel_id=1, source_target_pairs={{0,1},{1,0},{2,3},{3,2},{4,5},{5,4},{6,7},{7,6},{8,9},{9,8},{10,11... | collective-permute-start | bytes 552968 | tf_op jit(solution)/shard_map/ppermute | solution.py:349
  206.3 73.3 %copy-start = (bf16[5,48,384]{2,1,0:T(8,128)(2,1)}, bf16[5,48,384]{2,1,0:T(8,128)(2,1)S(1)}, u32[]{:S(2)}) copy-start(bf16[5,48,384]{2,1,0:T(8,128)(2,1)S(1)} %collective-permute-done.18.refs_4_) | copy-start | bytes 552964
  206.3 34.4 %collective-permute-start.22 = (bf16[5,48,384]{2,1,0:T(8,128)(2,1)}, bf16[5,48,384]{2,1,0:T(8,128)(2,1)}, u32[]{:S(2)}, u32[]{:S(2)}) collective-permute-start(bf16[5,48,384]{2,1,0:T(8,128)(2,1)} %get-tuple-element.98), channel_id=1, source_target_pairs={{0,8},{1,9},{2,10},{3,11},{4,12},{5,13},{6,14},{7,15},{8,0},{9,1},... | collective-permute-start | bytes 552968 | tf_op jit(solution)/shard_map/ppermute | solution.py:349
  212.1 67.5 %copy-start.1 = (bf16[5,48,384]{2,1,0:T(8,128)(2,1)}, bf16[5,48,384]{2,1,0:T(8,128)(2,1)S(1)}, u32[]{:S(2)}) copy-start(bf16[5,48,384]{2,1,0:T(8,128)(2,1)S(1)} %collective-permute-done.19.refs_5_) | copy-start | bytes 552964
  212.1 32.6 %collective-permute-start.25 = (bf16[5,48,384]{2,1,0:T(8,128)(2,1)}, bf16[5,48,384]{2,1,0:T(8,128)(2,1)}, u32[]{:S(2)}, u32[]{:S(2)}) collective-permute-start(bf16[5,48,384]{2,1,0:T(8,128)(2,1)} %get-tuple-element.104), channel_id=1, source_target_pairs={{0,11},{1,10},{2,9},{3,8},{4,15},{5,14},{6,13},{7,12},{8,3},{9,2},... | collective-permute-start | bytes 552968 | tf_op jit(solution)/shard_map/ppermute | solution.py:349
  215.8 63.8 %copy-start.2 = (bf16[5,48,384]{2,1,0:T(8,128)(2,1)}, bf16[5,48,384]{2,1,0:T(8,128)(2,1)S(1)}, u32[]{:S(2)}) copy-start(bf16[5,48,384]{2,1,0:T(8,128)(2,1)S(1)} %collective-permute-done.16.refs_2_) | copy-start | bytes 552964
  215.8 32.9 %collective-permute-start.21 = (bf16[5,48,384]{2,1,0:T(8,128)(2,1)}, bf16[5,48,384]{2,1,0:T(8,128)(2,1)}, u32[]{:S(2)}, u32[]{:S(2)}) collective-permute-start(bf16[5,48,384]{2,1,0:T(8,128)(2,1)} %get-tuple-element.96), channel_id=1, source_target_pairs={{0,7},{1,6},{2,5},{3,4},{4,3},{5,2},{6,1},{7,0},{8,15},{9,14},{10,... | collective-permute-start | bytes 552968 | tf_op jit(solution)/shard_map/ppermute | solution.py:349
  219.6 29.3 %collective-permute-start.23 = (bf16[5,48,384]{2,1,0:T(8,128)(2,1)}, bf16[5,48,384]{2,1,0:T(8,128)(2,1)}, u32[]{:S(2)}, u32[]{:S(2)}) collective-permute-start(bf16[5,48,384]{2,1,0:T(8,128)(2,1)} %get-tuple-element.100), channel_id=1, source_target_pairs={{0,9},{1,8},{2,11},{3,10},{4,13},{5,12},{6,15},{7,14},{8,1},{9,0},... | collective-permute-start | bytes 552968 | tf_op jit(solution)/shard_map/ppermute | solution.py:349
  219.6 32.0 %collective-permute-start.20 = (bf16[5,48,384]{2,1,0:T(8,128)(2,1)}, bf16[5,48,384]{2,1,0:T(8,128)(2,1)}, u32[]{:S(2)}, u32[]{:S(2)}) collective-permute-start(bf16[5,48,384]{2,1,0:T(8,128)(2,1)} %get-tuple-element.94), channel_id=1, source_target_pairs={{0,6},{1,7},{2,4},{3,5},{4,2},{5,3},{6,0},{7,1},{8,14},{9,15},{10,... | collective-permute-start | bytes 552968 | tf_op jit(solution)/shard_map/ppermute | solution.py:349
  240.7 14.7 %collective-permute-start.29 = (bf16[5,48,384]{2,1,0:T(8,128)(2,1)}, bf16[5,48,384]{2,1,0:T(8,128)(2,1)}, u32[]{:S(2)}, u32[]{:S(2)}) collective-permute-start(bf16[5,48,384]{2,1,0:T(8,128)(2,1)} %get-tuple-element.112), channel_id=1, source_target_pairs={{0,15},{1,14},{2,13},{3,12},{4,11},{5,10},{6,9},{7,8},{8,7},{9,6},... | collective-permute-start | bytes 552968 | tf_op jit(solution)/shard_map/ppermute | solution.py:349
  244.7 16.4 %collective-permute-start.28 = (bf16[5,48,384]{2,1,0:T(8,128)(2,1)}, bf16[5,48,384]{2,1,0:T(8,128)(2,1)}, u32[]{:S(2)}, u32[]{:S(2)}) collective-permute-start(bf16[5,48,384]{2,1,0:T(8,128)(2,1)} %get-tuple-element.110), channel_id=1, source_target_pairs={{0,14},{1,15},{2,12},{3,13},{4,10},{5,11},{6,8},{7,9},{8,6},{9,7},... | collective-permute-start | bytes 552968 | tf_op jit(solution)/shard_map/ppermute | solution.py:349
  248.7 18.1 %collective-permute-start.27 = (bf16[5,48,384]{2,1,0:T(8,128)(2,1)}, bf16[5,48,384]{2,1,0:T(8,128)(2,1)}, u32[]{:S(2)}, u32[]{:S(2)}) collective-permute-start(bf16[5,48,384]{2,1,0:T(8,128)(2,1)} %get-tuple-element.108), channel_id=1, source_target_pairs={{0,13},{1,12},{2,15},{3,14},{4,9},{5,8},{6,11},{7,10},{8,5},{9,4},... | collective-permute-start | bytes 552968 | tf_op jit(solution)/shard_map/ppermute | solution.py:349
  249.0 20.8 %collective-permute-start.26 = (bf16[5,48,384]{2,1,0:T(8,128)(2,1)}, bf16[5,48,384]{2,1,0:T(8,128)(2,1)}, u32[]{:S(2)}, u32[]{:S(2)}) collective-permute-start(bf16[5,48,384]{2,1,0:T(8,128)(2,1)} %get-tuple-element.106), channel_id=1, source_target_pairs={{0,12},{1,13},{2,14},{3,15},{4,8},{5,9},{6,10},{7,11},{8,4},{9,5},... | collective-permute-start | bytes 552968 | tf_op jit(solution)/shard_map/ppermute | solution.py:349
  251.6 21.8 %collective-permute-start.24 = (bf16[5,48,384]{2,1,0:T(8,128)(2,1)}, bf16[5,48,384]{2,1,0:T(8,128)(2,1)}, u32[]{:S(2)}, u32[]{:S(2)}) collective-permute-start(bf16[5,48,384]{2,1,0:T(8,128)(2,1)} %get-tuple-element.102), channel_id=1, source_target_pairs={{0,10},{1,11},{2,8},{3,9},{4,14},{5,15},{6,12},{7,13},{8,2},{9,3},... | collective-permute-start | bytes 552968 | tf_op jit(solution)/shard_map/ppermute | solution.py:349
  279.6 29.7 %all-to-all-start.2 = ((bf16[16,3,48,384]{3,2,1,0:T(8,128)(2,1)}), bf16[16,3,48,384]{3,2,1,0:T(8,128)(2,1)}, u32[]{:S(2)}, u32[]{:S(2)}) async-start(bf16[16,3,48,384]{3,2,1,0:T(8,128)(2,1)} %contract.3), calls=%async_computation.2 | async-start | bytes 3538944 | tf_op jit(solution)/shard_map/all_to_all | solution.py:340
